TPU v7x, 256 devices: a whole 4x4x8 slice. The times are simulated.
256 devices in a mesh: rows: 128 (over x_lo, z, y, core), img: 2 (over x_hi).
Axes of the slice: x: 4 (x_hi: 2, x_lo: 2; x = x_hi * 2 + x_lo), y: 4, z: 8, core: 2. Of those that a mesh axis runs over, the one named last changes fastest.
Arguments:
- local_maps: bfloat16 [2, 1024, 1024, 128], P('img', 'rows'), may hold values from -6 to 6
- global_maps: bfloat16 [2, 1024, 1024, 128], P('img', 'rows'), may hold values from -6 to 6
- conv_weight: bfloat16 [3, 3, 128, 128], replicated, may hold values from -0.1875 to 0.1875
- in_weight: bfloat16 [128, 64], replicated, may hold values from -0.5 to 0.5
- mix_weight: bfloat16 [128, 128], replicated, may hold values from -0.5 to 0.5
- out_weight: bfloat16 [64, 128], replicated, may hold values from -0.75 to 0.75
- out_cotangent: bfloat16 [2, 1024, 1024, 128], P('img', 'rows'), may hold values from -0.0234375 to 0.0234375
Outputs:
- local_out: bfloat16 [2, 1024, 1024, 128], P('img', 'rows')
- global_out: bfloat16 [2, 1024, 1024, 128], P('img', 'rows')
- mix_grad: float32 [128, 128], P(None, 'rows')
- out_grad: float32 [64, 128], P(None, 'rows')
All inputs are finite; a program needn't handle non-finite values.
Results may differ from a plain program's by a relative error of at most 0.017.
Values may be sent and summed in bfloat16 or wider, within the bound.
No kernel may reach another device: no remote copies, remote signals or barrier semaphores. Data moves between devices by JAX's collectives and lax.ppermute only.
A program may use at most 128 MiB of HBM per device.

v0:
```python
import math

import jax
import jax.numpy as jnp
from jax import lax
from jax.sharding import PartitionSpec as P

HEIGHT = 1024
WIDTH = 1024
SPEC_CH = 64
FREQS = 512


def extended(cells, sides, width):
    for axis, dim in sides:
        count = lax.axis_size(axis)
        ends = count - 1
        head = lax.slice_in_dim(cells, 0, width, axis=dim)
        tail = lax.slice_in_dim(cells, cells.shape[dim] - width, cells.shape[dim], axis=dim)
        cells = jnp.concatenate(
            [
                lax.ppermute(tail, axis, [(i, (i + 1) % count) for i in range(ends)]),
                cells,
                lax.ppermute(head, axis, [((i + 1) % count, i) for i in range(ends)]),
            ],
            axis=dim,
        )
    return cells


def row_tables():
    cols = jnp.arange(WIDTH, dtype=jnp.int32)
    freq = jnp.arange(FREQS, dtype=jnp.int32)
    phase = (cols[:, None] * freq[None, :] % WIDTH).astype(jnp.float32) * (2.0 * math.pi / WIDTH)
    cosine = jnp.cos(phase) / math.sqrt(WIDTH)
    sine = jnp.sin(phase) / math.sqrt(WIDTH)
    forward = jnp.stack([cosine, -sine], axis=2).reshape(WIDTH, 2 * FREQS)
    factor = jnp.where(freq == 0, 1.0, 2.0).astype(jnp.float32)
    inverse = jnp.stack([cosine * factor, -sine * factor], axis=2).reshape(WIDTH, 2 * FREQS).T
    return (forward.astype(jnp.bfloat16), inverse.astype(jnp.bfloat16))


def column_table():
    rows_idx = jnp.arange(HEIGHT, dtype=jnp.int32)
    phase = (rows_idx[:, None] * rows_idx[None, :] % HEIGHT).astype(jnp.float32) * (
        2.0 * math.pi / HEIGHT
    )
    both = jnp.concatenate([jnp.cos(phase), jnp.sin(phase)], axis=0) / math.sqrt(HEIGHT)
    return both.astype(jnp.bfloat16)


def forward_columns(block, column):
    prod = jnp.dot(column, block.reshape(block.shape[0], -1), preferred_element_type=jnp.float32)
    prod = prod.reshape((2,) + block.shape)
    half = block.shape[-1] // 2
    real = prod[0][..., :half] + prod[1][..., half:]
    imag = prod[0][..., half:] - prod[1][..., :half]
    return jnp.concatenate([real, imag], axis=-1)


def inverse_columns(block, column):
    prod = jnp.dot(column, block.reshape(block.shape[0], -1), preferred_element_type=jnp.float32)
    prod = prod.reshape((2,) + block.shape)
    half = block.shape[-1] // 2
    real = prod[0][..., :half] - prod[1][..., half:]
    imag = prod[0][..., half:] + prod[1][..., :half]
    return jnp.concatenate([real, imag], axis=-1)


def silu_slope(pre):
    sigma = jax.nn.sigmoid(pre)
    return sigma * (1.0 + pre * (1.0 - sigma))


def shards(local_maps, global_maps, conv_weight, in_weight, mix_weight, out_weight, out_cotangent):
    groups = lax.axis_size("rows")
    strip = global_maps.shape[1]
    per_group = FREQS // groups
    row_fwd, row_inv = row_tables()
    column = column_table()
    padded = extended(local_maps, (("rows", 1),), 1)
    local_out = lax.conv_general_dilated(
        padded,
        conv_weight,
        (1, 1),
        ((0, 0), (1, 1)),
        dimension_numbers=("NHWC", "HWIO", "NHWC"),
        preferred_element_type=jnp.float32,
    ).astype(jnp.bfloat16)
    inner = jax.nn.relu(
        jnp.einsum("hwc,cf->hwf", global_maps[0], in_weight, preferred_element_type=jnp.float32)
    ).astype(jnp.bfloat16)
    row_spec = jnp.einsum("wj,hwc->hjc", row_fwd, inner, preferred_element_type=jnp.float32).astype(
        jnp.bfloat16
    )
    row_spec = row_spec.reshape(strip, groups, per_group, 2 * SPEC_CH)
    cot_flat = out_cotangent[0]

    def pre_act(spectrum):
        return jnp.einsum("...i,io->...o", spectrum, mix_weight, preferred_element_type=jnp.float32)

    spectrum = forward_columns(
        lax.all_to_all(row_spec, "rows", split_axis=1, concat_axis=0, tiled=True), column
    ).astype(jnp.bfloat16)
    mixed = jax.nn.silu(pre_act(spectrum)).astype(jnp.bfloat16)
    back_spec = inverse_columns(mixed, column).astype(jnp.bfloat16)
    back_spec, spectrum = (back_spec, spectrum)
    back_rows = lax.all_to_all(back_spec, "rows", split_axis=0, concat_axis=1, tiled=True)
    back_rows = back_rows.reshape(strip, 2 * FREQS, SPEC_CH)
    spatial = jnp.einsum("jw,hjc->hwc", row_inv, back_rows, preferred_element_type=jnp.float32)
    summed = (inner.astype(jnp.float32) + spatial).astype(jnp.bfloat16)
    global_out = jnp.einsum(
        "hwf,fo->hwo", summed, out_weight, preferred_element_type=jnp.float32
    ).astype(jnp.bfloat16)
    inner_cot = jnp.einsum(
        "hwo,fo->hwf", cot_flat, out_weight, preferred_element_type=jnp.float32
    ).astype(jnp.bfloat16)
    back_cot = jnp.einsum(
        "jw,hwc->hjc", row_inv, inner_cot, preferred_element_type=jnp.float32
    ).astype(jnp.bfloat16)
    back_cot = back_cot.reshape(strip, groups, per_group, 2 * SPEC_CH)
    mixed_cot = forward_columns(
        lax.all_to_all(back_cot, "rows", split_axis=1, concat_axis=0, tiled=True), column
    )
    pre_cot = (mixed_cot * silu_slope(pre_act(spectrum))).astype(jnp.bfloat16)
    mix_part = jnp.einsum("hxki,hxko->io", spectrum, pre_cot, preferred_element_type=jnp.float32)
    out_part = jnp.einsum("hwf,hwo->fo", summed, cot_flat, preferred_element_type=jnp.float32)
    mix_total, out_total = lax.psum((mix_part, out_part), ("rows", "img"))
    position = lax.axis_index("rows")
    mix_cols = mix_total.shape[1] // groups
    out_cols = out_total.shape[1] // groups
    mix_grad = lax.dynamic_slice_in_dim(mix_total, position * mix_cols, mix_cols, 1)
    out_grad = lax.dynamic_slice_in_dim(out_total, position * out_cols, out_cols, 1)
    return (local_out, global_out[None], mix_grad, out_grad)


def solution(mesh):
    in_specs = (
        P("img", "rows", None, None),
        P("img", "rows", None, None),
        P(),
        P(),
        P(),
        P(),
        P("img", "rows", None, None),
    )
    out_specs = (
        P("img", "rows", None, None),
        P("img", "rows", None, None),
        P(None, "rows"),
        P(None, "rows"),
    )
    return jax.shard_map(shards, mesh=mesh, in_specs=in_specs, out_specs=out_specs, check_vma=False)
```

profile of v0, /device:TPU:1, one launch (start us, length us, event | category | flops | bytes accessed | tf_op | source)
XLA Modules:
  0.0 570.9 jit_solution(6005871996646911661)
XLA Ops:
  7.2 2.0 fusion.104
  9.2 5.1 collective-permute-start.1
  16.3 8.6 %multiply_convert_fusion.3 = (bf16[1024,512,1]{1,0,2:T(8,128)(2,1)S(1)}, bf16[1024,512,1]{1,0,2:T(8,128)(2,1)S(1)}) fusion(), kind=kLoop, calls=%fused_computation.56 | loop fusion | flops 9961472 | bytes 2097152 | tf_op jit(solution)/shard_map/convert.8
  26.4 6.2 %copy.69 = bf16[1024,512,2]{0,2,1:T(2,128)(2,1)} copy(bf16[1024,512,2]{1,0,2:T(8,128)(2,1)} %pad_maximum_fusion) | data formatting | bytes 4194304 | tf_op jit(solution)/shard_map/stack | solution.py:37
  32.6 4.1 convert_element_type.103
  36.7 2.6 maximum_convert_fusion
  39.3 2.3 fusion.60
  41.6 2.7 copy.71
  44.3 4.1 reshape.248
  48.4 2.6 copy.72
  51.0 15.8 %all-to-all-start = ((bf16[8,128,4,128]{3,2,0,1:T(4,128)(2,1)}), bf16[8,128,4,128]{3,2,0,1:T(4,128)(2,1)}, u32[]{:S(2)}, u32[]{:S(2)}) async-start(bf16[8,128,4,128]{3,2,0,1:T(4,128)(2,1)} %copy.72), calls=%async_computation | async-start | bytes 2097152 | tf_op jit(solution)/shard_map/all_to_all | solution.py:103
  66.8 8.7 %multiply_convert_fusion = (bf16[1024,512,1]{1,0,2:T(8,128)(2,1)S(1)}, bf16[1024,512,1]{1,0,2:T(8,128)(2,1)S(1)}) fusion(f32[512]{0:T(512)S(1)} %fusion.85, f32[512]{0:T(512)S(1)} %broadcast_multiply_fusion), kind=kLoop, calls=%fused_computation.47 | loop fusion | flops 10485760 | bytes 2101248 | tf_op jit(solution)/shard_map/convert.1
  77.1 6.2 %copy.85 = bf16[1024,512,2]{0,2,1:T(2,128)(2,1)} copy(bf16[1024,512,2]{1,0,2:T(8,128)(2,1)} %pad_maximum_fusion.1) | data formatting | bytes 4194304 | tf_op jit(solution)/shard_map/stack | solution.py:39
  83.3 4.2 convert_element_type.107
  87.5 4.6 fusion.55
  92.0 2.7 copy.89
  94.7 4.1 reshape.252
  98.8 2.6 copy.90
  101.4 17.6 %fusion.34 = (f32[1024,1024]{1,0:T(8,128)}, f32[1024,1024]{1,0:T(8,128)}) fusion(), kind=kLoop, calls=%fused_computation.59 | loop fusion | flops 14680064 | bytes 8388608 | tf_op jit(solution)/shard_map/sin | solution.py:48
  120.2 2.3 pad
  122.5 5.1 reshape.256
  127.6 2.2 copy.67
  129.8 5.3 select_convert_fusion
  136.8 13.2 %all-to-all-start.2 = ((bf16[8,128,4,128]{3,2,0,1:T(4,128)(2,1)}), bf16[8,128,4,128]{3,2,0,1:T(4,128)(2,1)}, u32[]{:S(2)}, u32[]{:S(2)}) async-start(bf16[8,128,4,128]{3,2,0,1:T(4,128)(2,1)} %copy.90), calls=%async_computation.2 | async-start | bytes 2097152 | tf_op jit(solution)/shard_map/all_to_all | solution.py:123
  150.0 6.2 %fusion.73 = f32[2048,512]{0,1:T(8,128)S(1)} fusion(bf16[8,128,4,128]{3,2,0,1:T(4,128)(2,1)} %all-to-all-done, f32[1024,1024]{1,0:T(8,128)} %get-tuple-element.38, f32[1024,1024]{1,0:T(8,128)} %get-tuple-element.39), kind=kOutput, calls=%fused_computation.82 | convolution fusion | flops 2153775104 | bytes 13631488 | tf_op jit(solution)/shard_map/dot_general | solution.py:53
  159.5 3.2 copy.106
  162.6 3.1 fusion.102
  165.8 3.2 copy.107
  168.9 3.2 copy.104
  172.1 3.2 copy.105
  175.3 2.6 fusion.68
  179.8 2.3 multiply_convert_fusion.2
  184.4 2.4 fusion.94
  189.8 2.7 copy.110
  192.6 3.1 fusion.100
  195.6 2.7 copy.111
  198.3 2.7 copy.108
  201.1 2.7 copy.109
  203.8 2.9 add_convert_fusion
  207.8 2.4 pad_maximum_fusion.3
  210.2 13.1 %all-to-all-start.1 = ((bf16[1024,1,4,128]{3,2,1,0:T(4,128)(2,1)}), bf16[1024,1,4,128]{3,2,1,0:T(4,128)(2,1)}, u32[]{:S(2)}, u32[]{:S(2)}) async-start(bf16[1024,1,4,128]{3,2,1,0:T(4,128)(2,1)} %pad_maximum_fusion.3), calls=%async_computation.1 | async-start | bytes 2097152 | tf_op jit(solution)/shard_map/all_to_all | solution.py:108
  223.3 6.2 %fusion.71 = f32[2048,512]{0,1:T(8,128)S(1)} fusion(bf16[8,128,4,128]{3,2,0,1:T(4,128)(2,1)} %all-to-all-done.2, f32[1024,1024]{1,0:T(8,128)} %get-tuple-element.38, f32[1024,1024]{1,0:T(8,128)} %get-tuple-element.39), kind=kOutput, calls=%fused_computation.80 | convolution fusion | flops 2153775104 | bytes 13631488 | tf_op jit(solution)/shard_map/dot_general | solution.py:53
  232.3 2.0 convolution_bitcast_fusion
  237.8 235.9 %all-reduce.2.cloned.1.call-done = f32[128,128]{0,1:T(8,128)} async-done(((f32[128,128]{0,1:T(8,128)}), f32[128,128]{0,1:T(8,128)}) %all-reduce.2.cloned.1.call-update) | async-done | bytes 65552 | tf_op jit(solution)/shard_map/psum | solution.py:128
  478.0 4.1 reshape.251
  482.1 3.5 fusion.23
  485.6 2.1 convert_bitcast_fusion
  488.6 74.6 %psum.15 = f32[64,128]{0,1:T(8,128)S(1)} all-reduce(f32[64,128]{0,1:T(8,128)S(1)} %fusion.64), channel_id=1, replica_groups=mesh['rows'=128,'img'=2] {'rows','img'}, use_global_device_ids=true, to_apply=%region_1.2 | all-reduce | flops 8192 | bytes 65536 | tf_op jit(solution)/shard_map/psum | solution.py:128
  (68 shorter events, 31.5 us)
Async XLA Ops:
  7.2 80.3 %copy-start = (bf16[1,8,1024,128]{3,2,1,0:T(8,128)(2,1)S(1)}, bf16[1,8,1024,128]{3,2,1,0:T(8,128)(2,1)}, u32[]{:S(2)}) copy-start(bf16[1,8,1024,128]{3,2,1,0:T(8,128)(2,1)} %param.13) | copy-start | bytes 6291460
  9.2 109.7 %collective-permute-start.1 = (bf16[1,1,1024,128]{3,2,1,0:T(8,128)(2,1)}, bf16[1,1,1024,128]{3,2,1,0:T(8,128)(2,1)S(1)}, u32[]{:S(2)}, u32[]{:S(2)}) collective-permute-start(bf16[1,1,1024,128]{3,2,1,0:T(8,128)(2,1)} %get-tuple-element.33), channel_id=1, source_target_pairs={{2,0},{4,2},{6,4},{8,6},{10,8},{12,10},{14,12},{16,14},{18,16},{20... | collective-permute-start | bytes 786440 | tf_op jit(solution)/shard_map/ppermute | solution.py:24
  14.3 104.6 %collective-permute-start = (bf16[1,1,1024,128]{3,2,1,0:T(8,128)(2,1)}, bf16[1,1,1024,128]{3,2,1,0:T(8,128)(2,1)}, u32[]{:S(2)}, u32[]{:S(2)}) collective-permute-start(bf16[1,1,1024,128]{3,2,1,0:T(8,128)(2,1)} %get-tuple-element.32), channel_id=1, source_target_pairs={{0,2},{2,4},{4,6},{6,8},{8,10},{10,12},{12,14},{14,16},{16,18},{18... | collective-permute-start | bytes 786440 | tf_op jit(solution)/shard_map/ppermute | solution.py:22
  32.6 4.1 copy-start.13
  36.7 2.6 copy-start.8
  51.0 85.8 %all-to-all-start = ((bf16[8,128,4,128]{3,2,0,1:T(4,128)(2,1)}), bf16[8,128,4,128]{3,2,0,1:T(4,128)(2,1)}, u32[]{:S(2)}, u32[]{:S(2)}) async-start(bf16[8,128,4,128]{3,2,0,1:T(4,128)(2,1)} %copy.72), calls=%async_computation | async-start | bytes 2097152 | tf_op jit(solution)/shard_map/all_to_all | solution.py:103
  83.3 4.2 copy-start.14
  101.4 17.6 %copy-start.7 = (bf16[1,8,1024,128]{3,2,1,0:T(8,128)(2,1)S(1)}, bf16[1,8,1024,128]{3,2,1,0:T(8,128)(2,1)}, u32[]{:S(2)}) copy-start(bf16[1,8,1024,128]{3,2,1,0:T(8,128)(2,1)} %param.7) | copy-start | bytes 6291460
  127.6 2.2 copy-start.15
  127.6 2.2 copy-start.17
  136.8 73.4 %all-to-all-start.2 = ((bf16[8,128,4,128]{3,2,0,1:T(4,128)(2,1)}), bf16[8,128,4,128]{3,2,0,1:T(4,128)(2,1)}, u32[]{:S(2)}, u32[]{:S(2)}) async-start(bf16[8,128,4,128]{3,2,0,1:T(4,128)(2,1)} %copy.90), calls=%async_computation.2 | async-start | bytes 2097152 | tf_op jit(solution)/shard_map/all_to_all | solution.py:123
  175.3 2.9 copy-start.1
  175.3 3.5 copy-start.3
  178.8 1.0 copy-start.9
  178.8 1.0 copy-start.16
  179.8 2.3 copy-start.11
  179.8 3.3 copy-start.5
  179.8 4.6 copy-start.6
  203.8 2.9 copy-start.2
  203.8 3.5 copy-start.4
  210.2 264.7 %all-to-all-start.1 = ((bf16[1024,1,4,128]{3,2,1,0:T(4,128)(2,1)}), bf16[1024,1,4,128]{3,2,1,0:T(4,128)(2,1)}, u32[]{:S(2)}, u32[]{:S(2)}) async-start(bf16[1024,1,4,128]{3,2,1,0:T(4,128)(2,1)} %pad_maximum_fusion.3), calls=%async_computation.1 | async-start | bytes 2097152 | tf_op jit(solution)/shard_map/all_to_all | solution.py:108
  223.3 250.4 %all-reduce.2.cloned.1.call-start = ((), (), s32[]{:S(2)}) async-start(), calls=%async_computation.3 | async-start | bytes 131072 | tf_op jit(solution)/shard_map/psum | solution.py:128
  230.1 1.2 copy-start.10
  230.1 1.5 copy-start.12
  230.1 2.2 copy-start.18
Sparse Core Ops, SparseCore 0:
  234.5 239.1 all-reduce.1
where the time goes:
time: 578 us; the launch traced here: 571 us
  waiting for transfers between devices  236 us (41%)
  local copies, waits for them, and re-layouts  108 us (19%)
  blocking collectives  74.6 us (13%)
  starting transfers between devices  49.3 us (9%)
  other arithmetic  48.2 us (8%)
  matrix products  40.4 us (7%)
  between operations  14.5 us (3%)
    psum x1, waiting for transfers between devices, shards(): mix_total, out_total = lax.psum((mix_part, out_part), ('rows', 'img'))  236 us
    psum x1, blocking collectives, shards(): mix_total, out_total = lax.psum((mix_part, out_part), ('rows', 'img'))  74.6 us
    unnamed x47, local copies, waits for them, and re-layouts  31.6 us
    another operation x4, other arithmetic  20.8 us
    sin x1, other arithmetic, column_table(): jnp.sin(phase)  17.6 us
    all_to_all x1, starting transfers between devices, shards(): lax.all_to_all(row_spec, 'rows', split_axis=1, concat_axis=0, tiled=True)  15.8 us
    all_to_all x1, starting transfers between devices, shards(): lax.all_to_all(back_cot, 'rows', split_axis=1, concat_axis=0, tiled=True)  13.2 us
    all_to_all x1, starting transfers between devices, shards(): lax.all_to_all(back_spec, 'rows', split_axis=0, concat_axis=1, tiled=True)  13.1 us
  transfers between devices with their start and end apart: 6, of which 1 were waited for; matrix products, arithmetic and copies ran while one was open for 30% of the time, Pallas kernels for 0%

commit v1 on v0

v1 whole, which is shorter than its diff:
```python
import math

import jax
import jax.numpy as jnp
import ml_dtypes
import numpy as np
from jax import lax
from jax.experimental import pallas as pl
from jax.experimental.pallas import tpu as pltpu
from jax.sharding import PartitionSpec as P

HEIGHT = 1024
WIDTH = 1024
SPEC_CH = 64
FREQS = 512
ROWS = 8
GROUPS = 128
PER_GROUP = 4
PAIR = 128
BF16 = jnp.bfloat16
F32 = jnp.float32
LIMIT = 56 * 1024 * 1024


def params():
    return pltpu.CompilerParams(vmem_limit_bytes=LIMIT)


def cost(flops, nbytes):
    return pl.CostEstimate(flops=flops, bytes_accessed=nbytes, transcendentals=0)


def row_tables():
    cols = np.arange(WIDTH)
    freq = np.arange(FREQS)
    phase = ((cols[:, None] * freq[None, :]) % WIDTH) * (2.0 * math.pi / WIDTH)
    forward = np.stack([np.cos(phase), -np.sin(phase)], axis=1) / math.sqrt(WIDTH)
    forward = forward.reshape(WIDTH, 2, GROUPS, PER_GROUP).transpose(0, 2, 1, 3)
    factor = np.where(freq == 0, 1.0, 2.0).reshape(1, GROUPS, 1, PER_GROUP)
    inverse = (forward * factor).reshape(WIDTH, 2 * FREQS)
    forward = np.ascontiguousarray(forward.reshape(WIDTH, 2 * FREQS).T)
    return forward.astype(ml_dtypes.bfloat16), inverse.astype(ml_dtypes.bfloat16)


def column_tables():
    idx = np.arange(GROUPS)
    phase = ((idx[:, None] * idx[None, :]) % GROUPS) * (2.0 * math.pi / GROUPS)
    cosine, sine = np.cos(phase) / math.sqrt(HEIGHT), np.sin(phase) / math.sqrt(HEIGHT)
    forward = np.block([[cosine, sine], [-sine, cosine]])
    backward = np.block([[cosine, -sine], [sine, cosine]])
    turn = (idx[:, None] * np.arange(ROWS)[None, :]) * (2.0 * math.pi / HEIGHT)
    twiddle = np.repeat(np.stack([np.cos(turn), np.sin(turn)]), SPEC_CH, axis=2)
    return (
        forward.astype(ml_dtypes.bfloat16),
        backward.astype(ml_dtypes.bfloat16),
        twiddle.astype(np.float32),
    )


def dot(a, b):
    return jnp.dot(a, b, preferred_element_type=F32)


def dot_t(a, b):
    return lax.dot_general(a, b, (((0,), (0,)), ((), ())), preferred_element_type=F32)


def iota(shape, dim):
    return lax.broadcasted_iota(jnp.int32, shape, dim)


def first_half():
    return jnp.where(iota((SPEC_CH, PAIR), 0) == iota((SPEC_CH, PAIR), 1), 1.0, 0.0).astype(BF16)


def second_half():
    hit = iota((SPEC_CH, PAIR), 0) + SPEC_CH == iota((SPEC_CH, PAIR), 1)
    return jnp.where(hit, 1.0, 0.0).astype(BF16)


def rows_kernel(maps, cot, in_w, out_w, table, spec_out, inner_out, both, in_pair, out_pair):
    step = pl.program_id(0)
    half = ROWS * SPEC_CH

    @pl.when(step == 0)
    def _():
        a, b = first_half(), second_half()
        in_pair[0:PAIR, :] = dot(in_w[...], a).astype(BF16)
        in_pair[PAIR:, :] = dot(in_w[...], b).astype(BF16)
        out_pair[0:PAIR, :] = dot_t(out_w[...], a).astype(BF16)
        out_pair[PAIR:, :] = dot_t(out_w[...], b).astype(BF16)

    @pl.when(step < 4)
    def _():
        start = pl.multiple_of(step * PAIR, PAIR)
        pair = jnp.concatenate([maps[0, 0], maps[0, 1]], axis=1)
        inner = jnp.maximum(dot(pair, in_pair[...]), 0.0).astype(BF16)
        both[:, pl.ds(start, PAIR)] = inner
        inner_out[:, pl.ds(start, PAIR)] = inner
        pair = jnp.concatenate([cot[0, 0], cot[0, 1]], axis=1)
        start = pl.multiple_of(half + step * PAIR, PAIR)
        both[:, pl.ds(start, PAIR)] = dot(pair, out_pair[...]).astype(BF16)

    @pl.when(step >= 4)
    def _():
        prod = dot(table[...], both[...])
        row = (step - 4) * 256 + iota((256, half), 0)
        factor = jnp.where((row == 0) | (row == PER_GROUP), 1.0, 2.0)
        spec_out[:, 0:half] = prod[:, 0:half].astype(BF16)
        spec_out[:, half:] = (prod[:, half:] * factor).astype(BF16)


def rows_forward(maps, cot, in_w, out_w, table):
    def block(i):
        return (0, jnp.minimum(i, 3), 0, 0)

    def late(i):
        return (jnp.maximum(i - 4, 0), 0)

    def whole(i):
        return (0, 0)

    return pl.pallas_call(
        rows_kernel,
        grid=(8,),
        in_specs=[
            pl.BlockSpec((1, 2, WIDTH, 128), block),
            pl.BlockSpec((1, 2, WIDTH, 128), block),
            pl.BlockSpec((128, SPEC_CH), whole),
            pl.BlockSpec((SPEC_CH, 128), whole),
            pl.BlockSpec((256, WIDTH), late),
        ],
        out_specs=[pl.BlockSpec((256, 1024), late), pl.BlockSpec((WIDTH, 512), whole)],
        out_shape=[
            jax.ShapeDtypeStruct((1024, 1024), BF16),
            jax.ShapeDtypeStruct((WIDTH, 512), BF16),
        ],
        scratch_shapes=[
            pltpu.VMEM((WIDTH, 1024), BF16),
            pltpu.VMEM((256, PAIR), BF16),
            pltpu.VMEM((256, PAIR), BF16),
        ],
        compiler_params=params(),
        cost_estimate=cost(5 * 10**9, 11 * 2**20),
    )(maps, cot, in_w, out_w, table)


ROOT = math.sqrt(0.5)


def lane_signs(shape):
    return jnp.where(iota(shape, 1) % PAIR < SPEC_CH, 1.0, -1.0).astype(F32)


def lane_butterfly(x, signs):
    return pltpu.roll(x, SPEC_CH, 1) + x * signs


def turn_second(re, im, first, real, imag):
    new_re = jnp.where(first, re, re * real - im * imag)
    new_im = jnp.where(first, im, re * imag + im * real)
    return new_re, new_im


EIGHTHS = ((1.0, 0.0), (ROOT, -ROOT), (0.0, -1.0), (-ROOT, -ROOT))


def spectrum_rows(prod, twiddle, rows, signs, first):
    re, im = [], []
    for m in range(4):
        lanes = slice(m * PAIR, (m + 1) * PAIR)
        a = prod[pl.ds(rows, RB), lanes]
        b = prod[pl.ds(GROUPS + rows, RB), lanes]
        c = twiddle[0, pl.ds(rows, RB), lanes]
        s = twiddle[1, pl.ds(rows, RB), lanes]
        re.append(a * c + b * s)
        im.append(b * c - a * s)
    s0r, s0i, d0r, d0i = re[0] + re[2], im[0] + im[2], re[0] - re[2], im[0] - im[2]
    s1r, s1i, d1r, d1i = re[1] + re[3], im[1] + im[3], re[1] - re[3], im[1] - im[3]
    four = (
        (s0r + s1r, s0i + s1i),
        (d0r + d1i, d0i - d1r),
        (s0r - s1r, s0i - s1i),
        (d0r - d1i, d0i + d1r),
    )
    out = []
    for q in range(4):
        zr, zi = four[q]
        if q:
            zr, zi = turn_second(zr, zi, first, *EIGHTHS[q])
        out.append((lane_butterfly(zr, signs), lane_butterfly(zi, signs)))
    return out


def inverse_rows(parts, twiddle, rows, signs, first):
    z = []
    for q in range(4):
        zr, zi = (lane_butterfly(x, signs) for x in parts[q])
        if q:
            zr, zi = turn_second(zr, zi, first, EIGHTHS[q][0], -EIGHTHS[q][1])
        z.append((zr, zi))
    s0r, s0i = z[0][0] + z[2][0], z[0][1] + z[2][1]
    d0r, d0i = z[0][0] - z[2][0], z[0][1] - z[2][1]
    s1r, s1i = z[1][0] + z[3][0], z[1][1] + z[3][1]
    d1r, d1i = z[1][0] - z[3][0], z[1][1] - z[3][1]
    four = (
        (s0r + s1r, s0i + s1i),
        (d0r - d1i, d0i + d1r),
        (s0r - s1r, s0i - s1i),
        (d0r + d1i, d0i - d1r),
    )
    out = []
    for m in range(4):
        lanes = slice(m * PAIR, (m + 1) * PAIR)
        c = twiddle[0, pl.ds(rows, RB), lanes]
        s = twiddle[1, pl.ds(rows, RB), lanes]
        a, b = four[m]
        out.append((a * c - b * s, b * c + a * s))
    return out


RB = 16


def fill_mix(mix_w, wide):
    total = jnp.zeros((256, 256), F32)
    for t in range(2):
        row, col = iota((256, 128), 0), iota((256, 128), 1)
        at = (row // PAIR) * SPEC_CH + row % SPEC_CH
        hit = (at == col) & (row // SPEC_CH % 2 == t)
        pick = jnp.where(hit, 1.0, 0.0).astype(BF16)
        left = dot(pick, mix_w[...]).astype(BF16)
        total = total + lax.dot_general(
            left, pick, (((1,), (1,)), ((), ())), preferred_element_type=F32
        )
    wide[...] = total.astype(BF16)


def sigmoid(x):
    return 1.0 / (1.0 + jnp.exp(-x))


def gather_parts(stage, kk):
    lanes = []
    for m in range(4):
        re = stage[m, pl.ds(kk, GROUPS, stride=ROWS), :]
        im = stage[m, pl.ds(PER_GROUP + kk, GROUPS, stride=ROWS), :]
        lanes.append(jnp.concatenate([re, im], axis=0).astype(BF16))
    return jnp.concatenate(lanes, axis=1)


def fill_stage(block, stage):
    for m in range(4):
        stage[m] = block[:, m * PAIR : (m + 1) * PAIR].astype(F32)


def columns_kernel(block, forward, backward, twiddle, mix_w, spec, back, stage, wide, prod, pre, inv):
    fill_mix(mix_w, wide)
    fill_stage(block, stage)
    signs = lane_signs((RB, PAIR))
    first = iota((RB, PAIR), 1) < SPEC_CH
    for kk in range(PER_GROUP):
        prod[...] = dot(forward[...], gather_parts(stage, kk))

        @pl.loop(0, GROUPS, step=RB)
        def _(rows):
            rows = pl.multiple_of(rows, RB)
            parts = spectrum_rows(prod, twiddle, rows, signs, first)
            for q in range(4):
                spec[kk * 4 + q, pl.ds(rows, RB), 0:PAIR] = parts[q][0].astype(BF16)
                spec[kk * 4 + q, pl.ds(rows, RB), PAIR:] = parts[q][1].astype(BF16)

        pre[...] = dot(spec[kk * 4 : kk * 4 + 4].reshape(512, 256), wide[...])

        @pl.loop(0, GROUPS, step=RB)
        def _(rows):
            rows = pl.multiple_of(rows, RB)
            parts = []
            for q in range(4):
                v = pre[pl.ds(q * GROUPS + rows, RB), :]
                v = v * sigmoid(v)
                parts.append((v[:, 0:PAIR], v[:, PAIR:]))
            pairs = inverse_rows(parts, twiddle, rows, signs, first)
            for m in range(4):
                lanes = slice(m * PAIR, (m + 1) * PAIR)
                inv[pl.ds(rows, RB), lanes] = pairs[m][0].astype(BF16)
                inv[pl.ds(GROUPS + rows, RB), lanes] = pairs[m][1].astype(BF16)

        result = dot(backward[...], inv[...])
        for m in range(4):
            lanes = slice(m * PAIR, (m + 1) * PAIR)
            stage[m, pl.ds(kk, GROUPS, stride=ROWS), :] = result[0:GROUPS, lanes]
            stage[m, pl.ds(PER_GROUP + kk, GROUPS, stride=ROWS), :] = result[GROUPS:, lanes]
    for m in range(4):
        back[:, m * PAIR : (m + 1) * PAIR] = stage[m].astype(BF16)


def whole_spec(shape):
    return pl.BlockSpec(shape, lambda *_: (0,) * len(shape))


def columns(block, forward, backward, twiddle, mix_w):
    return pl.pallas_call(
        columns_kernel,
        grid=(1,),
        in_specs=[
            pl.BlockSpec((1024, 512), lambda i: (0, 0)),
            whole_spec((256, 256)),
            whole_spec((256, 256)),
            whole_spec((2, GROUPS, 512)),
            whole_spec((128, 128)),
        ],
        out_specs=[whole_spec((16, GROUPS, 256)), whole_spec((1024, 512))],
        out_shape=[
            jax.ShapeDtypeStruct((16, GROUPS, 256), BF16),
            jax.ShapeDtypeStruct((1024, 512), BF16),
        ],
        scratch_shapes=[
            pltpu.VMEM((4, 1024, PAIR), F32),
            pltpu.VMEM((256, 256), BF16),
            pltpu.VMEM((256, 512), F32),
            pltpu.VMEM((512, 256), F32),
            pltpu.VMEM((256, 512), BF16),
        ],
        compiler_params=params(),
        cost_estimate=cost(8 * 10**9, 5 * 2**20),
    )(block, forward, backward, twiddle, mix_w)


def mix_kernel(block, spec, forward, twiddle, mix_w, grad, stage, wide, prod, pre, slope, acc):
    fill_mix(mix_w, wide)
    fill_stage(block, stage)
    signs = lane_signs((RB, PAIR))
    first = iota((RB, PAIR), 1) < SPEC_CH
    acc[...] = jnp.zeros_like(acc)
    for kk in range(PER_GROUP):
        prod[...] = dot(forward[...], gather_parts(stage, kk))
        pre[...] = dot(spec[kk * 4 : kk * 4 + 4].reshape(512, 256), wide[...])

        @pl.loop(0, GROUPS, step=RB)
        def _(rows):
            rows = pl.multiple_of(rows, RB)
            parts = spectrum_rows(prod, twiddle, rows, signs, first)
            for q in range(4):
                for part in range(2):
                    lanes = slice(part * PAIR, (part + 1) * PAIR)
                    v = pre[pl.ds(q * GROUPS + rows, RB), lanes]
                    s = sigmoid(v)
                    v = parts[q][part] * (s * (1.0 + v * (1.0 - s)))
                    slope[pl.ds(q * GROUPS + rows, RB), lanes] = v.astype(BF16)

        acc[...] += dot_t(slope[...], spec[kk * 4 : kk * 4 + 4].reshape(512, 256))
    lane = iota((SPEC_CH, PAIR), 1) < SPEC_CH
    for part in range(2):
        even = acc[part * PAIR : part * PAIR + SPEC_CH, :]
        odd = acc[part * PAIR + SPEC_CH : (part + 1) * PAIR, :]
        real = even[:, 0:PAIR] + pltpu.roll(odd[:, 0:PAIR], SPEC_CH, 1)
        imag = pltpu.roll(even[:, PAIR:], SPEC_CH, 1) + odd[:, PAIR:]
        grad[part * SPEC_CH : (part + 1) * SPEC_CH, :] = jnp.where(lane, real, imag)


def mix_terms(block, spec, forward, twiddle, mix_w):
    return pl.pallas_call(
        mix_kernel,
        grid=(1,),
        in_specs=[
            pl.BlockSpec((1024, 512), lambda i: (0, 1)),
            whole_spec((16, GROUPS, 256)),
            whole_spec((256, 256)),
            whole_spec((2, GROUPS, 512)),
            whole_spec((128, 128)),
        ],
        out_specs=whole_spec((128, 128)),
        out_shape=jax.ShapeDtypeStruct((128, 128), F32),
        scratch_shapes=[
            pltpu.VMEM((4, 1024, PAIR), F32),
            pltpu.VMEM((256, 256), BF16),
            pltpu.VMEM((256, 512), F32),
            pltpu.VMEM((512, 256), F32),
            pltpu.VMEM((512, 256), BF16),
            pltpu.VMEM((256, 256), F32),
        ],
        compiler_params=params(),
        cost_estimate=cost(6 * 10**9, 5 * 2**20),
    )(block, spec, forward, twiddle, mix_w)


def back_kernel(table, rows, inner, cot, mix_part, summed, terms, acc):
    step = pl.program_id(0)

    @pl.when(step == 0)
    def _():
        acc[...] = jnp.zeros_like(acc)

    total = (dot(table[...], rows[...]) + inner[...].astype(F32)).astype(BF16)
    summed[...] = total
    for p in range(4):
        pair = jnp.concatenate([cot[0, 2 * p], cot[0, 2 * p + 1]], axis=1)
        acc[...] += dot_t(pair, total[:, p * PAIR : (p + 1) * PAIR])

    @pl.when(step == 3)
    def _():
        lane = iota((128, PAIR), 1) < SPEC_CH
        out_part = acc[0:128, :] + pltpu.roll(acc[128:, :], SPEC_CH, 1)
        terms[:, 0:128] = mix_part[...]
        terms[:, 128:] = jnp.where(lane, out_part, 0.0)


def back_rows(table, rows, inner, cot, mix_part):
    return pl.pallas_call(
        back_kernel,
        grid=(4,),
        in_specs=[
            pl.BlockSpec((256, 1024), lambda i: (i, 0)),
            whole_spec((1024, 512)),
            pl.BlockSpec((256, 512), lambda i: (i, 0)),
            pl.BlockSpec((1, ROWS, 256, 128), lambda i: (0, 0, i, 0)),
            whole_spec((128, 128)),
        ],
        out_specs=[pl.BlockSpec((256, 512), lambda i: (i, 0)), whole_spec((128, 256))],
        out_shape=[
            jax.ShapeDtypeStruct((WIDTH, 512), BF16),
            jax.ShapeDtypeStruct((128, 256), F32),
        ],
        scratch_shapes=[pltpu.VMEM((256, 128), F32)],
        compiler_params=params(),
        cost_estimate=cost(2 * 10**9, 8 * 2**20),
    )(table, rows, inner, cot, mix_part)


def out_kernel(summed, out_w, out, wide):
    @pl.when(pl.program_id(0) == 0)
    def _():
        zero = jnp.zeros((SPEC_CH, 128), BF16)
        wide[0:SPEC_CH, :] = jnp.concatenate([out_w[...], zero], axis=1)
        wide[SPEC_CH:, :] = jnp.concatenate([zero, out_w[...]], axis=1)

    for p in range(4):
        prod = dot(summed[:, p * PAIR : (p + 1) * PAIR], wide[...]).astype(BF16)
        out[0, 2 * p] = prod[:, 0:128]
        out[0, 2 * p + 1] = prod[:, 128:]


def project_out(summed, out_w):
    return pl.pallas_call(
        out_kernel,
        grid=(4,),
        in_specs=[pl.BlockSpec((256, 512), lambda i: (i, 0)), whole_spec((SPEC_CH, 128))],
        out_specs=pl.BlockSpec((1, ROWS, 256, 128), lambda i: (0, 0, i, 0)),
        out_shape=jax.ShapeDtypeStruct((1, ROWS, WIDTH, 128), BF16),
        scratch_shapes=[pltpu.VMEM((128, 256), BF16)],
        compiler_params=params(),
        cost_estimate=cost(5 * 10**8, 3 * 2**20),
    )(summed, out_w)


def extended(cells):
    ends = GROUPS - 1
    head, tail = cells[:, 0:1], cells[:, ROWS - 1 :]
    above = lax.ppermute(tail, "rows", [(i, i + 1) for i in range(ends)])
    below = lax.ppermute(head, "rows", [(i + 1, i) for i in range(ends)])
    return jnp.concatenate([above, cells, below], axis=1)


def exchange(block):
    lanes = block.shape[1]
    moved = lax.all_to_all(
        block.reshape(GROUPS, ROWS, lanes), "rows", split_axis=0, concat_axis=0, tiled=True
    )
    return moved.reshape(GROUPS * ROWS, lanes)


def shards(local_maps, global_maps, conv_weight, in_weight, mix_weight, out_weight, out_cotangent):
    row_fwd, row_inv = row_tables()
    forward, backward, twiddle = column_tables()
    spec_rows, inner = rows_forward(global_maps, out_cotangent, in_weight, out_weight, row_fwd)
    spec_cols = exchange(spec_rows)
    padded = extended(local_maps)
    local_out = lax.conv_general_dilated(
        padded,
        conv_weight,
        (1, 1),
        ((0, 0), (1, 1)),
        dimension_numbers=("NHWC", "HWIO", "NHWC"),
        preferred_element_type=F32,
    ).astype(BF16)
    spectrum, back_cols = columns(spec_cols, forward, backward, twiddle, mix_weight)
    back = exchange(back_cols)
    mix_part = mix_terms(spec_cols, spectrum, forward, twiddle, mix_weight)
    summed, terms = back_rows(row_inv, back, inner, out_cotangent, mix_part)
    terms = jnp.broadcast_to(terms.reshape(128, 1, 2, 128), (128, 2, 2, 128)).reshape(256, 2, 128)
    terms = lax.all_to_all(terms, ("rows", "img"), split_axis=0, concat_axis=0, tiled=True)
    global_out = project_out(summed, out_weight)
    total = jnp.sum(terms, axis=0)
    mix_grad = total[0].reshape(128, 1)
    out_grad = total[1, 0:SPEC_CH].reshape(SPEC_CH, 1)
    return (local_out, global_out, mix_grad, out_grad)


def solution(mesh):
    maps = P("img", "rows", None, None)
    in_specs = (maps, maps, P(), P(), P(), P(), maps)
    out_specs = (maps, maps, P(None, "rows"), P(None, "rows"))
    return jax.shard_map(shards, mesh=mesh, in_specs=in_specs, out_specs=out_specs, check_vma=False)
```

time: 578 us -> 178 us (0.31); the launches traced: 571 us -> 177 us
  waiting for transfers between devices: 236 us -> 13.8 us
  local copies, waits for them, and re-layouts: 108 us -> 14.1 us
  other arithmetic: 48.2 us -> 0.6 us
  Pallas kernels: 0 us -> 39.9 us
  matrix products: 40.4 us -> 5.33 us
  starting transfers between devices: 49.3 us -> 33.9 us
  between operations: 14.5 us -> 0.78 us
  blocking collectives: 74.6 us -> 68.8 us
    psum x1 -> x0, waiting for transfers between devices: 236 us -> none  [shards(): mix_total, out_total = lax.psum((mix_part, out_part), ('rows', 'img'))]
    psum x1 -> x0, blocking collectives: 74.6 us -> none  [shards(): mix_total, out_total = lax.psum((mix_part, out_part), ('rows', 'img'))]
    all_to_all x0 -> x1, blocking collectives: none -> 68.8 us  [exchange(): lax.all_to_all(block.reshape(GROUPS, ROWS, lanes), 'rows', split_axis=0,...]
    pallas_call x0 -> x5, Pallas kernels: none -> 39.9 us  [the longest x1 12.4 us: columns(): pl.pallas_call(columns_kernel, grid=(1,), in_specs=[pl.BlockSpec((1024, 5...]
    dot_general x11 -> x0, matrix products: 35.1 us -> none  [the longest x2 12.4 us: forward_columns(): jnp.dot(column, block.reshape(block.shape[0], -1), preferred_element_type...]
    unnamed x47 -> x12, local copies, waits for them, and re-layouts: 31.6 us -> 4.66 us
    another operation x6 -> x0, other arithmetic: 23.8 us -> none
    sin x1 -> x0, other arithmetic: 17.6 us -> none  [column_table(): jnp.sin(phase)]
  transfers between devices with their start and end apart: 6 -> 4, of which waited for: 1 -> 4; matrix products, arithmetic and copies ran while one was open for 30% -> 8% of each run, Pallas kernels for 0% -> 7%
where the time goes in v1:
time: 178 us; the launch traced here: 177 us
  blocking collectives  68.8 us (39%)
  Pallas kernels  39.9 us (22%)
  starting transfers between devices  33.9 us (19%)
  local copies, waits for them, and re-layouts  14.1 us (8%)
  waiting for transfers between devices  13.8 us (8%)
  matrix products  5.33 us (3%)
    all_to_all x1, blocking collectives, exchange(): lax.all_to_all(block.reshape(GROUPS, ROWS, lanes), 'rows', split_axis=0,...  68.8 us
    all_to_all x1, starting transfers between devices, shards(): lax.all_to_all(terms, ('rows', 'img'), split_axis=0, concat_axis=0, tiled...  22.9 us
    pallas_call x1, Pallas kernels, columns(): pl.pallas_call(columns_kernel, grid=(1,), in_specs=[pl.BlockSpec((1024, 5...  12.4 us
    pallas_call x1, Pallas kernels, rows_forward(): pl.pallas_call(rows_kernel, grid=(8,), in_specs=[pl.BlockSpec((1, 2, WIDT...  9.37 us
    pallas_call x1, Pallas kernels, mix_terms(): pl.pallas_call(mix_kernel, grid=(1,), in_specs=[pl.BlockSpec((1024, 512),...  7.77 us
    all_to_all x1, starting transfers between devices, exchange(): lax.all_to_all(block.reshape(GROUPS, ROWS, lanes), 'rows', split_axis=0,...  6.43 us
    pallas_call x1, Pallas kernels, back_rows(): pl.pallas_call(back_kernel, grid=(4,), in_specs=[pl.BlockSpec((256, 1024)...  6.28 us
    conv_general_dilated x1, matrix products, shards(): lax.conv_general_dilated(padded, conv_weight, (1, 1), ((0, 0), (1, 1)), d...  5.33 us
  transfers between devices with their start and end apart: 4, of which 4 were waited for; matrix products, arithmetic and copies ran while one was open for 8% of the time, Pallas kernels for 7%

profile of v1, /device:TPU:1, one launch (start us, length us, event | category | flops | bytes accessed | tf_op | source)
XLA Modules:
  0.0 177.2 jit_solution(10625887092615284671)
XLA Ops:
  0.6 0.0 copy-start
  0.6 1.5 copy.31.in_w
  2.1 9.4 %shard_map.147 = (bf16[1024,1024]{1,0:T(8,128)(2,1)}, bf16[1024,512]{1,0:T(8,128)(2,1)}) custom-call(bf16[1,8,1024,128]{3,2,1,0:T(8,128)(2,1)} %maps.1, bf16[1,8,1024,128]{3,2,1,0:T(8,128)(2,1)} %cot.3, bf16[128,64]{1,0:T(8,128)(2,1)} %copy.31.in_w, bf16[64,128]{1,0:T(8,128)(2,1)} %out_w.3, bf16[1024,1024]{1,0:T(8,128)(2,1)} %constant.12.clone.table), custom_call_target="tpu_custom_call" | custom-call | flops 5000000000 | bytes 11534336 | tf_op jit(solution)/shard_map/pallas_call | solution.py:123
  11.5 68.8 %all_to_all.15 = bf16[128,8,1024]{2,1,0:T(8,128)(2,1)} all-to-all(bf16[128,8,1024]{2,1,0:T(8,128)(2,1)} %bitcast.27), channel_id=1, replica_groups=mesh['rows'=128,'img'=2] {'rows'}, dimensions={0} | all-to-all | bytes 4194304 | tf_op jit(solution)/shard_map/all_to_all | solution.py:467
  80.3 0.0 copy-start.1
  80.3 12.4 %shard_map.148 = (bf16[16,128,256]{2,1,0:T(8,128)(2,1)}, bf16[1024,512]{1,0:T(8,128)(2,1)}) custom-call(bf16[1024,1024]{1,0:T(8,128)(2,1)} %bitcast.25, bf16[256,256]{1,0:T(8,128)(2,1)} %constant.13.clone.forward, bf16[256,256]{1,0:T(8,128)(2,1)} %constant.14.clone.backward, f32[2,128,512]{2,1,0:T(8,128)} %constant.15.clone.twiddle, bf16[128,128]{1,0:T(8,128)(2,1)} %mix_w.3), custom_call_target="tpu_custom_call" | custom-call | flops 8000000000 | bytes 5242880 | tf_op jit(solution)/shard_map/pallas_call | solution.py:303
  92.7 6.4 %all-to-all-start.1 = ((bf16[128,8,512]{2,1,0:T(8,128)(2,1)}), bf16[128,8,512]{2,1,0:T(8,128)(2,1)}, u32[]{:S(2)}, u32[]{:S(2)}) async-start(bf16[128,8,512]{2,1,0:T(8,128)(2,1)} %bitcast.28), calls=%async_computation.1 | async-start | bytes 2097152 | tf_op jit(solution)/shard_map/all_to_all | solution.py:467
  99.1 0.0 copy-done.1
  99.2 2.4 %collective-permute-start = (bf16[1,1,1024,128]{3,2,1,0:T(8,128)(2,1)S(1)}, bf16[1,1,1024,128]{3,2,1,0:T(8,128)(2,1)S(1)}, u32[]{:S(2)}, u32[]{:S(2)}) collective-permute-start(bf16[1,1,1024,128]{3,2,1,0:T(8,128)(2,1)S(1)} %get-tuple-element.28), channel_id=1, source_target_pairs={{0,2},{2,4},{4,6},{6,8},{8,10},{10,12},{12,14},{14,16},{16,18},{18... | collective-permute-start | bytes 786440 | tf_op jit(solution)/shard_map/ppermute | solution.py:460
  101.6 2.1 %collective-permute-start.1 = (bf16[1,1,1024,128]{3,2,1,0:T(8,128)(2,1)S(1)}, bf16[1,1,1024,128]{3,2,1,0:T(8,128)(2,1)S(1)}, u32[]{:S(2)}, u32[]{:S(2)}) collective-permute-start(bf16[1,1,1024,128]{3,2,1,0:T(8,128)(2,1)S(1)} %get-tuple-element.29), channel_id=1, source_target_pairs={{2,0},{4,2},{6,4},{8,6},{10,8},{12,10},{14,12},{16,14},{18,16},{20... | collective-permute-start | bytes 786440 | tf_op jit(solution)/shard_map/ppermute | solution.py:461
  103.7 3.3 %collective-permute-done = bf16[1,1,1024,128]{3,2,1,0:T(8,128)(2,1)S(1)} collective-permute-done((bf16[1,1,1024,128]{3,2,1,0:T(8,128)(2,1)S(1)}, bf16[1,1,1024,128]{3,2,1,0:T(8,128)(2,1)S(1)}, u32[]{:S(2)}, u32[]{:S(2)}) %collective-permute-start) | collective-permute-done | bytes 262176 | tf_op jit(solution)/shard_map/ppermute | solution.py:460
  107.0 5.0 %collective-permute-done.1 = bf16[1,1,1024,128]{3,2,1,0:T(8,128)(2,1)S(1)} collective-permute-done((bf16[1,1,1024,128]{3,2,1,0:T(8,128)(2,1)S(1)}, bf16[1,1,1024,128]{3,2,1,0:T(8,128)(2,1)S(1)}, u32[]{:S(2)}, u32[]{:S(2)}) %collective-permute-start.1) | collective-permute-done | bytes 262176 | tf_op jit(solution)/shard_map/ppermute | solution.py:461
  112.0 0.3 maximum_bitcast_fusion
  112.3 2.2 %pad = bf16[10,1,1032,128]{3,2,0,1:T(8,128)(2,1)} pad(bf16[10,1,1024,128]{3,2,0,1:T(8,128)(2,1)S(1)} %maximum_bitcast_fusion, bf16[]{:T(256)} %constant.20), padding=0_0x0_0x1_7x0_0 | pad | bytes 5263362 | tf_op jit(solution)/shard_map/concatenate | solution.py:462
  114.5 3.7 %reshape.32 = bf16[10,1,8,129,128]{4,3,2,0,1:T(8,128)(2,1)S(1)} reshape(bf16[10,1,1032,128]{3,2,0,1:T(8,128)(2,1)} %pad) | data formatting | bytes 5283840 | tf_op jit(solution)/shard_map/conv_general_dilated | solution.py:479
  118.2 0.3 copy.29
  118.5 0.0 copy-start.2
  118.5 1.5 copy-done.2
  120.1 7.8 %shard_map.149.mix_part = f32[128,128]{1,0:T(8,128)} custom-call(bf16[1024,1024]{1,0:T(8,128)(2,1)} %bitcast.26, bf16[16,128,256]{2,1,0:T(8,128)(2,1)} %get-tuple-element.13.spec, bf16[256,256]{1,0:T(8,128)(2,1)} %constant.13.clone.forward, f32[2,128,512]{2,1,0:T(8,128)} %constant.15.clone.twiddle, bf16[128,128]{1,0:T(8,128)(2,1)} %mix_w.3), custom_call_target="tpu_custom_call" | custom-call | flops 6000000000 | bytes 5242880 | tf_op jit(solution)/shard_map/pallas_call | solution.py:363
  127.8 1.4 all-to-all-done.1
  129.3 0.0 copy-start.3
  129.3 0.0 copy-start.4
  129.3 6.3 %shard_map.150 = (bf16[1024,512]{1,0:T(8,128)(2,1)}, f32[128,256]{1,0:T(8,128)}) custom-call(bf16[1024,1024]{1,0:T(8,128)(2,1)} %constant.16.clone.table, bf16[1024,512]{1,0:T(8,128)(2,1)} %bitcast.7.rows, bf16[1024,512]{1,0:T(8,128)(2,1)} %get-tuple-element.12.inner, bf16[1,8,1024,128]{3,2,1,0:T(8,128)(2,1)} %cot.3, f32[128,128]{1,0:T(8,128)} %shard_map.149.mix_part), custom_call_target="tpu_custom_call" | custom-call | flops 2000000000 | bytes 8388608 | tf_op jit(solution)/shard_map/pallas_call | solution.py:410
  135.6 1.0 broadcast_in_dim.7
  136.5 0.8 broadcast_in_dim.8
  137.3 22.9 %all-to-all-start.2 = ((f32[256,2,128]{2,1,0:T(2,128)}), f32[256,2,128]{2,1,0:T(2,128)S(1)}, u32[]{:S(2)}, u32[]{:S(2)}) async-start(f32[256,2,128]{2,1,0:T(2,128)} %bitcast.8), calls=%async_computation.2 | async-start | bytes 524288 | tf_op jit(solution)/shard_map/all_to_all | solution.py:492
  160.3 0.0 copy-done
  160.3 0.0 copy-done.3
  160.3 0.0 copy-done.4
  160.3 5.3 %select_convert_fusion = bf16[8,8,129,128]{3,1,2,0:T(8,128)(2,1)S(1)} fusion(pred[8,129]{0,1:T(8,128)(4,1)S(1)} %copy-done.4, bf16[3,3,128,128]{3,2,1,0:T(8,128)(2,1)S(1)} %copy-done, bf16[10,1,7,2,128]{4,2,3,0,1:T(8,128)(2,1)S(1)} %slice.18, bf16[10,1,8,129,128]{4,2,3,0,1:T(8,128)(2,1)S(1)} %copy-done.3), kind=kOutput, calls=%fused_computation.2 | convolution fusion | flops 2444955648 | bytes 5087240 | tf_op jit(solution)/shard_map/conv_general_dilated | solution.py:479
  165.7 0.3 copy.30
  165.9 0.1 slice_bitcast_fusion
  166.1 1.7 copy.33
  167.7 4.1 %shard_map.151 = bf16[1,8,1024,128]{3,2,1,0:T(8,128)(2,1)} custom-call(bf16[1024,512]{1,0:T(8,128)(2,1)} %get-tuple-element.14.summed, bf16[64,128]{1,0:T(8,128)(2,1)} %out_w.3), custom_call_target="tpu_custom_call" | custom-call | flops 500000000 | bytes 3145728 | tf_op jit(solution)/shard_map/pallas_call | solution.py:445
  171.8 4.1 %all-to-all-done.2 = f32[256,2,128]{2,1,0:T(2,128)S(1)} async-done(((f32[256,2,128]{2,1,0:T(2,128)}), f32[256,2,128]{2,1,0:T(2,128)S(1)}, u32[]{:S(2)}, u32[]{:S(2)}) %all-to-all-start.2) | async-done | bytes 262176 | tf_op jit(solution)/shard_map/all_to_all | solution.py:492
  175.9 0.3 reduce_sum.9
  176.2 0.5 slice_bitcast_fusion.2
  176.7 0.5 slice_bitcast_fusion.1
  (2 shorter events, 0.1 us)
Async XLA Ops:
  0.6 159.7 %copy-start = (bf16[3,3,128,128]{3,2,1,0:T(8,128)(2,1)S(1)}, bf16[3,3,128,128]{3,2,1,0:T(8,128)(2,1)}, u32[]{:S(2)}) copy-start(bf16[3,3,128,128]{3,2,1,0:T(8,128)(2,1)} %param.14) | copy-start | bytes 884740
  80.3 18.8 %copy-start.1 = (bf16[1,8,1024,128]{3,2,1,0:T(8,128)(2,1)S(1)}, bf16[1,8,1024,128]{3,2,1,0:T(8,128)(2,1)}, u32[]{:S(2)}) copy-start(bf16[1,8,1024,128]{3,2,1,0:T(8,128)(2,1)} %param.12) | copy-start | bytes 6291460
  92.7 36.6 %all-to-all-start.1 = ((bf16[128,8,512]{2,1,0:T(8,128)(2,1)}), bf16[128,8,512]{2,1,0:T(8,128)(2,1)}, u32[]{:S(2)}, u32[]{:S(2)}) async-start(bf16[128,8,512]{2,1,0:T(8,128)(2,1)} %bitcast.28), calls=%async_computation.1 | async-start | bytes 2097152 | tf_op jit(solution)/shard_map/all_to_all | solution.py:467
  99.2 7.8 %collective-permute-start = (bf16[1,1,1024,128]{3,2,1,0:T(8,128)(2,1)S(1)}, bf16[1,1,1024,128]{3,2,1,0:T(8,128)(2,1)S(1)}, u32[]{:S(2)}, u32[]{:S(2)}) collective-permute-start(bf16[1,1,1024,128]{3,2,1,0:T(8,128)(2,1)S(1)} %get-tuple-element.28), channel_id=1, source_target_pairs={{0,2},{2,4},{4,6},{6,8},{8,10},{10,12},{12,14},{14,16},{16,18},{18... | collective-permute-start | bytes 786440 | tf_op jit(solution)/shard_map/ppermute | solution.py:460
  101.6 10.4 %collective-permute-start.1 = (bf16[1,1,1024,128]{3,2,1,0:T(8,128)(2,1)S(1)}, bf16[1,1,1024,128]{3,2,1,0:T(8,128)(2,1)S(1)}, u32[]{:S(2)}, u32[]{:S(2)}) collective-permute-start(bf16[1,1,1024,128]{3,2,1,0:T(8,128)(2,1)S(1)} %get-tuple-element.29), channel_id=1, source_target_pairs={{2,0},{4,2},{6,4},{8,6},{10,8},{12,10},{14,12},{16,14},{18,16},{20... | collective-permute-start | bytes 786440 | tf_op jit(solution)/shard_map/ppermute | solution.py:461
  118.5 1.5 copy-start.2
  129.3 31.0 %copy-start.3 = (bf16[10,1,8,129,128]{4,2,3,0,1:T(8,128)(2,1)S(1)}, bf16[10,1,8,129,128]{4,2,3,0,1:T(8,128)(2,1)}, u32[]{:S(2)}) copy-start(bf16[10,1,8,129,128]{4,2,3,0,1:T(8,128)(2,1)} %copy-done.2) | copy-start | bytes 7925764
  129.3 31.0 %copy-start.4 = (pred[8,129]{0,1:T(8,128)(4,1)S(1)}, pred[8,129]{0,1:T(8,128)(4,1)}, u32[]{:S(2)}) copy-start(pred[8,129]{0,1:T(8,128)(4,1)} %constant.24) | copy-start | bytes 3100
  137.3 38.6 %all-to-all-start.2 = ((f32[256,2,128]{2,1,0:T(2,128)}), f32[256,2,128]{2,1,0:T(2,128)S(1)}, u32[]{:S(2)}, u32[]{:S(2)}) async-start(f32[256,2,128]{2,1,0:T(2,128)} %bitcast.8), calls=%async_computation.2 | async-start | bytes 524288 | tf_op jit(solution)/shard_map/all_to_all | solution.py:492

commit v2 on v1

--- a/solution.py
+++ b/solution.py
@@ -85,8 +85,8 @@
     @pl.when(step == 0)
     def _():
         a, b = first_half(), second_half()
-        in_pair[0:PAIR, :] = dot(in_w[...], a).astype(BF16)
-        in_pair[PAIR:, :] = dot(in_w[...], b).astype(BF16)
+        in_pair[0:PAIR, :] = dot_t(in_w[...], a).astype(BF16)
+        in_pair[PAIR:, :] = dot_t(in_w[...], b).astype(BF16)
         out_pair[0:PAIR, :] = dot_t(out_w[...], a).astype(BF16)
         out_pair[PAIR:, :] = dot_t(out_w[...], b).astype(BF16)
 
@@ -126,7 +126,7 @@
         in_specs=[
             pl.BlockSpec((1, 2, WIDTH, 128), block),
             pl.BlockSpec((1, 2, WIDTH, 128), block),
-            pl.BlockSpec((128, SPEC_CH), whole),
+            pl.BlockSpec((SPEC_CH, 128), whole),
             pl.BlockSpec((SPEC_CH, 128), whole),
             pl.BlockSpec((256, WIDTH), late),
         ],
@@ -254,7 +254,8 @@
         stage[m] = block[:, m * PAIR : (m + 1) * PAIR].astype(F32)
 
 
-def columns_kernel(block, forward, backward, twiddle, mix_w, spec, back, stage, wide, prod, pre, inv):
+def columns_kernel(block, forward, backward, twiddle, mix_w, ready, spec, back, stage, wide, prod, pre, inv):
+    del ready
     fill_mix(mix_w, wide)
     fill_stage(block, stage)
     signs = lane_signs((RB, PAIR))
@@ -299,7 +300,7 @@
     return pl.BlockSpec(shape, lambda *_: (0,) * len(shape))
 
 
-def columns(block, forward, backward, twiddle, mix_w):
+def columns(block, forward, backward, twiddle, mix_w, ready):
     return pl.pallas_call(
         columns_kernel,
         grid=(1,),
@@ -309,6 +310,7 @@
             whole_spec((256, 256)),
             whole_spec((2, GROUPS, 512)),
             whole_spec((128, 128)),
+            pl.BlockSpec(memory_space=pl.ANY),
         ],
         out_specs=[whole_spec((16, GROUPS, 256)), whole_spec((1024, 512))],
         out_shape=[
@@ -324,7 +326,7 @@
         ],
         compiler_params=params(),
         cost_estimate=cost(8 * 10**9, 5 * 2**20),
-    )(block, forward, backward, twiddle, mix_w)
+    )(block, forward, backward, twiddle, mix_w, ready)
 
 
 def mix_kernel(block, spec, forward, twiddle, mix_w, grad, stage, wide, prod, pre, slope, acc):
@@ -385,7 +387,8 @@
     )(block, spec, forward, twiddle, mix_w)
 
 
-def back_kernel(table, rows, inner, cot, mix_part, summed, terms, acc):
+def back_kernel(table, rows, inner, cot, mix_part, above, below, summed, terms, acc):
+    del above, below
     step = pl.program_id(0)
 
     @pl.when(step == 0)
@@ -402,11 +405,13 @@
     def _():
         lane = iota((128, PAIR), 1) < SPEC_CH
         out_part = acc[0:128, :] + pltpu.roll(acc[128:, :], SPEC_CH, 1)
-        terms[:, 0:128] = mix_part[...]
-        terms[:, 128:] = jnp.where(lane, out_part, 0.0)
-
-
-def back_rows(table, rows, inner, cot, mix_part):
+        out_part = jnp.where(lane, out_part, 0.0)
+        for img in range(2):
+            terms[pl.ds(2 * img, 128, stride=4), :] = mix_part[...]
+            terms[pl.ds(2 * img + 1, 128, stride=4), :] = out_part
+
+
+def back_rows(table, rows, inner, cot, mix_part, above, below):
     return pl.pallas_call(
         back_kernel,
         grid=(4,),
@@ -416,16 +421,18 @@
             pl.BlockSpec((256, 512), lambda i: (i, 0)),
             pl.BlockSpec((1, ROWS, 256, 128), lambda i: (0, 0, i, 0)),
             whole_spec((128, 128)),
-        ],
-        out_specs=[pl.BlockSpec((256, 512), lambda i: (i, 0)), whole_spec((128, 256))],
+            pl.BlockSpec(memory_space=pl.ANY),
+            pl.BlockSpec(memory_space=pl.ANY),
+        ],
+        out_specs=[pl.BlockSpec((256, 512), lambda i: (i, 0)), whole_spec((512, 128))],
         out_shape=[
             jax.ShapeDtypeStruct((WIDTH, 512), BF16),
-            jax.ShapeDtypeStruct((128, 256), F32),
+            jax.ShapeDtypeStruct((512, 128), F32),
         ],
         scratch_shapes=[pltpu.VMEM((256, 128), F32)],
         compiler_params=params(),
         cost_estimate=cost(2 * 10**9, 8 * 2**20),
-    )(table, rows, inner, cot, mix_part)
+    )(table, rows, inner, cot, mix_part, above, below)
 
 
 def out_kernel(summed, out_w, out, wide):
@@ -454,12 +461,85 @@
     )(summed, out_w)
 
 
-def extended(cells):
+def conv_row(top, mid, bottom, weight, out, sums, wide):
+    @pl.when(pl.program_id(0) == 0)
+    def _():
+        for a in range(3):
+            for b in range(3):
+                wide[a * 128 : (a + 1) * 128, b * 128 : (b + 1) * 128] = weight[a, b]
+        sums[0, 0:8] = jnp.zeros((8, 128), F32)
+        sums[2, WIDTH + 8 :] = jnp.zeros((8, 128), F32)
+
+    prod = dot(jnp.concatenate([top, mid, bottom], axis=1), wide[...])
+    for b in range(3):
+        sums[b, 8 : WIDTH + 8] = prod[:, b * 128 : (b + 1) * 128]
+    total = sums[0, 7 : WIDTH + 7] + sums[1, 8 : WIDTH + 8] + sums[2, 9 : WIDTH + 9]
+    out[0, 0] = total.astype(BF16)
+
+
+def inner_kernel(above, mid, below, weight, ready, out, sums, wide):
+    del ready
+    conv_row(above[0, 0], mid[0, 0], below[0, 0], weight, out, sums, wide)
+
+
+def edge_kernel(mid, beside, edge_above, edge_below, weight, done, ready, out, sums, wide):
+    del done, ready
+    first = pl.program_id(0) == 0
+    top = jnp.where(first, edge_above[0, 0], beside[0, 0])
+    bottom = jnp.where(first, beside[0, 0], edge_below[0, 0])
+    conv_row(top, mid[0, 0], bottom, weight, out, sums, wide)
+
+
+def row_spec(index):
+    return pl.BlockSpec((1, 1, WIDTH, 128), lambda i: (0, index(i), 0, 0))
+
+
+def conv_call(kernel, rows, in_specs, out_index, aliases, args):
+    return pl.pallas_call(
+        kernel,
+        grid=(rows,),
+        in_specs=in_specs,
+        out_specs=row_spec(out_index),
+        out_shape=jax.ShapeDtypeStruct((1, ROWS, WIDTH, 128), BF16),
+        scratch_shapes=[pltpu.VMEM((3, WIDTH + 16, 128), F32), pltpu.VMEM((384, 384), BF16)],
+        input_output_aliases=aliases,
+        compiler_params=params(),
+        cost_estimate=cost(rows * 10**9, rows * 2**20),
+    )(*args)
+
+
+def inner_rows(cells, weight, ready):
+    specs = [
+        row_spec(lambda i: i),
+        row_spec(lambda i: i + 1),
+        row_spec(lambda i: i + 2),
+        whole_spec((3, 3, 128, 128)),
+        pl.BlockSpec(memory_space=pl.ANY),
+    ]
+    args = (cells, cells, cells, weight, ready)
+    return conv_call(inner_kernel, ROWS - 2, specs, lambda i: i + 1, {}, args)
+
+
+def neighbour_rows(cells):
     ends = GROUPS - 1
     head, tail = cells[:, 0:1], cells[:, ROWS - 1 :]
     above = lax.ppermute(tail, "rows", [(i, i + 1) for i in range(ends)])
     below = lax.ppermute(head, "rows", [(i + 1, i) for i in range(ends)])
-    return jnp.concatenate([above, cells, below], axis=1)
+    return above, below
+
+
+def edge_rows(cells, above, below, weight, done, ready):
+    specs = [
+        row_spec(lambda i: i * (ROWS - 1)),
+        row_spec(lambda i: 1 + i * (ROWS - 3)),
+        whole_spec((1, 1, WIDTH, 128)),
+        whole_spec((1, 1, WIDTH, 128)),
+        whole_spec((3, 3, 128, 128)),
+        pl.BlockSpec(memory_space=pl.ANY),
+        pl.BlockSpec(memory_space=pl.ANY),
+    ]
+    args = (cells, cells, above, below, weight, done, ready)
+    return conv_call(edge_kernel, 2, specs, lambda i: i * (ROWS - 1), {5: 0}, args)
 
 
 def exchange(block):
@@ -473,22 +553,16 @@
 def shards(local_maps, global_maps, conv_weight, in_weight, mix_weight, out_weight, out_cotangent):
     row_fwd, row_inv = row_tables()
     forward, backward, twiddle = column_tables()
-    spec_rows, inner = rows_forward(global_maps, out_cotangent, in_weight, out_weight, row_fwd)
+    spec_rows, inner = rows_forward(global_maps, out_cotangent, in_weight.T, out_weight, row_fwd)
     spec_cols = exchange(spec_rows)
-    padded = extended(local_maps)
-    local_out = lax.conv_general_dilated(
-        padded,
-        conv_weight,
-        (1, 1),
-        ((0, 0), (1, 1)),
-        dimension_numbers=("NHWC", "HWIO", "NHWC"),
-        preferred_element_type=F32,
-    ).astype(BF16)
-    spectrum, back_cols = columns(spec_cols, forward, backward, twiddle, mix_weight)
+    local_inner = inner_rows(local_maps, conv_weight, spec_rows)
+    spectrum, back_cols = columns(spec_cols, forward, backward, twiddle, mix_weight, local_inner)
     back = exchange(back_cols)
     mix_part = mix_terms(spec_cols, spectrum, forward, twiddle, mix_weight)
-    summed, terms = back_rows(row_inv, back, inner, out_cotangent, mix_part)
-    terms = jnp.broadcast_to(terms.reshape(128, 1, 2, 128), (128, 2, 2, 128)).reshape(256, 2, 128)
+    above, below = neighbour_rows(local_maps)
+    summed, terms = back_rows(row_inv, back, inner, out_cotangent, mix_part, above, below)
+    local_out = edge_rows(local_maps, above, below, conv_weight, local_inner, terms)
+    terms = terms.reshape(256, 2, 128)
     terms = lax.all_to_all(terms, ("rows", "img"), split_axis=0, concat_axis=0, tiled=True)
     global_out = project_out(summed, out_weight)
     total = jnp.sum(terms, axis=0)

time: 178 us -> 161 us (0.904)
  blocking collectives: 68.8 us -> 0 us
  waiting for transfers between devices: 13.8 us -> 71.2 us
  Pallas kernels: 39.9 us -> 51.2 us
  local copies, waits for them, and re-layouts: 14.1 us -> 4.38 us
  matrix products: 5.33 us -> 0 us
    all_to_all x1 -> x0, blocking collectives: 68.8 us -> none  [exchange(): lax.all_to_all(block.reshape(GROUPS, ROWS, lanes), 'rows', split_axis=0,...]
    all_to_all x1 -> x2, waiting for transfers between devices: 1.45 us -> 63.1 us  [exchange(): lax.all_to_all(block.reshape(GROUPS, ROWS, lanes), 'rows', split_axis=0,...]
    all_to_all x1, starting transfers between devices: 22.9 us -> 7.35 us  [shards(): lax.all_to_all(terms, ('rows', 'img'), split_axis=0, concat_axis=0, tiled...]
    all_to_all x1 -> x2, starting transfers between devices: 6.43 us -> 20.2 us  [exchange(): lax.all_to_all(block.reshape(GROUPS, ROWS, lanes), 'rows', split_axis=0,...]
    pallas_call x0 -> x2, Pallas kernels: none -> 11.5 us  [conv_call(): pl.pallas_call(kernel, grid=(rows,), in_specs=in_specs, out_specs=row_spe...]
    ppermute x2, waiting for transfers between devices: 8.27 us -> 0.32 us  [the longest x1 0.32 us: neighbour_rows(): below = lax.ppermute(head, 'rows', [(i + 1, i) for i in range(ends)])]
    conv_general_dilated x1 -> x0, matrix products: 5.33 us -> none  [shards(): lax.conv_general_dilated(padded, conv_weight, (1, 1), ((0, 0), (1, 1)), d...]
    conv_general_dilated x3 -> x0, local copies, waits for them, and re-layouts: 4.01 us -> none  [shards(): lax.conv_general_dilated(padded, conv_weight, (1, 1), ((0, 0), (1, 1)), d...]
  transfers between devices with their start and end apart: 4 -> 5, of which waited for: 4 -> 4; matrix products, arithmetic and copies ran while one was open for 8% -> 1% of each run, Pallas kernels for 7% -> 15%
where the time goes in v2:
time: 161 us; the launch traced here: 160 us
  waiting for transfers between devices  71.2 us (44%)
  Pallas kernels  51.2 us (32%)
  starting transfers between devices  32.5 us (20%)
  local copies, waits for them, and re-layouts  4.38 us (3%)
    all_to_all x2, waiting for transfers between devices, exchange(): lax.all_to_all(block.reshape(GROUPS, ROWS, lanes), 'rows', split_axis=0,...  63.1 us
    all_to_all x2, starting transfers between devices, exchange(): lax.all_to_all(block.reshape(GROUPS, ROWS, lanes), 'rows', split_axis=0,...  20.2 us
    pallas_call x1, Pallas kernels, columns(): pl.pallas_call(columns_kernel, grid=(1,), in_specs=[pl.BlockSpec((1024, 5...  12.3 us
    pallas_call x2, Pallas kernels, conv_call(): pl.pallas_call(kernel, grid=(rows,), in_specs=in_specs, out_specs=row_spe...  11.5 us
    pallas_call x1, Pallas kernels, rows_forward(): pl.pallas_call(rows_kernel, grid=(8,), in_specs=[pl.BlockSpec((1, 2, WIDT...  9.39 us
    all_to_all x1, waiting for transfers between devices, shards(): lax.all_to_all(terms, ('rows', 'img'), split_axis=0, concat_axis=0, tiled...  7.84 us
    pallas_call x1, Pallas kernels, mix_terms(): pl.pallas_call(mix_kernel, grid=(1,), in_specs=[pl.BlockSpec((1024, 512),...  7.77 us
    all_to_all x1, starting transfers between devices, shards(): lax.all_to_all(terms, ('rows', 'img'), split_axis=0, concat_axis=0, tiled...  7.35 us
  transfers between devices with their start and end apart: 5, of which 4 were waited for; matrix products, arithmetic and copies ran while one was open for 1% of the time, Pallas kernels for 15%

profile of v2, /device:TPU:1, one launch (start us, length us, event | category | flops | bytes accessed | tf_op | source)
XLA Modules:
  0.0 160.3 jit_solution(12962108323384287855)
XLA Ops:
  0.6 9.4 %shard_map.147 = (bf16[1024,1024]{1,0:T(8,128)(2,1)}, bf16[1024,512]{1,0:T(8,128)(2,1)}) custom-call(bf16[1,8,1024,128]{3,2,1,0:T(8,128)(2,1)} %maps.1, bf16[1,8,1024,128]{3,2,1,0:T(8,128)(2,1)} %cot.3, bf16[64,128]{1,0:T(8,128)(2,1)} %bitcast.16, bf16[64,128]{1,0:T(8,128)(2,1)} %out_w.3, bf16[1024,1024]{1,0:T(8,128)(2,1)} %constant.12.clone.table), custom_call_target="tpu_custom_call" | custom-call | flops 5000000000 | bytes 11534336 | tf_op jit(solution)/shard_map/pallas_call | solution.py:123
  10.0 14.9 %all-to-all-start = ((bf16[128,8,1024]{2,1,0:T(8,128)(2,1)}), bf16[128,8,1024]{2,1,0:T(8,128)(2,1)S(1)}, u32[]{:S(2)}, u32[]{:S(2)}) async-start(bf16[128,8,1024]{2,1,0:T(8,128)(2,1)} %bitcast.12), calls=%async_computation | async-start | bytes 4194304 | tf_op jit(solution)/shard_map/all_to_all | solution.py:547
  24.9 7.8 %shard_map.148.ready.done = bf16[1,8,1024,128]{3,2,1,0:T(8,128)(2,1)} custom-call(bf16[1,8,1024,128]{3,2,1,0:T(8,128)(2,1)} %beside.1, bf16[1,8,1024,128]{3,2,1,0:T(8,128)(2,1)} %beside.1, bf16[1,8,1024,128]{3,2,1,0:T(8,128)(2,1)} %beside.1, bf16[3,3,128,128]{3,2,1,0:T(8,128)(2,1)} %weight.3, bf16[1024,1024]{1,0:T(8,128)(2,1)} %get-tuple-element.10.ready), custom_call_target="tpu_custom_call" | custom-call | flops 6000000000 | bytes 6291456 | tf_op jit(solution)/shard_map/pallas_call | solution.py:498
  32.7 46.1 %all-to-all-done = bf16[128,8,1024]{2,1,0:T(8,128)(2,1)S(1)} async-done(((bf16[128,8,1024]{2,1,0:T(8,128)(2,1)}), bf16[128,8,1024]{2,1,0:T(8,128)(2,1)S(1)}, u32[]{:S(2)}, u32[]{:S(2)}) %all-to-all-start) | async-done | bytes 2097184 | tf_op jit(solution)/shard_map/all_to_all | solution.py:547
  78.7 0.0 copy-start
  78.7 1.3 copy-done
  80.1 12.3 %shard_map.149 = (bf16[16,128,256]{2,1,0:T(8,128)(2,1)}, bf16[1024,512]{1,0:T(8,128)(2,1)}) custom-call(bf16[1024,1024]{1,0:T(8,128)(2,1)} %bitcast.10, bf16[256,256]{1,0:T(8,128)(2,1)} %constant.13.clone.forward, bf16[256,256]{1,0:T(8,128)(2,1)} %constant.14.clone.backward, f32[2,128,512]{2,1,0:T(8,128)} %constant.15.clone.twiddle, bf16[128,128]{1,0:T(8,128)(2,1)} %mix_w.3, ...), custom_call_target="tpu_custom_call" | custom-call | flops 8000000000 | bytes 5242880 | tf_op jit(solution)/shard_map/pallas_call | solution.py:304
  92.3 5.3 %all-to-all-start.1 = ((bf16[128,8,512]{2,1,0:T(8,128)(2,1)}), bf16[128,8,512]{2,1,0:T(8,128)(2,1)S(1)}, u32[]{:S(2)}, u32[]{:S(2)}) async-start(bf16[128,8,512]{2,1,0:T(8,128)(2,1)} %bitcast.15), calls=%async_computation.1 | async-start | bytes 2097152 | tf_op jit(solution)/shard_map/all_to_all | solution.py:547
  97.7 1.1 fusion
  98.7 3.1 %collective-permute-start = (bf16[1,1,1024,128]{3,2,1,0:T(8,128)(2,1)S(1)}, bf16[1,1,1024,128]{3,2,1,0:T(8,128)(2,1)S(1)}, u32[]{:S(2)}, u32[]{:S(2)}) collective-permute-start(bf16[1,1,1024,128]{3,2,1,0:T(8,128)(2,1)S(1)} %get-tuple-element.17), channel_id=1, source_target_pairs={{0,2},{2,4},{4,6},{6,8},{8,10},{10,12},{12,14},{14,16},{16,18},{18... | collective-permute-start | bytes 786440 | tf_op jit(solution)/shard_map/ppermute | solution.py:526
  101.8 1.9 %collective-permute-start.1 = (bf16[1,1,1024,128]{3,2,1,0:T(8,128)(2,1)S(1)}, bf16[1,1,1024,128]{3,2,1,0:T(8,128)(2,1)S(1)}, u32[]{:S(2)}, u32[]{:S(2)}) collective-permute-start(bf16[1,1,1024,128]{3,2,1,0:T(8,128)(2,1)S(1)} %get-tuple-element.16), channel_id=1, source_target_pairs={{2,0},{4,2},{6,4},{8,6},{10,8},{12,10},{14,12},{16,14},{18,16},{20... | collective-permute-start | bytes 786440 | tf_op jit(solution)/shard_map/ppermute | solution.py:527
  103.8 7.8 %shard_map.150.mix_part = f32[128,128]{1,0:T(8,128)} custom-call(bf16[1024,1024]{1,0:T(8,128)(2,1)} %bitcast.11, bf16[16,128,256]{2,1,0:T(8,128)(2,1)} %get-tuple-element.13.spec, bf16[256,256]{1,0:T(8,128)(2,1)} %constant.13.clone.forward, f32[2,128,512]{2,1,0:T(8,128)} %constant.15.clone.twiddle, bf16[128,128]{1,0:T(8,128)(2,1)} %mix_w.3), custom_call_target="tpu_custom_call" | custom-call | flops 6000000000 | bytes 5242880 | tf_op jit(solution)/shard_map/pallas_call | solution.py:365
  111.5 0.0 collective-permute-done.above.edge_above
  111.5 0.0 copy-start.2
  111.5 0.3 collective-permute-done.1.below.edge_below
  111.9 0.0 copy-start.3
  111.9 17.0 %all-to-all-done.1 = bf16[128,8,512]{2,1,0:T(8,128)(2,1)S(1)} async-done(((bf16[128,8,512]{2,1,0:T(8,128)(2,1)}), bf16[128,8,512]{2,1,0:T(8,128)(2,1)S(1)}, u32[]{:S(2)}, u32[]{:S(2)}) %all-to-all-start.1) | async-done | bytes 1048608 | tf_op jit(solution)/shard_map/all_to_all | solution.py:547
  128.8 0.0 copy-start.1
  128.8 0.0 copy-done.2
  128.9 0.0 copy-done.3
  128.9 1.0 copy-done.1
  129.8 6.2 %shard_map.151 = (bf16[1024,512]{1,0:T(8,128)(2,1)}, f32[512,128]{1,0:T(8,128)}) custom-call(bf16[1024,1024]{1,0:T(8,128)(2,1)} %constant.16.clone.table, bf16[1024,512]{1,0:T(8,128)(2,1)} %bitcast.14, bf16[1024,512]{1,0:T(8,128)(2,1)} %get-tuple-element.12.inner, bf16[1,8,1024,128]{3,2,1,0:T(8,128)(2,1)} %cot.3, f32[128,128]{1,0:T(8,128)} %shard_map.150.mix_part, ...), custom_call_target="tpu_custom_call" | custom-call | flops 2000000000 | bytes 8388608 | tf_op jit(solution)/shard_map/pallas_call | solution.py:415
  136.0 7.4 %all-to-all-start.2 = ((f32[256,2,128]{2,1,0:T(2,128)}), f32[256,2,128]{2,1,0:T(2,128)S(1)}, u32[]{:S(2)}, u32[]{:S(2)}) async-start(f32[256,2,128]{2,1,0:T(2,128)} %bitcast.13), calls=%async_computation.2 | async-start | bytes 524288 | tf_op jit(solution)/shard_map/all_to_all | solution.py:566
  143.4 4.1 %shard_map.153 = bf16[1,8,1024,128]{3,2,1,0:T(8,128)(2,1)} custom-call(bf16[1024,512]{1,0:T(8,128)(2,1)} %get-tuple-element.15.summed, bf16[64,128]{1,0:T(8,128)(2,1)} %out_w.3), custom_call_target="tpu_custom_call" | custom-call | flops 500000000 | bytes 3145728 | tf_op jit(solution)/shard_map/pallas_call | solution.py:452
  147.5 3.7 %shard_map.152 = bf16[1,8,1024,128]{3,2,1,0:T(8,128)(2,1)} custom-call(bf16[1,8,1024,128]{3,2,1,0:T(8,128)(2,1)} %beside.1, bf16[1,8,1024,128]{3,2,1,0:T(8,128)(2,1)} %beside.1, bf16[1,1,1024,128]{3,2,1,0:T(8,128)(2,1)} %copy-done.2, bf16[1,1,1024,128]{3,2,1,0:T(8,128)(2,1)} %copy-done.3, ...), custom_call_target="tpu_custom_call", output_to_operand_aliasing={{}: (5, {})} | custom-call | flops 2000000000 | bytes 2097152 | tf_op jit(solution)/shard_map/pallas_call | solution.py:498
  151.2 7.8 %all-to-all-done.2 = f32[256,2,128]{2,1,0:T(2,128)S(1)} async-done(((f32[256,2,128]{2,1,0:T(2,128)}), f32[256,2,128]{2,1,0:T(2,128)S(1)}, u32[]{:S(2)}, u32[]{:S(2)}) %all-to-all-start.2) | async-done | bytes 262176 | tf_op jit(solution)/shard_map/all_to_all | solution.py:566
  159.0 0.3 reduce_sum.9
  159.3 0.5 slice_bitcast_fusion
  159.8 0.5 slice_bitcast_fusion.1
Async XLA Ops:
  10.0 68.7 %all-to-all-start = ((bf16[128,8,1024]{2,1,0:T(8,128)(2,1)}), bf16[128,8,1024]{2,1,0:T(8,128)(2,1)S(1)}, u32[]{:S(2)}, u32[]{:S(2)}) async-start(bf16[128,8,1024]{2,1,0:T(8,128)(2,1)} %bitcast.12), calls=%async_computation | async-start | bytes 4194304 | tf_op jit(solution)/shard_map/all_to_all | solution.py:547
  78.7 1.3 copy-start
  92.3 36.5 %all-to-all-start.1 = ((bf16[128,8,512]{2,1,0:T(8,128)(2,1)}), bf16[128,8,512]{2,1,0:T(8,128)(2,1)S(1)}, u32[]{:S(2)}, u32[]{:S(2)}) async-start(bf16[128,8,512]{2,1,0:T(8,128)(2,1)} %bitcast.15), calls=%async_computation.1 | async-start | bytes 2097152 | tf_op jit(solution)/shard_map/all_to_all | solution.py:547
  98.7 12.8 %collective-permute-start = (bf16[1,1,1024,128]{3,2,1,0:T(8,128)(2,1)S(1)}, bf16[1,1,1024,128]{3,2,1,0:T(8,128)(2,1)S(1)}, u32[]{:S(2)}, u32[]{:S(2)}) collective-permute-start(bf16[1,1,1024,128]{3,2,1,0:T(8,128)(2,1)S(1)} %get-tuple-element.17), channel_id=1, source_target_pairs={{0,2},{2,4},{4,6},{6,8},{8,10},{10,12},{12,14},{14,16},{16,18},{18... | collective-permute-start | bytes 786440 | tf_op jit(solution)/shard_map/ppermute | solution.py:526
  101.8 10.0 %collective-permute-start.1 = (bf16[1,1,1024,128]{3,2,1,0:T(8,128)(2,1)S(1)}, bf16[1,1,1024,128]{3,2,1,0:T(8,128)(2,1)S(1)}, u32[]{:S(2)}, u32[]{:S(2)}) collective-permute-start(bf16[1,1,1024,128]{3,2,1,0:T(8,128)(2,1)S(1)} %get-tuple-element.16), channel_id=1, source_target_pairs={{2,0},{4,2},{6,4},{8,6},{10,8},{12,10},{14,12},{16,14},{18,16},{20... | collective-permute-start | bytes 786440 | tf_op jit(solution)/shard_map/ppermute | solution.py:527
  111.5 17.3 %copy-start.2 = (bf16[1,1,1024,128]{3,2,1,0:T(8,128)(2,1)}, bf16[1,1,1024,128]{3,2,1,0:T(8,128)(2,1)S(1)}, u32[]{:S(2)}) copy-start(bf16[1,1,1024,128]{3,2,1,0:T(8,128)(2,1)S(1)} %collective-permute-done.above.edge_above) | copy-start | bytes 786436
  111.9 17.0 %copy-start.3 = (bf16[1,1,1024,128]{3,2,1,0:T(8,128)(2,1)}, bf16[1,1,1024,128]{3,2,1,0:T(8,128)(2,1)S(1)}, u32[]{:S(2)}) copy-start(bf16[1,1,1024,128]{3,2,1,0:T(8,128)(2,1)S(1)} %collective-permute-done.1.below.edge_below) | copy-start | bytes 786436
  128.8 1.0 copy-start.1
  136.0 23.0 %all-to-all-start.2 = ((f32[256,2,128]{2,1,0:T(2,128)}), f32[256,2,128]{2,1,0:T(2,128)S(1)}, u32[]{:S(2)}, u32[]{:S(2)}) async-start(f32[256,2,128]{2,1,0:T(2,128)} %bitcast.13), calls=%async_computation.2 | async-start | bytes 524288 | tf_op jit(solution)/shard_map/all_to_all | solution.py:566

commit v3 on v2

--- a/solution.py
+++ b/solution.py
@@ -19,11 +19,23 @@
 PAIR = 128
 BF16 = jnp.bfloat16
 F32 = jnp.float32
-LIMIT = 56 * 1024 * 1024
-
-
-def params():
-    return pltpu.CompilerParams(vmem_limit_bytes=LIMIT)
+
+LIMIT = 60 * 2**20
+SMALL = 40 * 2**20
+
+
+def params(limit=LIMIT):
+    return pltpu.CompilerParams(vmem_limit_bytes=limit)
+
+
+def in_hbm(x):
+    return pltpu.with_memory_space_constraint(x, pltpu.HBM)
+
+
+VMEM = pl.BlockSpec(memory_space=pltpu.VMEM)
+
+
+ANY = pl.BlockSpec(memory_space=pl.ANY)
 
 
 def cost(flops, nbytes):
@@ -78,67 +90,72 @@
     return jnp.where(hit, 1.0, 0.0).astype(BF16)
 
 
-def rows_kernel(maps, cot, in_w, out_w, table, spec_out, inner_out, both, in_pair, out_pair):
-    step = pl.program_id(0)
+def rows_kernel(
+    maps, cot, in_w, out_w, table, spec_out, inner_out,
+    pairs, held, both, result, in_pair, out_pair, sems, table_sems, out_sems,
+):
     half = ROWS * SPEC_CH
-
-    @pl.when(step == 0)
-    def _():
-        a, b = first_half(), second_half()
-        in_pair[0:PAIR, :] = dot_t(in_w[...], a).astype(BF16)
-        in_pair[PAIR:, :] = dot_t(in_w[...], b).astype(BF16)
-        out_pair[0:PAIR, :] = dot_t(out_w[...], a).astype(BF16)
-        out_pair[PAIR:, :] = dot_t(out_w[...], b).astype(BF16)
-
-    @pl.when(step < 4)
-    def _():
-        start = pl.multiple_of(step * PAIR, PAIR)
-        pair = jnp.concatenate([maps[0, 0], maps[0, 1]], axis=1)
-        inner = jnp.maximum(dot(pair, in_pair[...]), 0.0).astype(BF16)
-        both[:, pl.ds(start, PAIR)] = inner
-        inner_out[:, pl.ds(start, PAIR)] = inner
-        pair = jnp.concatenate([cot[0, 0], cot[0, 1]], axis=1)
-        start = pl.multiple_of(half + step * PAIR, PAIR)
-        both[:, pl.ds(start, PAIR)] = dot(pair, out_pair[...]).astype(BF16)
-
-    @pl.when(step >= 4)
-    def _():
-        prod = dot(table[...], both[...])
-        row = (step - 4) * 256 + iota((256, half), 0)
+    loads = []
+    for p in range(4):
+        for n, source in enumerate((maps, cot)):
+            rows = source.at[0, pl.ds(2 * p, 2)]
+            loads.append(pltpu.make_async_copy(rows, pairs.at[p, n], sems.at[p, n]))
+    tables = []
+    for b in range(4):
+        rows = pl.ds(b * 256, 256)
+        tables.append(pltpu.make_async_copy(table.at[rows], held.at[rows], table_sems.at[b]))
+    for copy in loads + tables:
+        copy.start()
+    a, b = first_half(), second_half()
+    in_pair[0:PAIR, :] = dot_t(in_w[...], a).astype(BF16)
+    in_pair[PAIR:, :] = dot_t(in_w[...], b).astype(BF16)
+    out_pair[0:PAIR, :] = dot_t(out_w[...], a).astype(BF16)
+    out_pair[PAIR:, :] = dot_t(out_w[...], b).astype(BF16)
+    for p in range(4):
+        lanes = slice(p * PAIR, (p + 1) * PAIR)
+        loads[2 * p].wait()
+        pair = jnp.concatenate([pairs[p, 0, 0], pairs[p, 0, 1]], axis=1)
+        both[:, lanes] = jnp.maximum(dot(pair, in_pair[...]), 0.0).astype(BF16)
+        lanes = slice(half + p * PAIR, half + (p + 1) * PAIR)
+        loads[2 * p + 1].wait()
+        pair = jnp.concatenate([pairs[p, 1, 0], pairs[p, 1, 1]], axis=1)
+        both[:, lanes] = dot(pair, out_pair[...]).astype(BF16)
+    stores = [pltpu.make_async_copy(both.at[:, pl.ds(0, half)], inner_out, out_sems.at[4])]
+    stores[0].start()
+    for b in range(4):
+        rows = pl.ds(b * 256, 256)
+        tables[b].wait()
+        prod = dot(held[rows, :], both[...])
+        result[rows, 0:half] = prod[:, 0:half].astype(BF16)
+        row = b * 256 + iota((256, half), 0)
         factor = jnp.where((row == 0) | (row == PER_GROUP), 1.0, 2.0)
-        spec_out[:, 0:half] = prod[:, 0:half].astype(BF16)
-        spec_out[:, half:] = (prod[:, half:] * factor).astype(BF16)
+        result[rows, half:] = (prod[:, half:] * factor).astype(BF16)
+        stores.append(pltpu.make_async_copy(result.at[rows], spec_out.at[rows], out_sems.at[b]))
+        stores[-1].start()
+    for copy in stores:
+        copy.wait()
 
 
 def rows_forward(maps, cot, in_w, out_w, table):
-    def block(i):
-        return (0, jnp.minimum(i, 3), 0, 0)
-
-    def late(i):
-        return (jnp.maximum(i - 4, 0), 0)
-
-    def whole(i):
-        return (0, 0)
-
     return pl.pallas_call(
         rows_kernel,
-        grid=(8,),
-        in_specs=[
-            pl.BlockSpec((1, 2, WIDTH, 128), block),
-            pl.BlockSpec((1, 2, WIDTH, 128), block),
-            pl.BlockSpec((SPEC_CH, 128), whole),
-            pl.BlockSpec((SPEC_CH, 128), whole),
-            pl.BlockSpec((256, WIDTH), late),
-        ],
-        out_specs=[pl.BlockSpec((256, 1024), late), pl.BlockSpec((WIDTH, 512), whole)],
+        grid=(1,),
+        in_specs=[ANY, ANY, whole_spec((SPEC_CH, 128)), whole_spec((SPEC_CH, 128)), ANY],
+        out_specs=[ANY, ANY],
         out_shape=[
-            jax.ShapeDtypeStruct((1024, 1024), BF16),
-            jax.ShapeDtypeStruct((WIDTH, 512), BF16),
+            pltpu.HBM((1024, 1024), BF16),
+            pltpu.HBM((WIDTH, 512), BF16),
         ],
         scratch_shapes=[
+            pltpu.VMEM((4, 2, 2, WIDTH, 128), BF16),
+            pltpu.VMEM((1024, WIDTH), BF16),
             pltpu.VMEM((WIDTH, 1024), BF16),
+            pltpu.VMEM((1024, 1024), BF16),
             pltpu.VMEM((256, PAIR), BF16),
             pltpu.VMEM((256, PAIR), BF16),
+            pltpu.SemaphoreType.DMA((4, 2)),
+            pltpu.SemaphoreType.DMA((4,)),
+            pltpu.SemaphoreType.DMA((5,)),
         ],
         compiler_params=params(),
         cost_estimate=cost(5 * 10**9, 11 * 2**20),
@@ -237,7 +254,7 @@
 
 
 def sigmoid(x):
-    return 1.0 / (1.0 + jnp.exp(-x))
+    return 0.5 * jnp.tanh(0.5 * x) + 0.5
 
 
 def gather_parts(stage, kk):
@@ -254,16 +271,31 @@
         stage[m] = block[:, m * PAIR : (m + 1) * PAIR].astype(F32)
 
 
-def columns_kernel(block, forward, backward, twiddle, mix_w, ready, spec, back, stage, wide, prod, pre, inv):
-    del ready
+def columns_kernel(
+    block, forward_in, backward_in, twiddle_in, mix_in, ready, above, below, spec_out, back_out,
+    land, forward, backward, twiddle, mix_w, spec, stage, wide, prod, pre, inv, sems, out_sems,
+):
+    del ready, above, below
+    mix_load = pltpu.make_async_copy(mix_in, mix_w, sems.at[4])
+    forward_load = pltpu.make_async_copy(forward_in, forward, sems.at[5])
+    twiddle_load = pltpu.make_async_copy(twiddle_in, twiddle, sems.at[6])
+    backward_load = pltpu.make_async_copy(backward_in, backward, sems.at[7])
+    for copy in (mix_load, forward_load, twiddle_load, backward_load):
+        copy.start()
+    for m in range(4):
+        stage[m] = block[:, m * PAIR : (m + 1) * PAIR].astype(F32)
+    mix_load.wait()
     fill_mix(mix_w, wide)
-    fill_stage(block, stage)
+    forward_load.wait()
+    twiddle_load.wait()
+    backward_load.wait()
+    stores = []
     signs = lane_signs((RB, PAIR))
     first = iota((RB, PAIR), 1) < SPEC_CH
     for kk in range(PER_GROUP):
         prod[...] = dot(forward[...], gather_parts(stage, kk))
 
-        @pl.loop(0, GROUPS, step=RB)
+        @pl.loop(0, GROUPS, step=RB, unroll=True)
         def _(rows):
             rows = pl.multiple_of(rows, RB)
             parts = spectrum_rows(prod, twiddle, rows, signs, first)
@@ -271,9 +303,12 @@
                 spec[kk * 4 + q, pl.ds(rows, RB), 0:PAIR] = parts[q][0].astype(BF16)
                 spec[kk * 4 + q, pl.ds(rows, RB), PAIR:] = parts[q][1].astype(BF16)
 
+        part = pl.ds(kk * 4, 4)
+        stores.append(pltpu.make_async_copy(spec.at[part], spec_out.at[part], out_sems.at[kk]))
+        stores[-1].start()
         pre[...] = dot(spec[kk * 4 : kk * 4 + 4].reshape(512, 256), wide[...])
 
-        @pl.loop(0, GROUPS, step=RB)
+        @pl.loop(0, GROUPS, step=RB, unroll=True)
         def _(rows):
             rows = pl.multiple_of(rows, RB)
             parts = []
@@ -293,40 +328,46 @@
             stage[m, pl.ds(kk, GROUPS, stride=ROWS), :] = result[0:GROUPS, lanes]
             stage[m, pl.ds(PER_GROUP + kk, GROUPS, stride=ROWS), :] = result[GROUPS:, lanes]
     for m in range(4):
-        back[:, m * PAIR : (m + 1) * PAIR] = stage[m].astype(BF16)
+        land[:, m * PAIR : (m + 1) * PAIR] = stage[m].astype(BF16)
+        lanes = pl.ds(m * PAIR, PAIR)
+        copy = pltpu.make_async_copy(land.at[:, lanes], back_out.at[:, lanes], out_sems.at[4 + m])
+        copy.start()
+        stores.append(copy)
+    for copy in stores:
+        copy.wait()
 
 
 def whole_spec(shape):
     return pl.BlockSpec(shape, lambda *_: (0,) * len(shape))
 
 
-def columns(block, forward, backward, twiddle, mix_w, ready):
+def columns(block, forward, backward, twiddle, mix_w, ready, above, below):
     return pl.pallas_call(
         columns_kernel,
-        grid=(1,),
-        in_specs=[
-            pl.BlockSpec((1024, 512), lambda i: (0, 0)),
-            whole_spec((256, 256)),
-            whole_spec((256, 256)),
-            whole_spec((2, GROUPS, 512)),
-            whole_spec((128, 128)),
-            pl.BlockSpec(memory_space=pl.ANY),
-        ],
-        out_specs=[whole_spec((16, GROUPS, 256)), whole_spec((1024, 512))],
+        in_specs=[VMEM] + [ANY] * 7,
+        out_specs=[ANY, ANY],
         out_shape=[
-            jax.ShapeDtypeStruct((16, GROUPS, 256), BF16),
-            jax.ShapeDtypeStruct((1024, 512), BF16),
+            pltpu.HBM((16, GROUPS, 256), BF16),
+            pltpu.HBM((1024, 512), BF16),
         ],
         scratch_shapes=[
+            pltpu.VMEM((1024, 512), BF16),
+            pltpu.VMEM((256, 256), BF16),
+            pltpu.VMEM((256, 256), BF16),
+            pltpu.VMEM((2, GROUPS, 512), F32),
+            pltpu.VMEM((128, 128), BF16),
+            pltpu.VMEM((16, GROUPS, 256), BF16),
             pltpu.VMEM((4, 1024, PAIR), F32),
             pltpu.VMEM((256, 256), BF16),
             pltpu.VMEM((256, 512), F32),
             pltpu.VMEM((512, 256), F32),
             pltpu.VMEM((256, 512), BF16),
-        ],
-        compiler_params=params(),
+            pltpu.SemaphoreType.DMA((8,)),
+            pltpu.SemaphoreType.DMA((8,)),
+        ],
+        compiler_params=params(SMALL),
         cost_estimate=cost(8 * 10**9, 5 * 2**20),
-    )(block, forward, backward, twiddle, mix_w, ready)
+    )(block, forward, backward, twiddle, mix_w, in_hbm(ready), above, below)
 
 
 def mix_kernel(block, spec, forward, twiddle, mix_w, grad, stage, wide, prod, pre, slope, acc):
@@ -339,7 +380,7 @@
         prod[...] = dot(forward[...], gather_parts(stage, kk))
         pre[...] = dot(spec[kk * 4 : kk * 4 + 4].reshape(512, 256), wide[...])
 
-        @pl.loop(0, GROUPS, step=RB)
+        @pl.loop(0, GROUPS, step=RB, unroll=True)
         def _(rows):
             rows = pl.multiple_of(rows, RB)
             parts = spectrum_rows(prod, twiddle, rows, signs, first)
@@ -387,52 +428,82 @@
     )(block, spec, forward, twiddle, mix_w)
 
 
-def back_kernel(table, rows, inner, cot, mix_part, above, below, summed, terms, acc):
-    del above, below
-    step = pl.program_id(0)
-
-    @pl.when(step == 0)
-    def _():
-        acc[...] = jnp.zeros_like(acc)
-
-    total = (dot(table[...], rows[...]) + inner[...].astype(F32)).astype(BF16)
-    summed[...] = total
-    for p in range(4):
-        pair = jnp.concatenate([cot[0, 2 * p], cot[0, 2 * p + 1]], axis=1)
-        acc[...] += dot_t(pair, total[:, p * PAIR : (p + 1) * PAIR])
-
-    @pl.when(step == 3)
-    def _():
-        lane = iota((128, PAIR), 1) < SPEC_CH
-        out_part = acc[0:128, :] + pltpu.roll(acc[128:, :], SPEC_CH, 1)
-        out_part = jnp.where(lane, out_part, 0.0)
-        for img in range(2):
-            terms[pl.ds(2 * img, 128, stride=4), :] = mix_part[...]
-            terms[pl.ds(2 * img + 1, 128, stride=4), :] = out_part
-
-
-def back_rows(table, rows, inner, cot, mix_part, above, below):
+def back_kernel(
+    table, block, inner, cot, mix_part, ready, summed_out, terms_out,
+    held, inners, cots, mix, summed, terms, acc, sems, out_sems,
+):
+    def load(source, target, sem):
+        copy = pltpu.make_async_copy(source, target, sems.at[sem])
+        copy.start()
+        return copy
+
+    del ready
+    loads = []
+    for b in range(4):
+        at = pl.ds(b * 256, 256)
+        loads.append(
+            (
+                load(table.at[at], held.at[at], 4 * b + 1),
+                load(inner.at[at], inners.at[at], 4 * b + 2),
+                load(cot.at[0, :, at], cots.at[:, at], 4 * b + 3),
+            )
+        )
+    last = load(mix_part, mix, 4)
+    stores = []
+    for b in range(4):
+        for copy in loads[b]:
+            copy.wait()
+        at = slice(b * 256, (b + 1) * 256)
+        total = (dot(held[at, :], block[...]) + inners[at, :].astype(F32)).astype(BF16)
+        summed[at, :] = total
+        rows_at = pl.ds(b * 256, 256)
+        copy = pltpu.make_async_copy(summed.at[rows_at], summed_out.at[rows_at], out_sems.at[b])
+        copy.start()
+        stores.append(copy)
+        for p in range(4):
+            pair = jnp.concatenate([cots[2 * p, at, :], cots[2 * p + 1, at, :]], axis=1)
+            part = dot_t(pair, total[:, p * PAIR : (p + 1) * PAIR])
+            if b + p:
+                acc[...] += part
+            else:
+                acc[...] = part
+    last.wait()
+    lane = iota((128, PAIR), 1) < SPEC_CH
+    out_part = acc[0:128, :] + pltpu.roll(acc[128:, :], SPEC_CH, 1)
+    out_part = jnp.where(lane, out_part, 0.0)
+    for img in range(2):
+        terms[pl.ds(2 * img, 128, stride=4), :] = mix[...]
+        terms[pl.ds(2 * img + 1, 128, stride=4), :] = out_part
+    copy = pltpu.make_async_copy(terms, terms_out, out_sems.at[4])
+    copy.start()
+    stores.append(copy)
+    for copy in stores:
+        copy.wait()
+
+
+def back_rows(table, rows, inner, cot, mix_part, ready):
     return pl.pallas_call(
         back_kernel,
-        grid=(4,),
-        in_specs=[
-            pl.BlockSpec((256, 1024), lambda i: (i, 0)),
-            whole_spec((1024, 512)),
-            pl.BlockSpec((256, 512), lambda i: (i, 0)),
-            pl.BlockSpec((1, ROWS, 256, 128), lambda i: (0, 0, i, 0)),
-            whole_spec((128, 128)),
-            pl.BlockSpec(memory_space=pl.ANY),
-            pl.BlockSpec(memory_space=pl.ANY),
-        ],
-        out_specs=[pl.BlockSpec((256, 512), lambda i: (i, 0)), whole_spec((512, 128))],
+        in_specs=[ANY, VMEM, ANY, ANY, ANY, ANY],
+        out_specs=[ANY, ANY],
         out_shape=[
-            jax.ShapeDtypeStruct((WIDTH, 512), BF16),
-            jax.ShapeDtypeStruct((512, 128), F32),
-        ],
-        scratch_shapes=[pltpu.VMEM((256, 128), F32)],
-        compiler_params=params(),
+            pltpu.HBM((WIDTH, 512), BF16),
+            pltpu.HBM((512, 128), F32),
+        ],
+        scratch_shapes=[
+            pltpu.VMEM((WIDTH, 1024), BF16),
+            pltpu.VMEM((WIDTH, 512), BF16),
+            pltpu.VMEM((ROWS, WIDTH, 128), BF16),
+            pltpu.VMEM((128, 128), F32),
+            pltpu.VMEM((WIDTH, 512), BF16),
+            pltpu.VMEM((512, 128), F32),
+            pltpu.VMEM((256, 128), F32),
+            pltpu.SemaphoreType.DMA((17,)),
+            pltpu.SemaphoreType.DMA((5,)),
+        ],
+        compiler_params=params(SMALL),
         cost_estimate=cost(2 * 10**9, 8 * 2**20),
-    )(table, rows, inner, cot, mix_part, above, below)
+    )(in_hbm(table), rows, in_hbm(inner), in_hbm(cot), in_hbm(mix_part), in_hbm(ready))
 
 
 def out_kernel(summed, out_w, out, wide):
@@ -461,9 +532,10 @@
     )(summed, out_w)
 
 
-def conv_row(top, mid, bottom, weight, out, sums, wide):
+def conv_row(top, mid, bottom, weight, out, token, sums, wide):
     @pl.when(pl.program_id(0) == 0)
     def _():
+        token[...] = jnp.zeros((8, 128), F32)
         for a in range(3):
             for b in range(3):
                 wide[a * 128 : (a + 1) * 128, b * 128 : (b + 1) * 128] = weight[a, b]
@@ -477,17 +549,17 @@
     out[0, 0] = total.astype(BF16)
 
 
-def inner_kernel(above, mid, below, weight, ready, out, sums, wide):
+def inner_kernel(above, mid, below, weight, ready, out, token, sums, wide):
     del ready
-    conv_row(above[0, 0], mid[0, 0], below[0, 0], weight, out, sums, wide)
-
-
-def edge_kernel(mid, beside, edge_above, edge_below, weight, done, ready, out, sums, wide):
+    conv_row(above[0, 0], mid[0, 0], below[0, 0], weight, out, token, sums, wide)
+
+
+def edge_kernel(mid, beside, edge_above, edge_below, weight, done, ready, out, token, sums, wide):
     del done, ready
     first = pl.program_id(0) == 0
     top = jnp.where(first, edge_above[0, 0], beside[0, 0])
     bottom = jnp.where(first, beside[0, 0], edge_below[0, 0])
-    conv_row(top, mid[0, 0], bottom, weight, out, sums, wide)
+    conv_row(top, mid[0, 0], bottom, weight, out, token, sums, wide)
 
 
 def row_spec(index):
@@ -499,8 +571,11 @@
         kernel,
         grid=(rows,),
         in_specs=in_specs,
-        out_specs=row_spec(out_index),
-        out_shape=jax.ShapeDtypeStruct((1, ROWS, WIDTH, 128), BF16),
+        out_specs=[row_spec(out_index), whole_spec((8, 128))],
+        out_shape=[
+            pltpu.HBM((1, ROWS, WIDTH, 128), BF16),
+            jax.ShapeDtypeStruct((8, 128), F32),
+        ],
         scratch_shapes=[pltpu.VMEM((3, WIDTH + 16, 128), F32), pltpu.VMEM((384, 384), BF16)],
         input_output_aliases=aliases,
         compiler_params=params(),
@@ -555,13 +630,15 @@
     forward, backward, twiddle = column_tables()
     spec_rows, inner = rows_forward(global_maps, out_cotangent, in_weight.T, out_weight, row_fwd)
     spec_cols = exchange(spec_rows)
-    local_inner = inner_rows(local_maps, conv_weight, spec_rows)
-    spectrum, back_cols = columns(spec_cols, forward, backward, twiddle, mix_weight, local_inner)
+    local_inner, token = inner_rows(local_maps, conv_weight, spec_rows)
+    above, below = neighbour_rows(local_maps)
+    spectrum, back_cols = columns(
+        spec_cols, forward, backward, twiddle, mix_weight, token, above, below
+    )
     back = exchange(back_cols)
     mix_part = mix_terms(spec_cols, spectrum, forward, twiddle, mix_weight)
-    above, below = neighbour_rows(local_maps)
-    summed, terms = back_rows(row_inv, back, inner, out_cotangent, mix_part, above, below)
-    local_out = edge_rows(local_maps, above, below, conv_weight, local_inner, terms)
+    local_out, token = edge_rows(local_maps, above, below, conv_weight, local_inner, back_cols)
+    summed, terms = back_rows(row_inv, back, inner, out_cotangent, mix_part, token)
     terms = terms.reshape(256, 2, 128)
     terms = lax.all_to_all(terms, ("rows", "img"), split_axis=0, concat_axis=0, tiled=True)
     global_out = project_out(summed, out_weight)

time: 161 us -> 152 us (0.944)
  Pallas kernels: 51.2 us -> 41.1 us
  local copies, waits for them, and re-layouts: 4.38 us -> 2.13 us
  waiting for transfers between devices: 71.2 us -> 73.2 us
    pallas_call x5, Pallas kernels: 39.4 us -> 31.5 us  [the longest x2 11.5 us: conv_call(): pl.pallas_call(kernel, grid=(rows,), in_specs=in_specs, out_specs=[row_sp...]
    all_to_all x1, waiting for transfers between devices: 7.84 us -> 11.6 us  [shards(): lax.all_to_all(terms, ('rows', 'img'), split_axis=0, concat_axis=0, tiled...]
    pallas_call x1, Pallas kernels: 7.77 us -> 5.51 us  [mix_terms(): pl.pallas_call(mix_kernel, grid=(1,), in_specs=[pl.BlockSpec((1024, 512),...]
    unnamed x8 -> x14, local copies, waits for them, and re-layouts: 2.29 us -> 0.04 us
    all_to_all x2, starting transfers between devices: 20.2 us -> 22.1 us  [exchange(): lax.all_to_all(block.reshape(GROUPS, ROWS, lanes), 'rows', split_axis=0,...]
    all_to_all x1, starting transfers between devices: 7.35 us -> 5.7 us  [shards(): lax.all_to_all(terms, ('rows', 'img'), split_axis=0, concat_axis=0, tiled...]
  transfers between devices with their start and end apart: 5 -> 5, of which waited for: 4 -> 3; matrix products, arithmetic and copies ran while one was open for 1% -> 1% of each run, Pallas kernels for 15% -> 14%
where the time goes in v3:
time: 152 us; the launch traced here: 151 us
  waiting for transfers between devices  73.2 us (48%)
  Pallas kernels  41.1 us (27%)
  starting transfers between devices  33.5 us (22%)
  local copies, waits for them, and re-layouts  2.13 us (1%)
    all_to_all x2, waiting for transfers between devices, exchange(): lax.all_to_all(block.reshape(GROUPS, ROWS, lanes), 'rows', split_axis=0,...  61.6 us
    all_to_all x2, starting transfers between devices, exchange(): lax.all_to_all(block.reshape(GROUPS, ROWS, lanes), 'rows', split_axis=0,...  22.1 us
    all_to_all x1, waiting for transfers between devices, shards(): lax.all_to_all(terms, ('rows', 'img'), split_axis=0, concat_axis=0, tiled...  11.6 us
    pallas_call x2, Pallas kernels, conv_call(): pl.pallas_call(kernel, grid=(rows,), in_specs=in_specs, out_specs=[row_sp...  11.5 us
    pallas_call x1, Pallas kernels, rows_forward(): pl.pallas_call(rows_kernel, grid=(1,), in_specs=[ANY, ANY, whole_spec((SP...  8.95 us
    pallas_call x1, Pallas kernels, columns(): pl.pallas_call(columns_kernel, in_specs=[VMEM] + [ANY] * 7, out_specs=[AN...  5.88 us
    all_to_all x1, starting transfers between devices, shards(): lax.all_to_all(terms, ('rows', 'img'), split_axis=0, concat_axis=0, tiled...  5.7 us
    pallas_call x1, Pallas kernels, mix_terms(): pl.pallas_call(mix_kernel, grid=(1,), in_specs=[pl.BlockSpec((1024, 512),...  5.51 us
  transfers between devices with their start and end apart: 5, of which 3 were waited for; matrix products, arithmetic and copies ran while one was open for 1% of the time, Pallas kernels for 14%

profile of v3, /device:TPU:1, one launch (start us, length us, event | category | flops | bytes accessed | tf_op | source)
XLA Modules:
  0.0 151.0 jit_solution(7501056569658643256)
XLA Ops:
  0.6 8.9 %shard_map.147 = (bf16[1024,1024]{1,0:T(8,128)(2,1)}, bf16[1024,512]{1,0:T(8,128)(2,1)}) custom-call(bf16[1,8,1024,128]{3,2,1,0:T(8,128)(2,1)} %maps.1, bf16[1,8,1024,128]{3,2,1,0:T(8,128)(2,1)} %cot.3, bf16[64,128]{1,0:T(8,128)(2,1)} %bitcast.16, bf16[64,128]{1,0:T(8,128)(2,1)} %out_w.3, bf16[1024,1024]{1,0:T(8,128)(2,1)} %constant.12.clone.table), custom_call_target="tpu_custom_call" | custom-call | flops 5000000000 | bytes 11534336 | tf_op jit(solution)/shard_map/pallas_call | solution.py:140
  9.6 14.9 %all-to-all-start = ((bf16[128,8,1024]{2,1,0:T(8,128)(2,1)}), bf16[128,8,1024]{2,1,0:T(8,128)(2,1)S(1)}, u32[]{:S(2)}, u32[]{:S(2)}) async-start(bf16[128,8,1024]{2,1,0:T(8,128)(2,1)} %bitcast.14), calls=%async_computation | async-start | bytes 4194304 | tf_op jit(solution)/shard_map/all_to_all | solution.py:622
  24.5 1.1 fusion
  25.5 2.8 %collective-permute-start.1 = (bf16[1,1,1024,128]{3,2,1,0:T(8,128)(2,1)S(1)}, bf16[1,1,1024,128]{3,2,1,0:T(8,128)(2,1)S(1)}, u32[]{:S(2)}, u32[]{:S(2)}) collective-permute-start(bf16[1,1,1024,128]{3,2,1,0:T(8,128)(2,1)S(1)} %get-tuple-element.24), channel_id=1, source_target_pairs={{2,0},{4,2},{6,4},{8,6},{10,8},{12,10},{14,12},{16,14},{18,16},{20... | collective-permute-start | bytes 786440 | tf_op jit(solution)/shard_map/ppermute | solution.py:602
  28.4 0.0 copy-start.3
  28.4 0.0 copy-start.4
  28.4 0.0 copy-start.5
  28.4 0.0 copy-start.6
  28.4 2.9 %collective-permute-start = (bf16[1,1,1024,128]{3,2,1,0:T(8,128)(2,1)S(1)}, bf16[1,1,1024,128]{3,2,1,0:T(8,128)(2,1)S(1)}, u32[]{:S(2)}, u32[]{:S(2)}) collective-permute-start(bf16[1,1,1024,128]{3,2,1,0:T(8,128)(2,1)S(1)} %get-tuple-element.25), channel_id=1, source_target_pairs={{0,2},{2,4},{4,6},{6,8},{8,10},{10,12},{12,14},{14,16},{16,18},{18... | collective-permute-start | bytes 786440 | tf_op jit(solution)/shard_map/ppermute | solution.py:601
  31.3 7.8 %shard_map.148 = (bf16[1,8,1024,128]{3,2,1,0:T(8,128)(2,1)}, f32[8,128]{1,0:T(8,128)}) custom-call(bf16[1,8,1024,128]{3,2,1,0:T(8,128)(2,1)} %beside.1, bf16[1,8,1024,128]{3,2,1,0:T(8,128)(2,1)} %beside.1, bf16[1,8,1024,128]{3,2,1,0:T(8,128)(2,1)} %beside.1, bf16[3,3,128,128]{3,2,1,0:T(8,128)(2,1)} %weight.3, bf16[1024,1024]{1,0:T(8,128)(2,1)} %get-tuple-element.14.ready), custom_call_target="tpu_custom_call" | custom-call | flops 6000000000 | bytes 6291456 | tf_op jit(solution)/shard_map/pallas_call | solution.py:570
  39.1 0.0 collective-permute-done.1.below.edge_below
  39.1 0.0 copy-start.1
  39.1 0.0 collective-permute-done.above.edge_above
  39.1 0.0 copy-start.2
  39.1 39.2 %all-to-all-done = bf16[128,8,1024]{2,1,0:T(8,128)(2,1)S(1)} async-done(((bf16[128,8,1024]{2,1,0:T(8,128)(2,1)}), bf16[128,8,1024]{2,1,0:T(8,128)(2,1)S(1)}, u32[]{:S(2)}, u32[]{:S(2)}) %all-to-all-start) | async-done | bytes 2097184 | tf_op jit(solution)/shard_map/all_to_all | solution.py:622
  78.3 0.0 copy-start
  78.3 0.0 copy-done.3
  78.3 0.0 copy-done.4
  78.3 0.0 copy-done.5
  78.3 0.0 copy-done.6
  78.3 5.9 %shard_map.149 = (bf16[16,128,256]{2,1,0:T(8,128)(2,1)}, bf16[1024,512]{1,0:T(8,128)(2,1)}) custom-call(bf16[1024,1024]{1,0:T(8,128)(2,1)S(1)} %bitcast.10, bf16[256,256]{1,0:T(8,128)(2,1)S(1)} %copy-done.5, bf16[256,256]{1,0:T(8,128)(2,1)S(1)} %copy-done.6, f32[2,128,512]{2,1,0:T(8,128)S(1)} %copy-done.4, bf16[128,128]{1,0:T(8,128)(2,1)S(1)} %copy-done.3, ...), custom_call_target="tpu_custom_call" | custom-call | flops 8000000000 | bytes 5242880 | tf_op jit(solution)/shard_map/pallas_call | solution.py:345
  84.2 0.0 copy-done.1
  84.2 0.0 copy-done.2
  84.2 0.0 copy-done
  84.3 7.2 %all-to-all-start.1 = ((bf16[128,8,512]{2,1,0:T(8,128)(2,1)}), bf16[128,8,512]{2,1,0:T(8,128)(2,1)S(1)}, u32[]{:S(2)}, u32[]{:S(2)}) async-start(bf16[128,8,512]{2,1,0:T(8,128)(2,1)} %bitcast.13), calls=%async_computation.1 | async-start | bytes 2097152 | tf_op jit(solution)/shard_map/all_to_all | solution.py:622
  91.5 3.7 %shard_map.150 = (bf16[1,8,1024,128]{3,2,1,0:T(8,128)(2,1)}, f32[8,128]{1,0:T(8,128)}) custom-call(bf16[1,8,1024,128]{3,2,1,0:T(8,128)(2,1)} %beside.1, bf16[1,8,1024,128]{3,2,1,0:T(8,128)(2,1)} %beside.1, bf16[1,1,1024,128]{3,2,1,0:T(8,128)(2,1)} %copy-done.2, bf16[1,1,1024,128]{3,2,1,0:T(8,128)(2,1)} %copy-done.1, ...), custom_call_target="tpu_custom_call", output_to_operand_aliasing={{0}: (5, {})} | custom-call | flops 2000000000 | bytes 2097152 | tf_op jit(solution)/shard_map/pallas_call | solution.py:570
  95.3 5.5 %shard_map.151.mix_part = f32[128,128]{1,0:T(8,128)} custom-call(bf16[1024,1024]{1,0:T(8,128)(2,1)} %bitcast.11, bf16[16,128,256]{2,1,0:T(8,128)(2,1)} %get-tuple-element.20.spec, bf16[256,256]{1,0:T(8,128)(2,1)} %constant.13.clone.forward_in.forward, f32[2,128,512]{2,1,0:T(8,128)} %constant.15.clone.twiddle_in.twiddle, bf16[128,128]{1,0:T(8,128)(2,1)} %mix_w.1), custom_call_target="tpu_custom_call" | custom-call | flops 6000000000 | bytes 5242880 | tf_op jit(solution)/shard_map/pallas_call | solution.py:406
  100.8 22.4 %all-to-all-done.1 = bf16[128,8,512]{2,1,0:T(8,128)(2,1)S(1)} async-done(((bf16[128,8,512]{2,1,0:T(8,128)(2,1)}), bf16[128,8,512]{2,1,0:T(8,128)(2,1)S(1)}, u32[]{:S(2)}, u32[]{:S(2)}) %all-to-all-start.1) | async-done | bytes 1048608 | tf_op jit(solution)/shard_map/all_to_all | solution.py:622
  123.1 5.1 %shard_map.152 = (bf16[1024,512]{1,0:T(8,128)(2,1)}, f32[512,128]{1,0:T(8,128)}) custom-call(bf16[1024,1024]{1,0:T(8,128)(2,1)} %constant.16.clone.table, bf16[1024,512]{1,0:T(8,128)(2,1)S(1)} %bitcast.12, bf16[1024,512]{1,0:T(8,128)(2,1)} %get-tuple-element.19.inner, bf16[1,8,1024,128]{3,2,1,0:T(8,128)(2,1)} %cot.3, f32[128,128]{1,0:T(8,128)} %shard_map.151.mix_part, ...), custom_call_target="tpu_custom_call" | custom-call | flops 2000000000 | bytes 8388608 | tf_op jit(solution)/shard_map/pallas_call | solution.py:485
  128.3 5.7 %all-to-all-start.2 = ((f32[256,2,128]{2,1,0:T(2,128)}), f32[256,2,128]{2,1,0:T(2,128)S(1)}, u32[]{:S(2)}, u32[]{:S(2)}) async-start(f32[256,2,128]{2,1,0:T(2,128)} %bitcast.15), calls=%async_computation.2 | async-start | bytes 524288 | tf_op jit(solution)/shard_map/all_to_all | solution.py:643
  134.0 4.1 %shard_map.153 = bf16[1,8,1024,128]{3,2,1,0:T(8,128)(2,1)} custom-call(bf16[1024,512]{1,0:T(8,128)(2,1)} %get-tuple-element.22.summed, bf16[64,128]{1,0:T(8,128)(2,1)} %out_w.3), custom_call_target="tpu_custom_call" | custom-call | flops 500000000 | bytes 3145728 | tf_op jit(solution)/shard_map/pallas_call | solution.py:523
  138.1 11.6 %all-to-all-done.2 = f32[256,2,128]{2,1,0:T(2,128)S(1)} async-done(((f32[256,2,128]{2,1,0:T(2,128)}), f32[256,2,128]{2,1,0:T(2,128)S(1)}, u32[]{:S(2)}, u32[]{:S(2)}) %all-to-all-start.2) | async-done | bytes 262176 | tf_op jit(solution)/shard_map/all_to_all | solution.py:643
  149.7 0.3 reduce_sum.9
  150.0 0.5 slice_bitcast_fusion
  150.5 0.5 slice_bitcast_fusion.1
Async XLA Ops:
  9.6 68.7 %all-to-all-start = ((bf16[128,8,1024]{2,1,0:T(8,128)(2,1)}), bf16[128,8,1024]{2,1,0:T(8,128)(2,1)S(1)}, u32[]{:S(2)}, u32[]{:S(2)}) async-start(bf16[128,8,1024]{2,1,0:T(8,128)(2,1)} %bitcast.14), calls=%async_computation | async-start | bytes 4194304 | tf_op jit(solution)/shard_map/all_to_all | solution.py:622
  25.5 13.5 %collective-permute-start.1 = (bf16[1,1,1024,128]{3,2,1,0:T(8,128)(2,1)S(1)}, bf16[1,1,1024,128]{3,2,1,0:T(8,128)(2,1)S(1)}, u32[]{:S(2)}, u32[]{:S(2)}) collective-permute-start(bf16[1,1,1024,128]{3,2,1,0:T(8,128)(2,1)S(1)} %get-tuple-element.24), channel_id=1, source_target_pairs={{2,0},{4,2},{6,4},{8,6},{10,8},{12,10},{14,12},{16,14},{18,16},{20... | collective-permute-start | bytes 786440 | tf_op jit(solution)/shard_map/ppermute | solution.py:602
  28.4 50.0 %copy-start.3 = (bf16[128,128]{1,0:T(8,128)(2,1)S(1)}, bf16[128,128]{1,0:T(8,128)(2,1)}, u32[]{:S(2)}) copy-start(bf16[128,128]{1,0:T(8,128)(2,1)} %mix_w.1) | copy-start | bytes 98308
  28.4 50.0 %copy-start.4 = (f32[2,128,512]{2,1,0:T(8,128)S(1)}, f32[2,128,512]{2,1,0:T(8,128)}, u32[]{:S(2)}) copy-start(f32[2,128,512]{2,1,0:T(8,128)} %constant.15.clone.twiddle_in.twiddle) | copy-start | bytes 1572868
  28.4 49.9 %copy-start.5 = (bf16[256,256]{1,0:T(8,128)(2,1)S(1)}, bf16[256,256]{1,0:T(8,128)(2,1)}, u32[]{:S(2)}) copy-start(bf16[256,256]{1,0:T(8,128)(2,1)} %constant.13.clone.forward_in.forward) | copy-start | bytes 393220
  28.4 49.9 %copy-start.6 = (bf16[256,256]{1,0:T(8,128)(2,1)S(1)}, bf16[256,256]{1,0:T(8,128)(2,1)}, u32[]{:S(2)}) copy-start(bf16[256,256]{1,0:T(8,128)(2,1)} %constant.14.clone.backward_in) | copy-start | bytes 393220
  28.4 10.7 %collective-permute-start = (bf16[1,1,1024,128]{3,2,1,0:T(8,128)(2,1)S(1)}, bf16[1,1,1024,128]{3,2,1,0:T(8,128)(2,1)S(1)}, u32[]{:S(2)}, u32[]{:S(2)}) collective-permute-start(bf16[1,1,1024,128]{3,2,1,0:T(8,128)(2,1)S(1)} %get-tuple-element.25), channel_id=1, source_target_pairs={{0,2},{2,4},{4,6},{6,8},{8,10},{10,12},{12,14},{14,16},{16,18},{18... | collective-permute-start | bytes 786440 | tf_op jit(solution)/shard_map/ppermute | solution.py:601
  39.1 45.1 %copy-start.1 = (bf16[1,1,1024,128]{3,2,1,0:T(8,128)(2,1)}, bf16[1,1,1024,128]{3,2,1,0:T(8,128)(2,1)S(1)}, u32[]{:S(2)}) copy-start(bf16[1,1,1024,128]{3,2,1,0:T(8,128)(2,1)S(1)} %collective-permute-done.1.below.edge_below) | copy-start | bytes 786436
  39.1 45.1 %copy-start.2 = (bf16[1,1,1024,128]{3,2,1,0:T(8,128)(2,1)}, bf16[1,1,1024,128]{3,2,1,0:T(8,128)(2,1)S(1)}, u32[]{:S(2)}) copy-start(bf16[1,1,1024,128]{3,2,1,0:T(8,128)(2,1)S(1)} %collective-permute-done.above.edge_above) | copy-start | bytes 786436
  78.3 5.9 %copy-start = (bf16[128,8,1024]{2,1,0:T(8,128)(2,1)}, bf16[128,8,1024]{2,1,0:T(8,128)(2,1)S(1)}, u32[]{:S(2)}) copy-start(bf16[128,8,1024]{2,1,0:T(8,128)(2,1)S(1)} %all-to-all-done) | copy-start | bytes 6291460
  84.3 38.9 %all-to-all-start.1 = ((bf16[128,8,512]{2,1,0:T(8,128)(2,1)}), bf16[128,8,512]{2,1,0:T(8,128)(2,1)S(1)}, u32[]{:S(2)}, u32[]{:S(2)}) async-start(bf16[128,8,512]{2,1,0:T(8,128)(2,1)} %bitcast.13), calls=%async_computation.1 | async-start | bytes 2097152 | tf_op jit(solution)/shard_map/all_to_all | solution.py:622
  128.3 21.4 %all-to-all-start.2 = ((f32[256,2,128]{2,1,0:T(2,128)}), f32[256,2,128]{2,1,0:T(2,128)S(1)}, u32[]{:S(2)}, u32[]{:S(2)}) async-start(f32[256,2,128]{2,1,0:T(2,128)} %bitcast.15), calls=%async_computation.2 | async-start | bytes 524288 | tf_op jit(solution)/shard_map/all_to_all | solution.py:643

commit v4 on v3

--- a/solution.py
+++ b/solution.py
@@ -42,16 +42,36 @@
     return pl.CostEstimate(flops=flops, bytes_accessed=nbytes, transcendentals=0)
 
 
+FIRSTS = ((0, 4), (1, 7), (2, 6), (3, 5))
+
+
 def row_tables():
-    cols = np.arange(WIDTH)
-    freq = np.arange(FREQS)
-    phase = ((cols[:, None] * freq[None, :]) % WIDTH) * (2.0 * math.pi / WIDTH)
-    forward = np.stack([np.cos(phase), -np.sin(phase)], axis=1) / math.sqrt(WIDTH)
-    forward = forward.reshape(WIDTH, 2, GROUPS, PER_GROUP).transpose(0, 2, 1, 3)
-    factor = np.where(freq == 0, 1.0, 2.0).reshape(1, GROUPS, 1, PER_GROUP)
-    inverse = (forward * factor).reshape(WIDTH, 2 * FREQS)
-    forward = np.ascontiguousarray(forward.reshape(WIDTH, 2 * FREQS).T)
-    return forward.astype(ml_dtypes.bfloat16), inverse.astype(ml_dtypes.bfloat16)
+    s = np.arange(128)
+    forward = np.zeros((4, 2, 16, 2, PER_GROUP, 2, 128))
+    inverse = np.zeros((4, 2, 128, 2, 16, 2, PER_GROUP))
+    for b, firsts in enumerate(FIRSTS):
+        for half, k0 in enumerate(firsts):
+            k = k0 + 8 * np.arange(64).reshape(16, PER_GROUP, 1)
+            phase = (k * s % WIDTH) * (2.0 * math.pi / WIDTH)
+            cosine, sine = np.cos(phase) / 32.0, np.sin(phase) / 32.0
+            factor = np.where(k == 0, 1.0, 2.0)
+            sign = 1.0 if half else -1.0
+            if b == 0:
+                forward[b, half, :, 0, :, half] = cosine
+                forward[b, half, :, 1, :, half] = -sine
+                inverse[b, half, :, half, :, 0] = (cosine * factor).transpose(2, 0, 1)
+                inverse[b, half, :, half, :, 1] = (-sine * factor).transpose(2, 0, 1)
+                continue
+            forward[b, half, :, 0, :, 0] = cosine
+            forward[b, half, :, 0, :, 1] = sign * sine
+            forward[b, half, :, 1, :, 0] = -sine
+            forward[b, half, :, 1, :, 1] = sign * cosine
+            inverse[b, 0, :, half, :, 0] = (cosine * factor).transpose(2, 0, 1)
+            inverse[b, 0, :, half, :, 1] = (-sine * factor).transpose(2, 0, 1)
+            inverse[b, 1, :, half, :, 0] = (-sign * sine * factor).transpose(2, 0, 1)
+            inverse[b, 1, :, half, :, 1] = (-sign * cosine * factor).transpose(2, 0, 1)
+    forward = forward.reshape(4, 256, 256).astype(ml_dtypes.bfloat16)
+    return forward, inverse.reshape(4, 256, 256).astype(ml_dtypes.bfloat16)
 
 
 def column_tables():
@@ -90,9 +110,35 @@
     return jnp.where(hit, 1.0, 0.0).astype(BF16)
 
 
+ROOT = math.sqrt(0.5)
+RB = 16
+
+
+def eight_points(x):
+    a = [x[r] + x[r + 4] for r in range(4)]
+    b = [x[r] - x[r + 4] for r in range(4)]
+    even, odd = a[0] + a[2], a[1] + a[3]
+    c, d = (b[1] - b[3]) * ROOT, (b[1] + b[3]) * ROOT
+    return (
+        (even + odd, even - odd),
+        (b[0] + c, d + b[2]),
+        (a[0] - a[2], a[1] - a[3]),
+        (b[0] - c, d - b[2]),
+    )
+
+
+def eight_back(u):
+    (u0, u4), (p1, q1), (p2, q2), (p3, q3) = u
+    total, rest = u0 + u4, u0 - u4
+    even = (total + p2, rest - q2, total - p2, rest + q2)
+    c, d = (p1 - p3) * ROOT, (q1 + q3) * ROOT
+    odd = (p1 + p3, c - d, q3 - q1, -c - d)
+    return [even[r] + odd[r] for r in range(4)] + [even[r] - odd[r] for r in range(4)]
+
+
 def rows_kernel(
     maps, cot, in_w, out_w, table, spec_out, inner_out,
-    pairs, held, both, result, in_pair, out_pair, sems, table_sems, out_sems,
+    pairs, held, part, inner, eights, result, in_pair, out_pair, sems, table_sem, out_sems,
 ):
     half = ROWS * SPEC_CH
     loads = []
@@ -100,36 +146,59 @@
         for n, source in enumerate((maps, cot)):
             rows = source.at[0, pl.ds(2 * p, 2)]
             loads.append(pltpu.make_async_copy(rows, pairs.at[p, n], sems.at[p, n]))
-    tables = []
-    for b in range(4):
-        rows = pl.ds(b * 256, 256)
-        tables.append(pltpu.make_async_copy(table.at[rows], held.at[rows], table_sems.at[b]))
-    for copy in loads + tables:
-        copy.start()
+    table_load = pltpu.make_async_copy(table, held, table_sem)
+    def start(i):
+        p, n = (i % 4, i // 4)
+        loads[2 * p + n].start()
+
+    for i in range(8):
+        start(i)
+    table_load.start()
     a, b = first_half(), second_half()
     in_pair[0:PAIR, :] = dot_t(in_w[...], a).astype(BF16)
     in_pair[PAIR:, :] = dot_t(in_w[...], b).astype(BF16)
-    out_pair[0:PAIR, :] = dot_t(out_w[...], a).astype(BF16)
-    out_pair[PAIR:, :] = dot_t(out_w[...], b).astype(BF16)
-    for p in range(4):
-        lanes = slice(p * PAIR, (p + 1) * PAIR)
-        loads[2 * p].wait()
-        pair = jnp.concatenate([pairs[p, 0, 0], pairs[p, 0, 1]], axis=1)
-        both[:, lanes] = jnp.maximum(dot(pair, in_pair[...]), 0.0).astype(BF16)
-        lanes = slice(half + p * PAIR, half + (p + 1) * PAIR)
-        loads[2 * p + 1].wait()
-        pair = jnp.concatenate([pairs[p, 1, 0], pairs[p, 1, 1]], axis=1)
-        both[:, lanes] = dot(pair, out_pair[...]).astype(BF16)
-    stores = [pltpu.make_async_copy(both.at[:, pl.ds(0, half)], inner_out, out_sems.at[4])]
+    out_pair[0:PAIR, :] = (2.0 * dot_t(out_w[...], a)).astype(BF16)
+    out_pair[PAIR:, :] = (2.0 * dot_t(out_w[...], b)).astype(BF16)
+    def project(i):
+        p, n = (i % 4, i // 4)
+        loads[2 * p + n].wait()
+        if i + 8 < 8:
+            start(i + 8)
+        pair = jnp.concatenate([pairs[p, n, 0], pairs[p, n, 1]], axis=1)
+        part[i % 2] = dot(pair, out_pair[...] if n else in_pair[...])
+
+    project(0)
+    for i in range(8):
+        p, n = (i % 4, i // 4)
+        if i < 7:
+            project(i + 1)
+        lanes = slice(n * half + p * PAIR, n * half + (p + 1) * PAIR)
+
+        @pl.loop(0, 128, step=RB, unroll=True)
+        def _(rows):
+            rows = pl.multiple_of(rows, RB)
+            x = [part[i % 2, pl.ds(128 * r + rows, RB), :] for r in range(8)]
+            if n == 0:
+                x = [jnp.maximum(v, 0.0) for v in x]
+                for r in range(8):
+                    inner[pl.ds(128 * r + rows, RB), lanes] = x[r].astype(BF16)
+            for block, both in enumerate(eight_points(x)):
+                for k in range(2):
+                    eights[block, pl.ds(128 * k + rows, RB), lanes] = both[k].astype(BF16)
+
+    stores = [pltpu.make_async_copy(inner, inner_out, out_sems.at[4])]
     stores[0].start()
+    table_load.wait()
     for b in range(4):
         rows = pl.ds(b * 256, 256)
-        tables[b].wait()
-        prod = dot(held[rows, :], both[...])
+        prod = dot(held[b], eights[b])
         result[rows, 0:half] = prod[:, 0:half].astype(BF16)
-        row = b * 256 + iota((256, half), 0)
-        factor = jnp.where((row == 0) | (row == PER_GROUP), 1.0, 2.0)
-        result[rows, half:] = (prod[:, half:] * factor).astype(BF16)
+        if b == 0:
+            row = iota((256, half), 0)
+            factor = jnp.where((row == 0) | (row == PER_GROUP), 0.5, 1.0)
+            result[rows, half:] = (prod[:, half:] * factor).astype(BF16)
+        else:
+            result[rows, half:] = prod[:, half:].astype(BF16)
         stores.append(pltpu.make_async_copy(result.at[rows], spec_out.at[rows], out_sems.at[b]))
         stores[-1].start()
     for copy in stores:
@@ -148,21 +217,20 @@
         ],
         scratch_shapes=[
             pltpu.VMEM((4, 2, 2, WIDTH, 128), BF16),
-            pltpu.VMEM((1024, WIDTH), BF16),
-            pltpu.VMEM((WIDTH, 1024), BF16),
+            pltpu.VMEM((4, 256, 256), BF16),
+            pltpu.VMEM((2, WIDTH, PAIR), F32),
+            pltpu.VMEM((WIDTH, 512), BF16),
+            pltpu.VMEM((4, 256, 1024), BF16),
             pltpu.VMEM((1024, 1024), BF16),
             pltpu.VMEM((256, PAIR), BF16),
             pltpu.VMEM((256, PAIR), BF16),
             pltpu.SemaphoreType.DMA((4, 2)),
-            pltpu.SemaphoreType.DMA((4,)),
+            pltpu.SemaphoreType.DMA,
             pltpu.SemaphoreType.DMA((5,)),
         ],
         compiler_params=params(),
         cost_estimate=cost(5 * 10**9, 11 * 2**20),
     )(maps, cot, in_w, out_w, table)
-
-
-ROOT = math.sqrt(0.5)
 
 
 def lane_signs(shape):
@@ -236,9 +304,6 @@
     return out
 
 
-RB = 16
-
-
 def fill_mix(mix_w, wide):
     total = jnp.zeros((256, 256), F32)
     for t in range(2):
@@ -273,7 +338,7 @@
 
 def columns_kernel(
     block, forward_in, backward_in, twiddle_in, mix_in, ready, above, below, spec_out, back_out,
-    land, forward, backward, twiddle, mix_w, spec, stage, wide, prod, pre, inv, sems, out_sems,
+    land, forward, backward, twiddle, mix_w, spec, stage, back, wide, prod, pre, inv, sems, out_sems,
 ):
     del ready, above, below
     mix_load = pltpu.make_async_copy(mix_in, mix_w, sems.at[4])
@@ -292,13 +357,14 @@
     stores = []
     signs = lane_signs((RB, PAIR))
     first = iota((RB, PAIR), 1) < SPEC_CH
-    for kk in range(PER_GROUP):
-        prod[...] = dot(forward[...], gather_parts(stage, kk))
-
+    def transform(kk):
+        prod[kk % 2] = dot(forward[...], gather_parts(stage, kk))
+
+    def spectrum(kk):
         @pl.loop(0, GROUPS, step=RB, unroll=True)
         def _(rows):
             rows = pl.multiple_of(rows, RB)
-            parts = spectrum_rows(prod, twiddle, rows, signs, first)
+            parts = spectrum_rows(prod.at[kk % 2], twiddle, rows, signs, first)
             for q in range(4):
                 spec[kk * 4 + q, pl.ds(rows, RB), 0:PAIR] = parts[q][0].astype(BF16)
                 spec[kk * 4 + q, pl.ds(rows, RB), PAIR:] = parts[q][1].astype(BF16)
@@ -306,29 +372,46 @@
         part = pl.ds(kk * 4, 4)
         stores.append(pltpu.make_async_copy(spec.at[part], spec_out.at[part], out_sems.at[kk]))
         stores[-1].start()
-        pre[...] = dot(spec[kk * 4 : kk * 4 + 4].reshape(512, 256), wide[...])
-
+
+    def mix(kk):
+        pre[kk % 2] = dot(spec[kk * 4 : kk * 4 + 4].reshape(512, 256), wide[...])
+
+    def activate(kk):
         @pl.loop(0, GROUPS, step=RB, unroll=True)
         def _(rows):
             rows = pl.multiple_of(rows, RB)
             parts = []
             for q in range(4):
-                v = pre[pl.ds(q * GROUPS + rows, RB), :]
+                v = pre[kk % 2, pl.ds(q * GROUPS + rows, RB), :]
                 v = v * sigmoid(v)
                 parts.append((v[:, 0:PAIR], v[:, PAIR:]))
             pairs = inverse_rows(parts, twiddle, rows, signs, first)
             for m in range(4):
                 lanes = slice(m * PAIR, (m + 1) * PAIR)
-                inv[pl.ds(rows, RB), lanes] = pairs[m][0].astype(BF16)
-                inv[pl.ds(GROUPS + rows, RB), lanes] = pairs[m][1].astype(BF16)
-
-        result = dot(backward[...], inv[...])
+                inv[kk % 2, pl.ds(rows, RB), lanes] = pairs[m][0].astype(BF16)
+                inv[kk % 2, pl.ds(GROUPS + rows, RB), lanes] = pairs[m][1].astype(BF16)
+
+    def transform_back(kk):
+        result = dot(backward[...], inv[kk % 2])
         for m in range(4):
             lanes = slice(m * PAIR, (m + 1) * PAIR)
-            stage[m, pl.ds(kk, GROUPS, stride=ROWS), :] = result[0:GROUPS, lanes]
-            stage[m, pl.ds(PER_GROUP + kk, GROUPS, stride=ROWS), :] = result[GROUPS:, lanes]
+            back[m, pl.ds(kk, GROUPS, stride=ROWS), :] = result[0:GROUPS, lanes]
+            back[m, pl.ds(PER_GROUP + kk, GROUPS, stride=ROWS), :] = result[GROUPS:, lanes]
+
+    transform(0)
+    for kk in range(PER_GROUP + 2):
+        if kk + 1 < PER_GROUP:
+            transform(kk + 1)
+        if kk < PER_GROUP:
+            spectrum(kk)
+        if 0 <= kk - 1 < PER_GROUP:
+            activate(kk - 1)
+        if kk < PER_GROUP:
+            mix(kk)
+        if 0 <= kk - 1 < PER_GROUP:
+            transform_back(kk - 1)
     for m in range(4):
-        land[:, m * PAIR : (m + 1) * PAIR] = stage[m].astype(BF16)
+        land[:, m * PAIR : (m + 1) * PAIR] = back[m].astype(BF16)
         lanes = pl.ds(m * PAIR, PAIR)
         copy = pltpu.make_async_copy(land.at[:, lanes], back_out.at[:, lanes], out_sems.at[4 + m])
         copy.start()
@@ -358,10 +441,11 @@
             pltpu.VMEM((128, 128), BF16),
             pltpu.VMEM((16, GROUPS, 256), BF16),
             pltpu.VMEM((4, 1024, PAIR), F32),
+            pltpu.VMEM((4, 1024, PAIR), F32),
             pltpu.VMEM((256, 256), BF16),
-            pltpu.VMEM((256, 512), F32),
-            pltpu.VMEM((512, 256), F32),
-            pltpu.VMEM((256, 512), BF16),
+            pltpu.VMEM((2, 256, 512), F32),
+            pltpu.VMEM((2, 512, 256), F32),
+            pltpu.VMEM((2, 256, 512), BF16),
             pltpu.SemaphoreType.DMA((8,)),
             pltpu.SemaphoreType.DMA((8,)),
         ],
@@ -430,55 +514,53 @@
 
 def back_kernel(
     table, block, inner, cot, mix_part, ready, summed_out, terms_out,
-    held, inners, cots, mix, summed, terms, acc, sems, out_sems,
+    held, inners, cots, mix, summed, terms, packed, parts, sems, out_sems,
 ):
+    del ready
+
     def load(source, target, sem):
         copy = pltpu.make_async_copy(source, target, sems.at[sem])
         copy.start()
         return copy
 
-    del ready
-    loads = []
+    first = load(table, held, 0)
+    second = load(inner, inners, 1)
+    pairs = [load(cot.at[0, pl.ds(2 * p, 2)], cots.at[p], 2 + p) for p in range(4)]
+    last = load(mix_part, mix, 6)
+    first.wait()
     for b in range(4):
-        at = pl.ds(b * 256, 256)
-        loads.append(
-            (
-                load(table.at[at], held.at[at], 4 * b + 1),
-                load(inner.at[at], inners.at[at], 4 * b + 2),
-                load(cot.at[0, :, at], cots.at[:, at], 4 * b + 3),
-            )
-        )
-    last = load(mix_part, mix, 4)
-    stores = []
-    for b in range(4):
-        for copy in loads[b]:
-            copy.wait()
-        at = slice(b * 256, (b + 1) * 256)
-        total = (dot(held[at, :], block[...]) + inners[at, :].astype(F32)).astype(BF16)
-        summed[at, :] = total
-        rows_at = pl.ds(b * 256, 256)
-        copy = pltpu.make_async_copy(summed.at[rows_at], summed_out.at[rows_at], out_sems.at[b])
-        copy.start()
-        stores.append(copy)
-        for p in range(4):
-            pair = jnp.concatenate([cots[2 * p, at, :], cots[2 * p + 1, at, :]], axis=1)
-            part = dot_t(pair, total[:, p * PAIR : (p + 1) * PAIR])
-            if b + p:
-                acc[...] += part
-            else:
-                acc[...] = part
+        parts[b] = dot(held[b], block[b * 256 : (b + 1) * 256, :])
+    second.wait()
+    acc = jnp.zeros((PAIR, 256), F32)
+    for p in range(4):
+        lanes = slice(p * PAIR, (p + 1) * PAIR)
+
+        @pl.loop(0, 128, step=RB, unroll=True)
+        def _(rows):
+            rows = pl.multiple_of(rows, RB)
+            u = [
+                [parts[b, pl.ds(128 * i + rows, RB), lanes] for i in range(2)] for b in range(4)
+            ]
+            for r, x in enumerate(eight_back(u)):
+                at = pl.ds(128 * r + rows, RB)
+                summed[at, lanes] = (x + inners[at, lanes].astype(F32)).astype(BF16)
+
+        pairs[p].wait()
+        pair = jnp.concatenate([cots[p, 0], cots[p, 1]], axis=1)
+        acc = acc + dot_t(summed[:, lanes], pair)
+    store = pltpu.make_async_copy(summed, summed_out, out_sems.at[0])
+    store.start()
     last.wait()
-    lane = iota((128, PAIR), 1) < SPEC_CH
-    out_part = acc[0:128, :] + pltpu.roll(acc[128:, :], SPEC_CH, 1)
-    out_part = jnp.where(lane, out_part, 0.0)
+    out_part = acc[0:SPEC_CH, 0:128] + acc[SPEC_CH:, 128:]
+    out_part = jnp.concatenate([out_part, jnp.zeros((SPEC_CH, 128), F32)], axis=0).T
     for img in range(2):
         terms[pl.ds(2 * img, 128, stride=4), :] = mix[...]
         terms[pl.ds(2 * img + 1, 128, stride=4), :] = out_part
-    copy = pltpu.make_async_copy(terms, terms_out, out_sems.at[4])
+    packed[...] = terms[...].astype(BF16)
+    copy = pltpu.make_async_copy(packed, terms_out, out_sems.at[1])
     copy.start()
-    stores.append(copy)
-    for copy in stores:
-        copy.wait()
+    store.wait()
+    copy.wait()
 
 
 def back_rows(table, rows, inner, cot, mix_part, ready):
@@ -488,18 +570,19 @@
         out_specs=[ANY, ANY],
         out_shape=[
             pltpu.HBM((WIDTH, 512), BF16),
-            pltpu.HBM((512, 128), F32),
+            pltpu.HBM((512, 128), BF16),
         ],
         scratch_shapes=[
-            pltpu.VMEM((WIDTH, 1024), BF16),
+            pltpu.VMEM((4, 256, 256), BF16),
             pltpu.VMEM((WIDTH, 512), BF16),
-            pltpu.VMEM((ROWS, WIDTH, 128), BF16),
+            pltpu.VMEM((4, 2, WIDTH, 128), BF16),
             pltpu.VMEM((128, 128), F32),
             pltpu.VMEM((WIDTH, 512), BF16),
             pltpu.VMEM((512, 128), F32),
-            pltpu.VMEM((256, 128), F32),
-            pltpu.SemaphoreType.DMA((17,)),
-            pltpu.SemaphoreType.DMA((5,)),
+            pltpu.VMEM((512, 128), BF16),
+            pltpu.VMEM((4, 256, 512), F32),
+            pltpu.SemaphoreType.DMA((7,)),
+            pltpu.SemaphoreType.DMA((2,)),
         ],
         compiler_params=params(SMALL),
         cost_estimate=cost(2 * 10**9, 8 * 2**20),
@@ -642,7 +725,7 @@
     terms = terms.reshape(256, 2, 128)
     terms = lax.all_to_all(terms, ("rows", "img"), split_axis=0, concat_axis=0, tiled=True)
     global_out = project_out(summed, out_weight)
-    total = jnp.sum(terms, axis=0)
+    total = jnp.sum(terms.astype(F32), axis=0)
     mix_grad = total[0].reshape(128, 1)
     out_grad = total[1, 0:SPEC_CH].reshape(SPEC_CH, 1)
     return (local_out, global_out, mix_grad, out_grad)

time: 152 us -> 145 us (0.954)
  Pallas kernels: 41.1 us -> 37.3 us
  waiting for transfers between devices: 73.2 us -> 70.3 us
    all_to_all x1, waiting for transfers between devices: 11.6 us -> 8.71 us  [shards(): lax.all_to_all(terms, ('rows', 'img'), split_axis=0, concat_axis=0, tiled...]
    pallas_call x1, Pallas kernels: 8.95 us -> 7.1 us  [rows_forward(): pl.pallas_call(rows_kernel, grid=(1,), in_specs=[ANY, ANY, whole_spec((SP...]
  transfers between devices with their start and end apart: 5 -> 5, of which waited for: 3 -> 3; matrix products, arithmetic and copies ran while one was open for 1% -> 1% of each run, Pallas kernels for 14% -> 15%
where the time goes in v4:
time: 145 us; the launch traced here: 144 us
  waiting for transfers between devices  70.3 us (48%)
  Pallas kernels  37.3 us (26%)
  starting transfers between devices  33.4 us (23%)
  local copies, waits for them, and re-layouts  2.13 us (1%)
    all_to_all x2, waiting for transfers between devices, exchange(): lax.all_to_all(block.reshape(GROUPS, ROWS, lanes), 'rows', split_axis=0,...  61.6 us
    all_to_all x2, starting transfers between devices, exchange(): lax.all_to_all(block.reshape(GROUPS, ROWS, lanes), 'rows', split_axis=0,...  22 us
    pallas_call x2, Pallas kernels, conv_call(): pl.pallas_call(kernel, grid=(rows,), in_specs=in_specs, out_specs=[row_sp...  11.5 us
    all_to_all x1, waiting for transfers between devices, shards(): lax.all_to_all(terms, ('rows', 'img'), split_axis=0, concat_axis=0, tiled...  8.71 us
    pallas_call x1, Pallas kernels, rows_forward(): pl.pallas_call(rows_kernel, grid=(1,), in_specs=[ANY, ANY, whole_spec((SP...  7.1 us
    all_to_all x1, starting transfers between devices, shards(): lax.all_to_all(terms, ('rows', 'img'), split_axis=0, concat_axis=0, tiled...  5.72 us
    pallas_call x1, Pallas kernels, mix_terms(): pl.pallas_call(mix_kernel, grid=(1,), in_specs=[pl.BlockSpec((1024, 512),...  5.51 us
    pallas_call x1, Pallas kernels, columns(): pl.pallas_call(columns_kernel, in_specs=[VMEM] + [ANY] * 7, out_specs=[AN...  5.3 us
  transfers between devices with their start and end apart: 5, of which 3 were waited for; matrix products, arithmetic and copies ran while one was open for 1% of the time, Pallas kernels for 15%

profile of v4, /device:TPU:1, one launch (start us, length us, event | category | flops | bytes accessed | tf_op | source)
XLA Modules:
  0.0 144.1 jit_solution(17812209883116222075)
XLA Ops:
  0.6 7.1 %shard_map.147 = (bf16[1024,1024]{1,0:T(8,128)(2,1)}, bf16[1024,512]{1,0:T(8,128)(2,1)}) custom-call(bf16[1,8,1024,128]{3,2,1,0:T(8,128)(2,1)} %maps.1, bf16[1,8,1024,128]{3,2,1,0:T(8,128)(2,1)} %cot.3, bf16[64,128]{1,0:T(8,128)(2,1)} %bitcast.16, bf16[64,128]{1,0:T(8,128)(2,1)} %out_w.3, bf16[4,256,256]{2,1,0:T(8,128)(2,1)} %constant.12.clone.table), custom_call_target="tpu_custom_call" | custom-call | flops 5000000000 | bytes 11534336 | tf_op jit(solution)/shard_map/pallas_call | solution.py:209
  7.7 14.9 %all-to-all-start = ((bf16[128,8,1024]{2,1,0:T(8,128)(2,1)}), bf16[128,8,1024]{2,1,0:T(8,128)(2,1)S(1)}, u32[]{:S(2)}, u32[]{:S(2)}) async-start(bf16[128,8,1024]{2,1,0:T(8,128)(2,1)} %bitcast.14), calls=%async_computation | async-start | bytes 4194304 | tf_op jit(solution)/shard_map/all_to_all | solution.py:705
  22.6 1.1 fusion
  23.7 2.8 %collective-permute-start.1 = (bf16[1,1,1024,128]{3,2,1,0:T(8,128)(2,1)S(1)}, bf16[1,1,1024,128]{3,2,1,0:T(8,128)(2,1)S(1)}, u32[]{:S(2)}, u32[]{:S(2)}) collective-permute-start(bf16[1,1,1024,128]{3,2,1,0:T(8,128)(2,1)S(1)} %get-tuple-element.24), channel_id=1, source_target_pairs={{2,0},{4,2},{6,4},{8,6},{10,8},{12,10},{14,12},{16,14},{18,16},{20... | collective-permute-start | bytes 786440 | tf_op jit(solution)/shard_map/ppermute | solution.py:685
  26.5 0.0 copy-start.3
  26.5 0.0 copy-start.4
  26.5 0.0 copy-start.5
  26.5 0.0 copy-start.6
  26.6 2.9 %collective-permute-start = (bf16[1,1,1024,128]{3,2,1,0:T(8,128)(2,1)S(1)}, bf16[1,1,1024,128]{3,2,1,0:T(8,128)(2,1)S(1)}, u32[]{:S(2)}, u32[]{:S(2)}) collective-permute-start(bf16[1,1,1024,128]{3,2,1,0:T(8,128)(2,1)S(1)} %get-tuple-element.25), channel_id=1, source_target_pairs={{0,2},{2,4},{4,6},{6,8},{8,10},{10,12},{12,14},{14,16},{16,18},{18... | collective-permute-start | bytes 786440 | tf_op jit(solution)/shard_map/ppermute | solution.py:684
  29.5 7.8 %shard_map.148 = (bf16[1,8,1024,128]{3,2,1,0:T(8,128)(2,1)}, f32[8,128]{1,0:T(8,128)}) custom-call(bf16[1,8,1024,128]{3,2,1,0:T(8,128)(2,1)} %beside.1, bf16[1,8,1024,128]{3,2,1,0:T(8,128)(2,1)} %beside.1, bf16[1,8,1024,128]{3,2,1,0:T(8,128)(2,1)} %beside.1, bf16[3,3,128,128]{3,2,1,0:T(8,128)(2,1)} %weight.3, bf16[1024,1024]{1,0:T(8,128)(2,1)} %get-tuple-element.14.ready), custom_call_target="tpu_custom_call" | custom-call | flops 6000000000 | bytes 6291456 | tf_op jit(solution)/shard_map/pallas_call | solution.py:653
  37.2 0.0 collective-permute-done.1.below.edge_below
  37.2 0.0 copy-start.1
  37.2 0.0 collective-permute-done.above.edge_above
  37.3 0.0 copy-start.2
  37.3 39.2 %all-to-all-done = bf16[128,8,1024]{2,1,0:T(8,128)(2,1)S(1)} async-done(((bf16[128,8,1024]{2,1,0:T(8,128)(2,1)}), bf16[128,8,1024]{2,1,0:T(8,128)(2,1)S(1)}, u32[]{:S(2)}, u32[]{:S(2)}) %all-to-all-start) | async-done | bytes 2097184 | tf_op jit(solution)/shard_map/all_to_all | solution.py:705
  76.5 0.0 copy-start
  76.5 0.0 copy-done.3
  76.5 0.0 copy-done.4
  76.5 0.0 copy-done.5
  76.5 0.0 copy-done.6
  76.5 5.3 %shard_map.149 = (bf16[16,128,256]{2,1,0:T(8,128)(2,1)}, bf16[1024,512]{1,0:T(8,128)(2,1)}) custom-call(bf16[1024,1024]{1,0:T(8,128)(2,1)S(1)} %bitcast.10, bf16[256,256]{1,0:T(8,128)(2,1)S(1)} %copy-done.5, bf16[256,256]{1,0:T(8,128)(2,1)S(1)} %copy-done.6, f32[2,128,512]{2,1,0:T(8,128)S(1)} %copy-done.4, bf16[128,128]{1,0:T(8,128)(2,1)S(1)} %copy-done.3, ...), custom_call_target="tpu_custom_call" | custom-call | flops 8000000000 | bytes 5242880 | tf_op jit(solution)/shard_map/pallas_call | solution.py:428
  81.8 0.0 copy-done.1
  81.8 0.0 copy-done.2
  81.8 0.0 copy-done
  81.8 7.1 %all-to-all-start.1 = ((bf16[128,8,512]{2,1,0:T(8,128)(2,1)}), bf16[128,8,512]{2,1,0:T(8,128)(2,1)S(1)}, u32[]{:S(2)}, u32[]{:S(2)}) async-start(bf16[128,8,512]{2,1,0:T(8,128)(2,1)} %bitcast.13), calls=%async_computation.1 | async-start | bytes 2097152 | tf_op jit(solution)/shard_map/all_to_all | solution.py:705
  88.9 3.7 %shard_map.150 = (bf16[1,8,1024,128]{3,2,1,0:T(8,128)(2,1)}, f32[8,128]{1,0:T(8,128)}) custom-call(bf16[1,8,1024,128]{3,2,1,0:T(8,128)(2,1)} %beside.1, bf16[1,8,1024,128]{3,2,1,0:T(8,128)(2,1)} %beside.1, bf16[1,1,1024,128]{3,2,1,0:T(8,128)(2,1)} %copy-done.2, bf16[1,1,1024,128]{3,2,1,0:T(8,128)(2,1)} %copy-done.1, ...), custom_call_target="tpu_custom_call", output_to_operand_aliasing={{0}: (5, {})} | custom-call | flops 2000000000 | bytes 2097152 | tf_op jit(solution)/shard_map/pallas_call | solution.py:653
  92.7 5.5 %shard_map.151.mix_part = f32[128,128]{1,0:T(8,128)} custom-call(bf16[1024,1024]{1,0:T(8,128)(2,1)} %bitcast.11, bf16[16,128,256]{2,1,0:T(8,128)(2,1)} %get-tuple-element.20.spec, bf16[256,256]{1,0:T(8,128)(2,1)} %constant.13.clone.forward_in.forward, f32[2,128,512]{2,1,0:T(8,128)} %constant.15.clone.twiddle_in.twiddle, bf16[128,128]{1,0:T(8,128)(2,1)} %mix_w.1), custom_call_target="tpu_custom_call" | custom-call | flops 6000000000 | bytes 5242880 | tf_op jit(solution)/shard_map/pallas_call | solution.py:490
  98.2 22.4 %all-to-all-done.1 = bf16[128,8,512]{2,1,0:T(8,128)(2,1)S(1)} async-done(((bf16[128,8,512]{2,1,0:T(8,128)(2,1)}), bf16[128,8,512]{2,1,0:T(8,128)(2,1)S(1)}, u32[]{:S(2)}, u32[]{:S(2)}) %all-to-all-start.1) | async-done | bytes 1048608 | tf_op jit(solution)/shard_map/all_to_all | solution.py:705
  120.5 3.7 %shard_map.152 = (bf16[1024,512]{1,0:T(8,128)(2,1)}, bf16[512,128]{1,0:T(8,128)(2,1)}) custom-call(bf16[4,256,256]{2,1,0:T(8,128)(2,1)} %constant.16.clone.table, bf16[1024,512]{1,0:T(8,128)(2,1)S(1)} %bitcast.12, bf16[1024,512]{1,0:T(8,128)(2,1)} %get-tuple-element.19.inner, bf16[1,8,1024,128]{3,2,1,0:T(8,128)(2,1)} %cot.3, ...), custom_call_target="tpu_custom_call" | custom-call | flops 2000000000 | bytes 8388608 | tf_op jit(solution)/shard_map/pallas_call | solution.py:567
  124.3 5.7 %all-to-all-start.2 = ((bf16[256,2,128]{2,1,0:T(2,128)(2,1)}), bf16[256,2,128]{2,1,0:T(2,128)(2,1)S(1)}, u32[]{:S(2)}, u32[]{:S(2)}) async-start(bf16[256,2,128]{2,1,0:T(2,128)(2,1)} %bitcast.15), calls=%async_computation.2 | async-start | bytes 262144 | tf_op jit(solution)/shard_map/all_to_all | solution.py:726
  130.0 4.1 %shard_map.153 = bf16[1,8,1024,128]{3,2,1,0:T(8,128)(2,1)} custom-call(bf16[1024,512]{1,0:T(8,128)(2,1)} %get-tuple-element.22.summed, bf16[64,128]{1,0:T(8,128)(2,1)} %out_w.3), custom_call_target="tpu_custom_call" | custom-call | flops 500000000 | bytes 3145728 | tf_op jit(solution)/shard_map/pallas_call | solution.py:606
  134.1 8.7 %all-to-all-done.2 = bf16[256,2,128]{2,1,0:T(2,128)(2,1)S(1)} async-done(((bf16[256,2,128]{2,1,0:T(2,128)(2,1)}), bf16[256,2,128]{2,1,0:T(2,128)(2,1)S(1)}, u32[]{:S(2)}, u32[]{:S(2)}) %all-to-all-start.2) | async-done | bytes 131104 | tf_op jit(solution)/shard_map/all_to_all | solution.py:726
  142.8 0.3 convert_reduce_fusion
  143.1 0.5 slice_bitcast_fusion
  143.6 0.5 slice_bitcast_fusion.1
Async XLA Ops:
  7.7 68.7 %all-to-all-start = ((bf16[128,8,1024]{2,1,0:T(8,128)(2,1)}), bf16[128,8,1024]{2,1,0:T(8,128)(2,1)S(1)}, u32[]{:S(2)}, u32[]{:S(2)}) async-start(bf16[128,8,1024]{2,1,0:T(8,128)(2,1)} %bitcast.14), calls=%async_computation | async-start | bytes 4194304 | tf_op jit(solution)/shard_map/all_to_all | solution.py:705
  23.7 13.5 %collective-permute-start.1 = (bf16[1,1,1024,128]{3,2,1,0:T(8,128)(2,1)S(1)}, bf16[1,1,1024,128]{3,2,1,0:T(8,128)(2,1)S(1)}, u32[]{:S(2)}, u32[]{:S(2)}) collective-permute-start(bf16[1,1,1024,128]{3,2,1,0:T(8,128)(2,1)S(1)} %get-tuple-element.24), channel_id=1, source_target_pairs={{2,0},{4,2},{6,4},{8,6},{10,8},{12,10},{14,12},{16,14},{18,16},{20... | collective-permute-start | bytes 786440 | tf_op jit(solution)/shard_map/ppermute | solution.py:685
  26.5 50.0 %copy-start.3 = (bf16[128,128]{1,0:T(8,128)(2,1)S(1)}, bf16[128,128]{1,0:T(8,128)(2,1)}, u32[]{:S(2)}) copy-start(bf16[128,128]{1,0:T(8,128)(2,1)} %mix_w.1) | copy-start | bytes 98308
  26.5 50.0 %copy-start.4 = (f32[2,128,512]{2,1,0:T(8,128)S(1)}, f32[2,128,512]{2,1,0:T(8,128)}, u32[]{:S(2)}) copy-start(f32[2,128,512]{2,1,0:T(8,128)} %constant.15.clone.twiddle_in.twiddle) | copy-start | bytes 1572868
  26.5 49.9 %copy-start.5 = (bf16[256,256]{1,0:T(8,128)(2,1)S(1)}, bf16[256,256]{1,0:T(8,128)(2,1)}, u32[]{:S(2)}) copy-start(bf16[256,256]{1,0:T(8,128)(2,1)} %constant.13.clone.forward_in.forward) | copy-start | bytes 393220
  26.5 49.9 %copy-start.6 = (bf16[256,256]{1,0:T(8,128)(2,1)S(1)}, bf16[256,256]{1,0:T(8,128)(2,1)}, u32[]{:S(2)}) copy-start(bf16[256,256]{1,0:T(8,128)(2,1)} %constant.14.clone.backward_in) | copy-start | bytes 393220
  26.6 10.7 %collective-permute-start = (bf16[1,1,1024,128]{3,2,1,0:T(8,128)(2,1)S(1)}, bf16[1,1,1024,128]{3,2,1,0:T(8,128)(2,1)S(1)}, u32[]{:S(2)}, u32[]{:S(2)}) collective-permute-start(bf16[1,1,1024,128]{3,2,1,0:T(8,128)(2,1)S(1)} %get-tuple-element.25), channel_id=1, source_target_pairs={{0,2},{2,4},{4,6},{6,8},{8,10},{10,12},{12,14},{14,16},{16,18},{18... | collective-permute-start | bytes 786440 | tf_op jit(solution)/shard_map/ppermute | solution.py:684
  37.2 44.6 %copy-start.1 = (bf16[1,1,1024,128]{3,2,1,0:T(8,128)(2,1)}, bf16[1,1,1024,128]{3,2,1,0:T(8,128)(2,1)S(1)}, u32[]{:S(2)}) copy-start(bf16[1,1,1024,128]{3,2,1,0:T(8,128)(2,1)S(1)} %collective-permute-done.1.below.edge_below) | copy-start | bytes 786436
  37.3 44.6 %copy-start.2 = (bf16[1,1,1024,128]{3,2,1,0:T(8,128)(2,1)}, bf16[1,1,1024,128]{3,2,1,0:T(8,128)(2,1)S(1)}, u32[]{:S(2)}) copy-start(bf16[1,1,1024,128]{3,2,1,0:T(8,128)(2,1)S(1)} %collective-permute-done.above.edge_above) | copy-start | bytes 786436
  76.5 5.4 %copy-start = (bf16[128,8,1024]{2,1,0:T(8,128)(2,1)}, bf16[128,8,1024]{2,1,0:T(8,128)(2,1)S(1)}, u32[]{:S(2)}) copy-start(bf16[128,8,1024]{2,1,0:T(8,128)(2,1)S(1)} %all-to-all-done) | copy-start | bytes 6291460
  81.8 38.7 %all-to-all-start.1 = ((bf16[128,8,512]{2,1,0:T(8,128)(2,1)}), bf16[128,8,512]{2,1,0:T(8,128)(2,1)S(1)}, u32[]{:S(2)}, u32[]{:S(2)}) async-start(bf16[128,8,512]{2,1,0:T(8,128)(2,1)} %bitcast.13), calls=%async_computation.1 | async-start | bytes 2097152 | tf_op jit(solution)/shard_map/all_to_all | solution.py:705
  124.3 18.5 %all-to-all-start.2 = ((bf16[256,2,128]{2,1,0:T(2,128)(2,1)}), bf16[256,2,128]{2,1,0:T(2,128)(2,1)S(1)}, u32[]{:S(2)}, u32[]{:S(2)}) async-start(bf16[256,2,128]{2,1,0:T(2,128)(2,1)} %bitcast.15), calls=%async_computation.2 | async-start | bytes 262144 | tf_op jit(solution)/shard_map/all_to_all | solution.py:726

commit v5 on v4

--- a/solution.py
+++ b/solution.py
@@ -552,10 +552,11 @@
     store.start()
     last.wait()
     out_part = acc[0:SPEC_CH, 0:128] + acc[SPEC_CH:, 128:]
-    out_part = jnp.concatenate([out_part, jnp.zeros((SPEC_CH, 128), F32)], axis=0).T
+    high = out_part.astype(BF16).astype(F32)
+    out_both = jnp.concatenate([high, out_part - high], axis=0).T
     for img in range(2):
         terms[pl.ds(2 * img, 128, stride=4), :] = mix[...]
-        terms[pl.ds(2 * img + 1, 128, stride=4), :] = out_part
+        terms[pl.ds(2 * img + 1, 128, stride=4), :] = out_both
     packed[...] = terms[...].astype(BF16)
     copy = pltpu.make_async_copy(packed, terms_out, out_sems.at[1])
     copy.start()
@@ -589,47 +590,70 @@
     )(in_hbm(table), rows, in_hbm(inner), in_hbm(cot), in_hbm(mix_part), in_hbm(ready))
 
 
-def out_kernel(summed, out_w, out, wide):
-    @pl.when(pl.program_id(0) == 0)
-    def _():
-        zero = jnp.zeros((SPEC_CH, 128), BF16)
-        wide[0:SPEC_CH, :] = jnp.concatenate([out_w[...], zero], axis=1)
-        wide[SPEC_CH:, :] = jnp.concatenate([zero, out_w[...]], axis=1)
-
+def out_kernel(summed, out_w, out, held, wide, result, sems, out_sems):
+    loads = []
     for p in range(4):
-        prod = dot(summed[:, p * PAIR : (p + 1) * PAIR], wide[...]).astype(BF16)
-        out[0, 2 * p] = prod[:, 0:128]
-        out[0, 2 * p + 1] = prod[:, 128:]
+        lanes = pl.ds(p * PAIR, PAIR)
+        loads.append(pltpu.make_async_copy(summed.at[:, lanes], held.at[p], sems.at[p]))
+        loads[p].start()
+    zero = jnp.zeros((SPEC_CH, 128), BF16)
+    wide[0:SPEC_CH, :] = jnp.concatenate([out_w[...], zero], axis=1)
+    wide[SPEC_CH:, :] = jnp.concatenate([zero, out_w[...]], axis=1)
+    stores = []
+    for p in range(4):
+        loads[p].wait()
+        prod = dot(held[p], wide[...])
+        result[2 * p] = prod[:, 0:128].astype(BF16)
+        result[2 * p + 1] = prod[:, 128:].astype(BF16)
+        rows = pl.ds(2 * p, 2)
+        stores.append(pltpu.make_async_copy(result.at[rows], out.at[0, rows], out_sems.at[p]))
+        stores[p].start()
+    for copy in stores:
+        copy.wait()
 
 
 def project_out(summed, out_w):
     return pl.pallas_call(
         out_kernel,
-        grid=(4,),
-        in_specs=[pl.BlockSpec((256, 512), lambda i: (i, 0)), whole_spec((SPEC_CH, 128))],
-        out_specs=pl.BlockSpec((1, ROWS, 256, 128), lambda i: (0, 0, i, 0)),
-        out_shape=jax.ShapeDtypeStruct((1, ROWS, WIDTH, 128), BF16),
-        scratch_shapes=[pltpu.VMEM((128, 256), BF16)],
+        grid=(1,),
+        in_specs=[ANY, whole_spec((SPEC_CH, 128))],
+        out_specs=ANY,
+        out_shape=pltpu.HBM((1, ROWS, WIDTH, 128), BF16),
+        scratch_shapes=[
+            pltpu.VMEM((4, WIDTH, PAIR), BF16),
+            pltpu.VMEM((128, 256), BF16),
+            pltpu.VMEM((ROWS, WIDTH, 128), BF16),
+            pltpu.SemaphoreType.DMA((4,)),
+            pltpu.SemaphoreType.DMA((4,)),
+        ],
         compiler_params=params(),
         cost_estimate=cost(5 * 10**8, 3 * 2**20),
     )(summed, out_w)
+
+
+def fill_wide(weight, wide, sums):
+    for a in range(3):
+        for b in range(3):
+            wide[a * 128 : (a + 1) * 128, b * 128 : (b + 1) * 128] = weight[a, b]
+    sums[0, 0:8] = jnp.zeros((8, 128), F32)
+    sums[2, WIDTH + 8 :] = jnp.zeros((8, 128), F32)
+
+
+def conv_sums(top, mid, bottom, sums, wide):
+    prod = dot(jnp.concatenate([top, mid, bottom], axis=1), wide[...])
+    for b in range(3):
+        sums[b, 8 : WIDTH + 8] = prod[:, b * 128 : (b + 1) * 128]
+    total = sums[0, 7 : WIDTH + 7] + sums[1, 8 : WIDTH + 8] + sums[2, 9 : WIDTH + 9]
+    return total.astype(BF16)
 
 
 def conv_row(top, mid, bottom, weight, out, token, sums, wide):
     @pl.when(pl.program_id(0) == 0)
     def _():
         token[...] = jnp.zeros((8, 128), F32)
-        for a in range(3):
-            for b in range(3):
-                wide[a * 128 : (a + 1) * 128, b * 128 : (b + 1) * 128] = weight[a, b]
-        sums[0, 0:8] = jnp.zeros((8, 128), F32)
-        sums[2, WIDTH + 8 :] = jnp.zeros((8, 128), F32)
-
-    prod = dot(jnp.concatenate([top, mid, bottom], axis=1), wide[...])
-    for b in range(3):
-        sums[b, 8 : WIDTH + 8] = prod[:, b * 128 : (b + 1) * 128]
-    total = sums[0, 7 : WIDTH + 7] + sums[1, 8 : WIDTH + 8] + sums[2, 9 : WIDTH + 9]
-    out[0, 0] = total.astype(BF16)
+        fill_wide(weight, wide, sums)
+
+    out[0, 0] = conv_sums(top, mid, bottom, sums, wide)
 
 
 def inner_kernel(above, mid, below, weight, ready, out, token, sums, wide):
@@ -643,6 +667,28 @@
     top = jnp.where(first, edge_above[0, 0], beside[0, 0])
     bottom = jnp.where(first, beside[0, 0], edge_below[0, 0])
     conv_row(top, mid[0, 0], bottom, weight, out, token, sums, wide)
+
+
+def sum_kernel(terms, mix, out):
+    total = jnp.sum(terms[...].astype(F32).reshape(64, 8, 128), axis=0)
+    even = iota((8, 128), 0) % 2 == 0
+    mix[...] = jnp.sum(jnp.where(even, total, 0.0), axis=0, keepdims=True)
+    odd = jnp.sum(jnp.where(even, 0.0, total), axis=0, keepdims=True)
+    out[...] = odd[:, 0:SPEC_CH] + odd[:, SPEC_CH:]
+
+
+def sum_terms(terms):
+    return pl.pallas_call(
+        sum_kernel,
+        in_specs=[VMEM],
+        out_specs=[VMEM, VMEM],
+        out_shape=[
+            jax.ShapeDtypeStruct((1, 128), F32),
+            jax.ShapeDtypeStruct((1, SPEC_CH), F32),
+        ],
+        compiler_params=params(SMALL),
+        cost_estimate=cost(10**6, 2**17),
+    )(terms)
 
 
 def row_spec(index):
@@ -678,12 +724,22 @@
     return conv_call(inner_kernel, ROWS - 2, specs, lambda i: i + 1, {}, args)
 
 
+BLOCK = 8
+
+
 def neighbour_rows(cells):
-    ends = GROUPS - 1
     head, tail = cells[:, 0:1], cells[:, ROWS - 1 :]
-    above = lax.ppermute(tail, "rows", [(i, i + 1) for i in range(ends)])
-    below = lax.ppermute(head, "rows", [(i + 1, i) for i in range(ends)])
+    near = [i for i in range(GROUPS - 1) if i % BLOCK != BLOCK - 1]
+    above = lax.ppermute(tail, "rows", [(i, i + 1) for i in near])
+    below = lax.ppermute(head, "rows", [(i + 1, i) for i in near])
     return above, below
+
+
+def far_row(cells):
+    last = lax.axis_index("rows") % BLOCK == BLOCK - 1
+    row = lax.dynamic_slice_in_dim(cells, jnp.where(last, ROWS - 1, 0), 1, axis=1)
+    far = range(BLOCK - 1, GROUPS - 1, BLOCK)
+    return lax.ppermute(row, "rows", [(i, i + 1) for i in far] + [(i + 1, i) for i in far])
 
 
 def edge_rows(cells, above, below, weight, done, ready):
@@ -698,6 +754,59 @@
     ]
     args = (cells, cells, above, below, weight, done, ready)
     return conv_call(edge_kernel, 2, specs, lambda i: i * (ROWS - 1), {5: 0}, args)
+
+
+def far_kernel(cells, above, far, weight_in, done, ready, out, lines, weight, row_out, sums, wide, sems):
+    del done, ready
+    at = lax.axis_index("rows") % BLOCK
+    last = at == BLOCK - 1
+    row = jnp.where(last, ROWS - 1, 0)
+    beside = jnp.where(last, ROWS - 2, 1)
+    outer = jnp.where(last, 2, 0)
+    weights = pltpu.make_async_copy(weight_in, weight, sems.at[0])
+    weights.start()
+    own = pltpu.make_async_copy(cells.at[0, row], lines.at[1], sems.at[1])
+    own.start()
+    inside = pltpu.make_async_copy(cells.at[0, beside], lines.at[2 - outer], sems.at[2])
+    inside.start()
+
+    @pl.when((at == 0) | last)
+    def _():
+        pltpu.make_async_copy(far.at[0, 0], lines.at[outer], sems.at[3]).start()
+
+    @pl.when((at > 0) & (at < BLOCK - 1))
+    def _():
+        pltpu.make_async_copy(above.at[0, 0], lines.at[outer], sems.at[3]).start()
+
+    weights.wait()
+    fill_wide(weight, wide, sums)
+    own.wait()
+    inside.wait()
+    pltpu.make_async_copy(above.at[0, 0], lines.at[outer], sems.at[3]).wait()
+    row_out[...] = conv_sums(lines[0], lines[1], lines[2], sums, wide)
+    copy = pltpu.make_async_copy(row_out, out.at[0, row], sems.at[4])
+    copy.start()
+    copy.wait()
+
+
+def far_edge(cells, above, far, weight, done, ready):
+    return pl.pallas_call(
+        far_kernel,
+        in_specs=[ANY] * 6,
+        out_specs=ANY,
+        out_shape=pltpu.HBM((1, ROWS, WIDTH, 128), BF16),
+        scratch_shapes=[
+            pltpu.VMEM((3, WIDTH, 128), BF16),
+            pltpu.VMEM((3, 3, 128, 128), BF16),
+            pltpu.VMEM((WIDTH, 128), BF16),
+            pltpu.VMEM((3, WIDTH + 16, 128), F32),
+            pltpu.VMEM((384, 384), BF16),
+            pltpu.SemaphoreType.DMA((5,)),
+        ],
+        input_output_aliases={4: 0},
+        compiler_params=params(SMALL),
+        cost_estimate=cost(10**9, 2**20),
+    )(in_hbm(cells), in_hbm(above), far, in_hbm(weight), in_hbm(done), in_hbm(ready))
 
 
 def exchange(block):
@@ -722,12 +831,14 @@
     mix_part = mix_terms(spec_cols, spectrum, forward, twiddle, mix_weight)
     local_out, token = edge_rows(local_maps, above, below, conv_weight, local_inner, back_cols)
     summed, terms = back_rows(row_inv, back, inner, out_cotangent, mix_part, token)
+    local_out = far_edge(
+        local_maps, above, far_row(local_maps), conv_weight, local_out, in_hbm(terms)
+    )
     terms = terms.reshape(256, 2, 128)
     terms = lax.all_to_all(terms, ("rows", "img"), split_axis=0, concat_axis=0, tiled=True)
     global_out = project_out(summed, out_weight)
-    total = jnp.sum(terms.astype(F32), axis=0)
-    mix_grad = total[0].reshape(128, 1)
-    out_grad = total[1, 0:SPEC_CH].reshape(SPEC_CH, 1)
+    mix_grad, out_grad = sum_terms(terms.reshape(512, 128))
+    mix_grad, out_grad = mix_grad.reshape(128, 1), out_grad.reshape(SPEC_CH, 1)
     return (local_out, global_out, mix_grad, out_grad)
 
 

time: 145 us -> 142 us (0.979)
  waiting for transfers between devices: 70.3 us -> 65.6 us
  Pallas kernels: 37.3 us -> 40.6 us
    pallas_call x1 -> x3, Pallas kernels: 4.09 us -> 7.44 us  [the longest x1 4.15 us: project_out(): pl.pallas_call(out_kernel, grid=(1,), in_specs=[ANY, whole_spec((SPEC_CH,...]
    all_to_all x2, waiting for transfers between devices: 61.6 us -> 58.8 us  [exchange(): lax.all_to_all(block.reshape(GROUPS, ROWS, lanes), 'rows', split_axis=0,...]
    all_to_all x1, waiting for transfers between devices: 8.71 us -> 5.99 us  [shards(): lax.all_to_all(terms, ('rows', 'img'), split_axis=0, concat_axis=0, tiled...]
    all_to_all x2, starting transfers between devices: 22 us -> 20.3 us  [exchange(): lax.all_to_all(block.reshape(GROUPS, ROWS, lanes), 'rows', split_axis=0,...]
    ppermute x2 -> x3, starting transfers between devices: 5.69 us -> 6.44 us  [the longest x1 3.53 us: neighbour_rows(): above = lax.ppermute(tail, 'rows', [(i, i + 1) for i in near])]
  transfers between devices with their start and end apart: 5 -> 6, of which waited for: 3 -> 4; matrix products, arithmetic and copies ran while one was open for 1% -> 1% of each run, Pallas kernels for 15% -> 19%
where the time goes in v5:
time: 142 us
  waiting for transfers between devices  65.6 us (46%)
  Pallas kernels  40.6 us (29%)
  starting transfers between devices  32.7 us (23%)
  local copies, waits for them, and re-layouts  1.9 us (1%)
    all_to_all x2, waiting for transfers between devices, exchange(): lax.all_to_all(block.reshape(GROUPS, ROWS, lanes), 'rows', split_axis=0,...  58.8 us
    all_to_all x2, starting transfers between devices, exchange(): lax.all_to_all(block.reshape(GROUPS, ROWS, lanes), 'rows', split_axis=0,...  20.3 us
    pallas_call x2, Pallas kernels, conv_call(): pl.pallas_call(kernel, grid=(rows,), in_specs=in_specs, out_specs=[row_sp...  11.5 us
    pallas_call x1, Pallas kernels, rows_forward(): pl.pallas_call(rows_kernel, grid=(1,), in_specs=[ANY, ANY, whole_spec((SP...  7.1 us
    all_to_all x1, waiting for transfers between devices, shards(): lax.all_to_all(terms, ('rows', 'img'), split_axis=0, concat_axis=0, tiled...  5.99 us
    all_to_all x1, starting transfers between devices, shards(): lax.all_to_all(terms, ('rows', 'img'), split_axis=0, concat_axis=0, tiled...  5.88 us
    pallas_call x1, Pallas kernels, mix_terms(): pl.pallas_call(mix_kernel, grid=(1,), in_specs=[pl.BlockSpec((1024, 512),...  5.49 us
    pallas_call x1, Pallas kernels, columns(): pl.pallas_call(columns_kernel, in_specs=[VMEM] + [ANY] * 7, out_specs=[AN...  5.29 us
  transfers between devices with their start and end apart: 6, of which 4 were waited for; matrix products, arithmetic and copies ran while one was open for 1% of the time, Pallas kernels for 19%

profile of v5, /device:TPU:1, one launch (start us, length us, event | category | flops | bytes accessed | tf_op | source)
XLA Modules:
  0.0 141.6 jit_solution(13242636866638742033)
XLA Ops:
  0.6 7.1 %shard_map.147 = (bf16[1024,1024]{1,0:T(8,128)(2,1)}, bf16[1024,512]{1,0:T(8,128)(2,1)}) custom-call(bf16[1,8,1024,128]{3,2,1,0:T(8,128)(2,1)} %maps.1, bf16[1,8,1024,128]{3,2,1,0:T(8,128)(2,1)} %cot.3, bf16[64,128]{1,0:T(8,128)(2,1)} %bitcast.16, bf16[64,128]{1,0:T(8,128)(2,1)} %out_w.3, bf16[4,256,256]{2,1,0:T(8,128)(2,1)} %constant.32.clone.table), custom_call_target="tpu_custom_call" | custom-call | flops 5000000000 | bytes 11534336 | tf_op jit(solution)/shard_map/pallas_call | solution.py:209
  7.7 14.9 %all-to-all-start = ((bf16[128,8,1024]{2,1,0:T(8,128)(2,1)}), bf16[128,8,1024]{2,1,0:T(8,128)(2,1)S(1)}, u32[]{:S(2)}, u32[]{:S(2)}) async-start(bf16[128,8,1024]{2,1,0:T(8,128)(2,1)} %bitcast.14), calls=%async_computation | async-start | bytes 4194304 | tf_op jit(solution)/shard_map/all_to_all | solution.py:814
  22.6 1.9 %fusion = (bf16[1,1,1024,128]{3,2,1,0:T(8,128)(2,1)S(1)}, bf16[1,1,1024,128]{3,2,1,0:T(8,128)(2,1)}, bf16[1,1,1024,128]{3,2,1,0:T(8,128)(2,1)S(1)}) fusion(bf16[1,8,1024,128]{3,2,1,0:T(8,128)(2,1)} %cells.1, s32[]{:T(128)S(6)} %select_n.13), kind=kLoop, calls=%fused_computation.1 | loop fusion | bytes 1572868 | tf_op jit(solution)/shard_map/slice | solution.py:731
  24.5 3.5 %collective-permute-start = (bf16[1,1,1024,128]{3,2,1,0:T(8,128)(2,1)S(1)}, bf16[1,1,1024,128]{3,2,1,0:T(8,128)(2,1)S(1)}, u32[]{:S(2)}, u32[]{:S(2)}) collective-permute-start(bf16[1,1,1024,128]{3,2,1,0:T(8,128)(2,1)S(1)} %get-tuple-element.30), channel_id=1, source_target_pairs={{0,2},{2,4},{4,6},{6,8},{8,10},{10,12},{12,14},{16,18},{18,20},{20... | collective-permute-start | bytes 786440 | tf_op jit(solution)/shard_map/ppermute | solution.py:733
  28.0 0.0 copy-start.3
  28.0 0.0 copy-start.4
  28.1 0.0 copy-start.5
  28.1 0.0 copy-start.6
  28.1 2.1 %collective-permute-start.2 = (bf16[1,1,1024,128]{3,2,1,0:T(8,128)(2,1)S(1)}, bf16[1,1,1024,128]{3,2,1,0:T(8,128)(2,1)S(1)}, u32[]{:S(2)}, u32[]{:S(2)}) collective-permute-start(bf16[1,1,1024,128]{3,2,1,0:T(8,128)(2,1)S(1)} %get-tuple-element.28), channel_id=1, source_target_pairs={{2,0},{4,2},{6,4},{8,6},{10,8},{12,10},{14,12},{18,16},{20,18},{22... | collective-permute-start | bytes 786440 | tf_op jit(solution)/shard_map/ppermute | solution.py:734
  30.1 7.8 %shard_map.148 = (bf16[1,8,1024,128]{3,2,1,0:T(8,128)(2,1)}, f32[8,128]{1,0:T(8,128)}) custom-call(bf16[1,8,1024,128]{3,2,1,0:T(8,128)(2,1)} %cells.1, bf16[1,8,1024,128]{3,2,1,0:T(8,128)(2,1)} %cells.1, bf16[1,8,1024,128]{3,2,1,0:T(8,128)(2,1)} %cells.1, bf16[3,3,128,128]{3,2,1,0:T(8,128)(2,1)} %weight_in.1, bf16[1024,1024]{1,0:T(8,128)(2,1)} %get-tuple-element.16.ready), custom_call_target="tpu_custom_call" | custom-call | flops 6000000000 | bytes 6291456 | tf_op jit(solution)/shard_map/pallas_call | solution.py:699
  37.9 0.0 collective-permute-done.above.edge_above
  37.9 0.0 copy-start.1
  37.9 0.8 collective-permute-done.2.below.edge_below
  38.7 0.0 copy-start.2
  38.7 37.8 %all-to-all-done = bf16[128,8,1024]{2,1,0:T(8,128)(2,1)S(1)} async-done(((bf16[128,8,1024]{2,1,0:T(8,128)(2,1)}), bf16[128,8,1024]{2,1,0:T(8,128)(2,1)S(1)}, u32[]{:S(2)}, u32[]{:S(2)}) %all-to-all-start) | async-done | bytes 2097184 | tf_op jit(solution)/shard_map/all_to_all | solution.py:814
  76.5 0.0 copy-start
  76.5 0.0 copy-done.3
  76.5 0.0 copy-done.4
  76.5 0.0 copy-done.5
  76.5 0.0 copy-done.6
  76.5 5.3 %shard_map.149 = (bf16[16,128,256]{2,1,0:T(8,128)(2,1)}, bf16[1024,512]{1,0:T(8,128)(2,1)}) custom-call(bf16[1024,1024]{1,0:T(8,128)(2,1)S(1)} %bitcast.9, bf16[256,256]{1,0:T(8,128)(2,1)S(1)} %copy-done.5, bf16[256,256]{1,0:T(8,128)(2,1)S(1)} %copy-done.6, f32[2,128,512]{2,1,0:T(8,128)S(1)} %copy-done.4, bf16[128,128]{1,0:T(8,128)(2,1)S(1)} %copy-done.3, ...), custom_call_target="tpu_custom_call" | custom-call | flops 8000000000 | bytes 5242880 | tf_op jit(solution)/shard_map/pallas_call | solution.py:428
  81.8 0.0 copy-done.1
  81.8 0.0 copy-done.2
  81.8 0.0 copy-done
  81.8 0.0 copy-start.7
  81.8 5.5 %all-to-all-start.1 = ((bf16[128,8,512]{2,1,0:T(8,128)(2,1)}), bf16[128,8,512]{2,1,0:T(8,128)(2,1)S(1)}, u32[]{:S(2)}, u32[]{:S(2)}) async-start(bf16[128,8,512]{2,1,0:T(8,128)(2,1)} %bitcast.13), calls=%async_computation.1 | async-start | bytes 2097152 | tf_op jit(solution)/shard_map/all_to_all | solution.py:814
  87.3 0.0 copy-done.7
  87.3 0.9 collective-permute-start.1
  88.2 3.7 %shard_map.150 = (bf16[1,8,1024,128]{3,2,1,0:T(8,128)(2,1)}, f32[8,128]{1,0:T(8,128)}) custom-call(bf16[1,8,1024,128]{3,2,1,0:T(8,128)(2,1)} %cells.1, bf16[1,8,1024,128]{3,2,1,0:T(8,128)(2,1)} %cells.1, bf16[1,1,1024,128]{3,2,1,0:T(8,128)(2,1)} %copy-done.1, bf16[1,1,1024,128]{3,2,1,0:T(8,128)(2,1)} %copy-done.2, ...), custom_call_target="tpu_custom_call", output_to_operand_aliasing={{0}: (5, {})} | custom-call | flops 2000000000 | bytes 2097152 | tf_op jit(solution)/shard_map/pallas_call | solution.py:699
  91.9 5.5 %shard_map.151.mix_part = f32[128,128]{1,0:T(8,128)} custom-call(bf16[1024,1024]{1,0:T(8,128)(2,1)} %bitcast.10, bf16[16,128,256]{2,1,0:T(8,128)(2,1)} %get-tuple-element.22.spec, bf16[256,256]{1,0:T(8,128)(2,1)} %constant.33.clone.forward_in.forward, f32[2,128,512]{2,1,0:T(8,128)} %constant.35.clone.twiddle_in.twiddle, bf16[128,128]{1,0:T(8,128)(2,1)} %mix_w.1), custom_call_target="tpu_custom_call" | custom-call | flops 6000000000 | bytes 5242880 | tf_op jit(solution)/shard_map/pallas_call | solution.py:490
  97.4 21.1 %all-to-all-done.1 = bf16[128,8,512]{2,1,0:T(8,128)(2,1)S(1)} async-done(((bf16[128,8,512]{2,1,0:T(8,128)(2,1)}), bf16[128,8,512]{2,1,0:T(8,128)(2,1)S(1)}, u32[]{:S(2)}, u32[]{:S(2)}) %all-to-all-start.1) | async-done | bytes 1048608 | tf_op jit(solution)/shard_map/all_to_all | solution.py:814
  118.5 3.7 %shard_map.152 = (bf16[1024,512]{1,0:T(8,128)(2,1)}, bf16[512,128]{1,0:T(8,128)(2,1)}) custom-call(bf16[4,256,256]{2,1,0:T(8,128)(2,1)} %constant.36.clone.table, bf16[1024,512]{1,0:T(8,128)(2,1)S(1)} %bitcast.11, bf16[1024,512]{1,0:T(8,128)(2,1)} %get-tuple-element.21.inner, bf16[1,8,1024,128]{3,2,1,0:T(8,128)(2,1)} %cot.3, ...), custom_call_target="tpu_custom_call" | custom-call | flops 2000000000 | bytes 8388608 | tf_op jit(solution)/shard_map/pallas_call | solution.py:568
  122.2 5.9 %all-to-all-start.2 = ((bf16[256,2,128]{2,1,0:T(2,128)(2,1)}), bf16[256,2,128]{2,1,0:T(2,128)(2,1)S(1)}, u32[]{:S(2)}, u32[]{:S(2)}) async-start(bf16[256,2,128]{2,1,0:T(2,128)(2,1)} %bitcast.15), calls=%async_computation.2 | async-start | bytes 262144 | tf_op jit(solution)/shard_map/all_to_all | solution.py:838
  128.1 4.2 %shard_map.154 = bf16[1,8,1024,128]{3,2,1,0:T(8,128)(2,1)} custom-call(bf16[1024,512]{1,0:T(8,128)(2,1)} %get-tuple-element.25.summed, bf16[64,128]{1,0:T(8,128)(2,1)} %out_w.3), custom_call_target="tpu_custom_call" | custom-call | flops 500000000 | bytes 3145728 | tf_op jit(solution)/shard_map/pallas_call | solution.py:616
  132.3 0.0 collective-permute-done.1.far
  132.3 2.6 %shard_map.153 = bf16[1,8,1024,128]{3,2,1,0:T(8,128)(2,1)} custom-call(bf16[1,8,1024,128]{3,2,1,0:T(8,128)(2,1)} %cells.1, bf16[1,1,1024,128]{3,2,1,0:T(8,128)(2,1)} %copy-done.1, bf16[1,1,1024,128]{3,2,1,0:T(8,128)(2,1)S(1)} %collective-permute-done.1.far, bf16[3,3,128,128]{3,2,1,0:T(8,128)(2,1)} %weight_in.1, ...), custom_call_target="tpu_custom_call", output_to_operand_aliasing={{}: (4, {})} | custom-call | flops 1000000000 | bytes 1048576 | tf_op jit(solution)/shard_map/pallas_call | solution.py:793
  134.9 6.0 %all-to-all-done.2 = bf16[256,2,128]{2,1,0:T(2,128)(2,1)S(1)} async-done(((bf16[256,2,128]{2,1,0:T(2,128)(2,1)}), bf16[256,2,128]{2,1,0:T(2,128)(2,1)S(1)}, u32[]{:S(2)}, u32[]{:S(2)}) %all-to-all-start.2) | async-done | bytes 131104 | tf_op jit(solution)/shard_map/all_to_all | solution.py:838
  140.9 0.7 shard_map.155
Async XLA Ops:
  7.7 68.7 %all-to-all-start = ((bf16[128,8,1024]{2,1,0:T(8,128)(2,1)}), bf16[128,8,1024]{2,1,0:T(8,128)(2,1)S(1)}, u32[]{:S(2)}, u32[]{:S(2)}) async-start(bf16[128,8,1024]{2,1,0:T(8,128)(2,1)} %bitcast.14), calls=%async_computation | async-start | bytes 4194304 | tf_op jit(solution)/shard_map/all_to_all | solution.py:814
  24.5 13.4 %collective-permute-start = (bf16[1,1,1024,128]{3,2,1,0:T(8,128)(2,1)S(1)}, bf16[1,1,1024,128]{3,2,1,0:T(8,128)(2,1)S(1)}, u32[]{:S(2)}, u32[]{:S(2)}) collective-permute-start(bf16[1,1,1024,128]{3,2,1,0:T(8,128)(2,1)S(1)} %get-tuple-element.30), channel_id=1, source_target_pairs={{0,2},{2,4},{4,6},{6,8},{8,10},{10,12},{12,14},{16,18},{18,20},{20... | collective-permute-start | bytes 786440 | tf_op jit(solution)/shard_map/ppermute | solution.py:733
  28.0 48.4 %copy-start.3 = (bf16[128,128]{1,0:T(8,128)(2,1)S(1)}, bf16[128,128]{1,0:T(8,128)(2,1)}, u32[]{:S(2)}) copy-start(bf16[128,128]{1,0:T(8,128)(2,1)} %mix_w.1) | copy-start | bytes 98308
  28.0 48.4 %copy-start.4 = (f32[2,128,512]{2,1,0:T(8,128)S(1)}, f32[2,128,512]{2,1,0:T(8,128)}, u32[]{:S(2)}) copy-start(f32[2,128,512]{2,1,0:T(8,128)} %constant.35.clone.twiddle_in.twiddle) | copy-start | bytes 1572868
  28.1 48.4 %copy-start.5 = (bf16[256,256]{1,0:T(8,128)(2,1)S(1)}, bf16[256,256]{1,0:T(8,128)(2,1)}, u32[]{:S(2)}) copy-start(bf16[256,256]{1,0:T(8,128)(2,1)} %constant.33.clone.forward_in.forward) | copy-start | bytes 393220
  28.1 48.4 %copy-start.6 = (bf16[256,256]{1,0:T(8,128)(2,1)S(1)}, bf16[256,256]{1,0:T(8,128)(2,1)}, u32[]{:S(2)}) copy-start(bf16[256,256]{1,0:T(8,128)(2,1)} %constant.34.clone.backward_in) | copy-start | bytes 393220
  28.1 10.6 %collective-permute-start.2 = (bf16[1,1,1024,128]{3,2,1,0:T(8,128)(2,1)S(1)}, bf16[1,1,1024,128]{3,2,1,0:T(8,128)(2,1)S(1)}, u32[]{:S(2)}, u32[]{:S(2)}) collective-permute-start(bf16[1,1,1024,128]{3,2,1,0:T(8,128)(2,1)S(1)} %get-tuple-element.28), channel_id=1, source_target_pairs={{2,0},{4,2},{6,4},{8,6},{10,8},{12,10},{14,12},{18,16},{20,18},{22... | collective-permute-start | bytes 786440 | tf_op jit(solution)/shard_map/ppermute | solution.py:734
  37.9 43.9 %copy-start.1 = (bf16[1,1,1024,128]{3,2,1,0:T(8,128)(2,1)}, bf16[1,1,1024,128]{3,2,1,0:T(8,128)(2,1)S(1)}, u32[]{:S(2)}) copy-start(bf16[1,1,1024,128]{3,2,1,0:T(8,128)(2,1)S(1)} %collective-permute-done.above.edge_above) | copy-start | bytes 786436
  38.7 43.1 %copy-start.2 = (bf16[1,1,1024,128]{3,2,1,0:T(8,128)(2,1)}, bf16[1,1,1024,128]{3,2,1,0:T(8,128)(2,1)S(1)}, u32[]{:S(2)}) copy-start(bf16[1,1,1024,128]{3,2,1,0:T(8,128)(2,1)S(1)} %collective-permute-done.2.below.edge_below) | copy-start | bytes 786436
  76.5 5.3 %copy-start = (bf16[128,8,1024]{2,1,0:T(8,128)(2,1)}, bf16[128,8,1024]{2,1,0:T(8,128)(2,1)S(1)}, u32[]{:S(2)}) copy-start(bf16[128,8,1024]{2,1,0:T(8,128)(2,1)S(1)} %all-to-all-done) | copy-start | bytes 6291460
  81.8 5.5 %copy-start.7 = (bf16[1,1,1024,128]{3,2,1,0:T(8,128)(2,1)S(1)}, bf16[1,1,1024,128]{3,2,1,0:T(8,128)(2,1)}, u32[]{:S(2)}) copy-start(bf16[1,1,1024,128]{3,2,1,0:T(8,128)(2,1)} %get-tuple-element.29) | copy-start | bytes 786436
  81.8 36.6 %all-to-all-start.1 = ((bf16[128,8,512]{2,1,0:T(8,128)(2,1)}), bf16[128,8,512]{2,1,0:T(8,128)(2,1)S(1)}, u32[]{:S(2)}, u32[]{:S(2)}) async-start(bf16[128,8,512]{2,1,0:T(8,128)(2,1)} %bitcast.13), calls=%async_computation.1 | async-start | bytes 2097152 | tf_op jit(solution)/shard_map/all_to_all | solution.py:814
  87.3 45.0 %collective-permute-start.1 = (bf16[1,1,1024,128]{3,2,1,0:T(8,128)(2,1)S(1)}, bf16[1,1,1024,128]{3,2,1,0:T(8,128)(2,1)S(1)}, u32[]{:S(2)}, u32[]{:S(2)}) collective-permute-start(bf16[1,1,1024,128]{3,2,1,0:T(8,128)(2,1)S(1)} %copy-done.7), channel_id=1, source_target_pairs={{14,16},{30,32},{46,48},{62,64},{78,80},{94,96},{110,112},{126,128... | collective-permute-start | bytes 786440 | tf_op jit(solution)/shard_map/ppermute | solution.py:742
  122.2 18.7 %all-to-all-start.2 = ((bf16[256,2,128]{2,1,0:T(2,128)(2,1)}), bf16[256,2,128]{2,1,0:T(2,128)(2,1)S(1)}, u32[]{:S(2)}, u32[]{:S(2)}) async-start(bf16[256,2,128]{2,1,0:T(2,128)(2,1)} %bitcast.15), calls=%async_computation.2 | async-start | bytes 262144 | tf_op jit(solution)/shard_map/all_to_all | solution.py:838

commit v6 on v5

--- a/solution.py
+++ b/solution.py
@@ -161,15 +161,17 @@
     out_pair[PAIR:, :] = (2.0 * dot_t(out_w[...], b)).astype(BF16)
     def project(i):
         p, n = (i % 4, i // 4)
-        loads[2 * p + n].wait()
-        if i + 8 < 8:
-            start(i + 8)
         pair = jnp.concatenate([pairs[p, n, 0], pairs[p, n, 1]], axis=1)
         part[i % 2] = dot(pair, out_pair[...] if n else in_pair[...])
 
+    for copy in loads[0::2]:
+        copy.wait()
     project(0)
     for i in range(8):
         p, n = (i % 4, i // 4)
+        if i == 3:
+            for copy in loads[1::2]:
+                copy.wait()
         if i < 7:
             project(i + 1)
         lanes = slice(n * half + p * PAIR, n * half + (p + 1) * PAIR)
@@ -337,11 +339,11 @@
 
 
 def columns_kernel(
-    block, forward_in, backward_in, twiddle_in, mix_in, ready, above, below, spec_out, back_out,
-    land, forward, backward, twiddle, mix_w, spec, stage, back, wide, prod, pre, inv, sems, out_sems,
+    block, forward_in, backward_in, twiddle_in, mix_in, above, below, spec_out, back_out,
+    land, forward, backward, twiddle, wide, spec, stage, back, prod, pre, inv, sems, out_sems,
 ):
-    del ready, above, below
-    mix_load = pltpu.make_async_copy(mix_in, mix_w, sems.at[4])
+    del above, below
+    mix_load = pltpu.make_async_copy(mix_in, wide, sems.at[4])
     forward_load = pltpu.make_async_copy(forward_in, forward, sems.at[5])
     twiddle_load = pltpu.make_async_copy(twiddle_in, twiddle, sems.at[6])
     backward_load = pltpu.make_async_copy(backward_in, backward, sems.at[7])
@@ -350,7 +352,6 @@
     for m in range(4):
         stage[m] = block[:, m * PAIR : (m + 1) * PAIR].astype(F32)
     mix_load.wait()
-    fill_mix(mix_w, wide)
     forward_load.wait()
     twiddle_load.wait()
     backward_load.wait()
@@ -424,10 +425,10 @@
     return pl.BlockSpec(shape, lambda *_: (0,) * len(shape))
 
 
-def columns(block, forward, backward, twiddle, mix_w, ready, above, below):
+def columns(block, forward, backward, twiddle, wide, above, below):
     return pl.pallas_call(
         columns_kernel,
-        in_specs=[VMEM] + [ANY] * 7,
+        in_specs=[VMEM] + [ANY] * 6,
         out_specs=[ANY, ANY],
         out_shape=[
             pltpu.HBM((16, GROUPS, 256), BF16),
@@ -438,11 +439,10 @@
             pltpu.VMEM((256, 256), BF16),
             pltpu.VMEM((256, 256), BF16),
             pltpu.VMEM((2, GROUPS, 512), F32),
-            pltpu.VMEM((128, 128), BF16),
+            pltpu.VMEM((256, 256), BF16),
             pltpu.VMEM((16, GROUPS, 256), BF16),
             pltpu.VMEM((4, 1024, PAIR), F32),
             pltpu.VMEM((4, 1024, PAIR), F32),
-            pltpu.VMEM((256, 256), BF16),
             pltpu.VMEM((2, 256, 512), F32),
             pltpu.VMEM((2, 512, 256), F32),
             pltpu.VMEM((2, 256, 512), BF16),
@@ -451,11 +451,10 @@
         ],
         compiler_params=params(SMALL),
         cost_estimate=cost(8 * 10**9, 5 * 2**20),
-    )(block, forward, backward, twiddle, mix_w, in_hbm(ready), above, below)
-
-
-def mix_kernel(block, spec, forward, twiddle, mix_w, grad, stage, wide, prod, pre, slope, acc):
-    fill_mix(mix_w, wide)
+    )(block, forward, backward, twiddle, wide, above, below)
+
+
+def mix_kernel(block, spec, forward, twiddle, wide, grad, stage, prod, pre, slope, acc):
     fill_stage(block, stage)
     signs = lane_signs((RB, PAIR))
     first = iota((RB, PAIR), 1) < SPEC_CH
@@ -486,7 +485,7 @@
         grad[part * SPEC_CH : (part + 1) * SPEC_CH, :] = jnp.where(lane, real, imag)
 
 
-def mix_terms(block, spec, forward, twiddle, mix_w):
+def mix_terms(block, spec, forward, twiddle, wide):
     return pl.pallas_call(
         mix_kernel,
         grid=(1,),
@@ -495,13 +494,12 @@
             whole_spec((16, GROUPS, 256)),
             whole_spec((256, 256)),
             whole_spec((2, GROUPS, 512)),
-            whole_spec((128, 128)),
+            whole_spec((256, 256)),
         ],
         out_specs=whole_spec((128, 128)),
         out_shape=jax.ShapeDtypeStruct((128, 128), F32),
         scratch_shapes=[
             pltpu.VMEM((4, 1024, PAIR), F32),
-            pltpu.VMEM((256, 256), BF16),
             pltpu.VMEM((256, 512), F32),
             pltpu.VMEM((512, 256), F32),
             pltpu.VMEM((512, 256), BF16),
@@ -509,7 +507,7 @@
         ],
         compiler_params=params(),
         cost_estimate=cost(6 * 10**9, 5 * 2**20),
-    )(block, spec, forward, twiddle, mix_w)
+    )(block, spec, forward, twiddle, wide)
 
 
 def back_kernel(
@@ -647,26 +645,32 @@
     return total.astype(BF16)
 
 
-def conv_row(top, mid, bottom, weight, out, token, sums, wide):
+def conv_row(top, mid, bottom, weight, out, sums, wide):
     @pl.when(pl.program_id(0) == 0)
     def _():
-        token[...] = jnp.zeros((8, 128), F32)
         fill_wide(weight, wide, sums)
 
     out[0, 0] = conv_sums(top, mid, bottom, sums, wide)
 
 
-def inner_kernel(above, mid, below, weight, ready, out, token, sums, wide):
+def inner_kernel(above, mid, below, weight, mix_w, ready, out, mix, sums, wide):
     del ready
-    conv_row(above[0, 0], mid[0, 0], below[0, 0], weight, out, token, sums, wide)
-
-
-def edge_kernel(mid, beside, edge_above, edge_below, weight, done, ready, out, token, sums, wide):
+    conv_row(above[0, 0], mid[0, 0], below[0, 0], weight, out, sums, wide)
+
+    @pl.when(pl.program_id(0) == 0)
+    def _():
+        fill_mix(mix_w, mix)
+
+
+def edge_kernel(
+    mid, beside, edge_above, edge_below, weight, done, ready, out, token, sums, wide
+):
     del done, ready
+    token[...] = jnp.zeros((8, 128), F32)
     first = pl.program_id(0) == 0
     top = jnp.where(first, edge_above[0, 0], beside[0, 0])
     bottom = jnp.where(first, beside[0, 0], edge_below[0, 0])
-    conv_row(top, mid[0, 0], bottom, weight, out, token, sums, wide)
+    conv_row(top, mid[0, 0], bottom, weight, out, sums, wide)
 
 
 def sum_kernel(terms, mix, out):
@@ -695,15 +699,15 @@
     return pl.BlockSpec((1, 1, WIDTH, 128), lambda i: (0, index(i), 0, 0))
 
 
-def conv_call(kernel, rows, in_specs, out_index, aliases, args):
+def conv_call(kernel, rows, in_specs, out_index, second, aliases, args):
     return pl.pallas_call(
         kernel,
         grid=(rows,),
         in_specs=in_specs,
-        out_specs=[row_spec(out_index), whole_spec((8, 128))],
+        out_specs=[row_spec(out_index), whole_spec(second.shape)],
         out_shape=[
             pltpu.HBM((1, ROWS, WIDTH, 128), BF16),
-            jax.ShapeDtypeStruct((8, 128), F32),
+            second,
         ],
         scratch_shapes=[pltpu.VMEM((3, WIDTH + 16, 128), F32), pltpu.VMEM((384, 384), BF16)],
         input_output_aliases=aliases,
@@ -712,16 +716,18 @@
     )(*args)
 
 
-def inner_rows(cells, weight, ready):
+def inner_rows(cells, weight, mix_w, ready):
     specs = [
         row_spec(lambda i: i),
         row_spec(lambda i: i + 1),
         row_spec(lambda i: i + 2),
         whole_spec((3, 3, 128, 128)),
+        whole_spec((128, 128)),
         pl.BlockSpec(memory_space=pl.ANY),
     ]
-    args = (cells, cells, cells, weight, ready)
-    return conv_call(inner_kernel, ROWS - 2, specs, lambda i: i + 1, {}, args)
+    args = (cells, cells, cells, weight, mix_w, ready)
+    second = jax.ShapeDtypeStruct((256, 256), BF16)
+    return conv_call(inner_kernel, ROWS - 2, specs, lambda i: i + 1, second, {}, args)
 
 
 BLOCK = 8
@@ -753,7 +759,8 @@
         pl.BlockSpec(memory_space=pl.ANY),
     ]
     args = (cells, cells, above, below, weight, done, ready)
-    return conv_call(edge_kernel, 2, specs, lambda i: i * (ROWS - 1), {5: 0}, args)
+    second = jax.ShapeDtypeStruct((8, 128), F32)
+    return conv_call(edge_kernel, 2, specs, lambda i: i * (ROWS - 1), second, {5: 0}, args)
 
 
 def far_kernel(cells, above, far, weight_in, done, ready, out, lines, weight, row_out, sums, wide, sems):
@@ -822,13 +829,13 @@
     forward, backward, twiddle = column_tables()
     spec_rows, inner = rows_forward(global_maps, out_cotangent, in_weight.T, out_weight, row_fwd)
     spec_cols = exchange(spec_rows)
-    local_inner, token = inner_rows(local_maps, conv_weight, spec_rows)
+    local_inner, wide = inner_rows(local_maps, conv_weight, mix_weight, spec_rows)
     above, below = neighbour_rows(local_maps)
     spectrum, back_cols = columns(
-        spec_cols, forward, backward, twiddle, mix_weight, token, above, below
+        spec_cols, forward, backward, twiddle, wide, above, below
     )
     back = exchange(back_cols)
-    mix_part = mix_terms(spec_cols, spectrum, forward, twiddle, mix_weight)
+    mix_part = mix_terms(spec_cols, spectrum, forward, twiddle, wide)
     local_out, token = edge_rows(local_maps, above, below, conv_weight, local_inner, back_cols)
     summed, terms = back_rows(row_inv, back, inner, out_cotangent, mix_part, token)
     local_out = far_edge(

time: 142 us -> 142 us (level)
  transfers between devices with their start and end apart: 6 -> 6, of which waited for: 4 -> 4; matrix products, arithmetic and copies ran while one was open for 1% -> 1% of each run, Pallas kernels for 19% -> 20%
where the time goes in v6:
time: 142 us; the launch traced here: 141 us
  waiting for transfers between devices  65.3 us (46%)
  Pallas kernels  39.2 us (28%)
  starting transfers between devices  32.7 us (23%)
  local copies, waits for them, and re-layouts  2.93 us (2%)
    all_to_all x2, waiting for transfers between devices, exchange(): lax.all_to_all(block.reshape(GROUPS, ROWS, lanes), 'rows', split_axis=0,...  58.9 us
    all_to_all x2, starting transfers between devices, exchange(): lax.all_to_all(block.reshape(GROUPS, ROWS, lanes), 'rows', split_axis=0,...  20.3 us
    pallas_call x2, Pallas kernels, conv_call(): pl.pallas_call(kernel, grid=(rows,), in_specs=in_specs, out_specs=[row_sp...  11.9 us
    all_to_all x1, waiting for transfers between devices, shards(): lax.all_to_all(terms, ('rows', 'img'), split_axis=0, concat_axis=0, tiled...  5.99 us
    all_to_all x1, starting transfers between devices, shards(): lax.all_to_all(terms, ('rows', 'img'), split_axis=0, concat_axis=0, tiled...  5.88 us
    pallas_call x1, Pallas kernels, rows_forward(): pl.pallas_call(rows_kernel, grid=(1,), in_specs=[ANY, ANY, whole_spec((SP...  5.74 us
    pallas_call x1, Pallas kernels, mix_terms(): pl.pallas_call(mix_kernel, grid=(1,), in_specs=[pl.BlockSpec((1024, 512),...  5.44 us
    pallas_call x1, Pallas kernels, columns(): pl.pallas_call(columns_kernel, in_specs=[VMEM] + [ANY] * 6, out_specs=[AN...  4.94 us
  transfers between devices with their start and end apart: 6, of which 4 were waited for; matrix products, arithmetic and copies ran while one was open for 1% of the time, Pallas kernels for 20%

profile of v6, /device:TPU:1, one launch (start us, length us, event | category | flops | bytes accessed | tf_op | source)
XLA Modules:
  0.0 140.9 jit_solution(16972935856559950922)
XLA Ops:
  0.6 5.7 %shard_map.147 = (bf16[1024,1024]{1,0:T(8,128)(2,1)}, bf16[1024,512]{1,0:T(8,128)(2,1)}) custom-call(bf16[1,8,1024,128]{3,2,1,0:T(8,128)(2,1)} %maps.1, bf16[1,8,1024,128]{3,2,1,0:T(8,128)(2,1)} %cot.3, bf16[64,128]{1,0:T(8,128)(2,1)} %bitcast.16, bf16[64,128]{1,0:T(8,128)(2,1)} %out_w.3, bf16[4,256,256]{2,1,0:T(8,128)(2,1)} %constant.32.clone.table), custom_call_target="tpu_custom_call" | custom-call | flops 5000000000 | bytes 11534336 | tf_op jit(solution)/shard_map/pallas_call | solution.py:211
  6.4 14.9 %all-to-all-start = ((bf16[128,8,1024]{2,1,0:T(8,128)(2,1)}), bf16[128,8,1024]{2,1,0:T(8,128)(2,1)S(1)}, u32[]{:S(2)}, u32[]{:S(2)}) async-start(bf16[128,8,1024]{2,1,0:T(8,128)(2,1)} %bitcast.14), calls=%async_computation | async-start | bytes 4194304 | tf_op jit(solution)/shard_map/all_to_all | solution.py:821
  21.3 1.9 %fusion = (bf16[1,1,1024,128]{3,2,1,0:T(8,128)(2,1)S(1)}, bf16[1,1,1024,128]{3,2,1,0:T(8,128)(2,1)}, bf16[1,1,1024,128]{3,2,1,0:T(8,128)(2,1)S(1)}) fusion(bf16[1,8,1024,128]{3,2,1,0:T(8,128)(2,1)} %cells.1, s32[]{:T(128)S(6)} %select_n.13), kind=kLoop, calls=%fused_computation.1 | loop fusion | bytes 1572868 | tf_op jit(solution)/shard_map/slice | solution.py:737
  23.1 3.5 %collective-permute-start = (bf16[1,1,1024,128]{3,2,1,0:T(8,128)(2,1)S(1)}, bf16[1,1,1024,128]{3,2,1,0:T(8,128)(2,1)S(1)}, u32[]{:S(2)}, u32[]{:S(2)}) collective-permute-start(bf16[1,1,1024,128]{3,2,1,0:T(8,128)(2,1)S(1)} %get-tuple-element.30), channel_id=1, source_target_pairs={{0,2},{2,4},{4,6},{6,8},{8,10},{10,12},{12,14},{16,18},{18,20},{20... | collective-permute-start | bytes 786440 | tf_op jit(solution)/shard_map/ppermute | solution.py:739
  26.7 0.0 copy-start.3
  26.7 0.0 copy-start.4
  26.7 0.0 copy-start.5
  26.7 2.1 %collective-permute-start.2 = (bf16[1,1,1024,128]{3,2,1,0:T(8,128)(2,1)S(1)}, bf16[1,1,1024,128]{3,2,1,0:T(8,128)(2,1)S(1)}, u32[]{:S(2)}, u32[]{:S(2)}) collective-permute-start(bf16[1,1,1024,128]{3,2,1,0:T(8,128)(2,1)S(1)} %get-tuple-element.28), channel_id=1, source_target_pairs={{2,0},{4,2},{6,4},{8,6},{10,8},{12,10},{14,12},{18,16},{20,18},{22... | collective-permute-start | bytes 786440 | tf_op jit(solution)/shard_map/ppermute | solution.py:740
  28.8 8.2 %shard_map.148 = (bf16[1,8,1024,128]{3,2,1,0:T(8,128)(2,1)}, bf16[256,256]{1,0:T(8,128)(2,1)}) custom-call(bf16[1,8,1024,128]{3,2,1,0:T(8,128)(2,1)} %cells.1, bf16[1,8,1024,128]{3,2,1,0:T(8,128)(2,1)} %cells.1, bf16[1,8,1024,128]{3,2,1,0:T(8,128)(2,1)} %cells.1, bf16[3,3,128,128]{3,2,1,0:T(8,128)(2,1)} %weight_in.1, bf16[128,128]{1,0:T(8,128)(2,1)} %mix_w.1, ...), custom_call_target="tpu_custom_call" | custom-call | flops 6000000000 | bytes 6291456 | tf_op jit(solution)/shard_map/pallas_call | solution.py:703
  36.9 0.0 collective-permute-done.above.edge_above
  36.9 0.0 copy-start.1
  36.9 0.4 collective-permute-done.2.below.edge_below
  37.3 0.0 copy-start.2
  37.3 37.8 %all-to-all-done = bf16[128,8,1024]{2,1,0:T(8,128)(2,1)S(1)} async-done(((bf16[128,8,1024]{2,1,0:T(8,128)(2,1)}), bf16[128,8,1024]{2,1,0:T(8,128)(2,1)S(1)}, u32[]{:S(2)}, u32[]{:S(2)}) %all-to-all-start) | async-done | bytes 2097184 | tf_op jit(solution)/shard_map/all_to_all | solution.py:821
  75.1 0.0 copy-start
  75.1 0.0 copy-done.3
  75.1 0.0 copy-done.4
  75.1 0.0 copy-done.5
  75.1 0.0 copy-start.6
  75.1 1.0 copy-done.6
  76.2 4.9 %shard_map.149 = (bf16[16,128,256]{2,1,0:T(8,128)(2,1)}, bf16[1024,512]{1,0:T(8,128)(2,1)}) custom-call(bf16[1024,1024]{1,0:T(8,128)(2,1)S(1)} %bitcast.9, bf16[256,256]{1,0:T(8,128)(2,1)S(1)} %copy-done.4, bf16[256,256]{1,0:T(8,128)(2,1)S(1)} %copy-done.5, f32[2,128,512]{2,1,0:T(8,128)S(1)} %copy-done.3, bf16[256,256]{1,0:T(8,128)(2,1)S(1)} %copy-done.6, ...), custom_call_target="tpu_custom_call" | custom-call | flops 8000000000 | bytes 5242880 | tf_op jit(solution)/shard_map/pallas_call | solution.py:429
  81.1 0.0 copy-done.1
  81.1 0.0 copy-done.2
  81.1 0.0 copy-done
  81.1 0.0 copy-start.7
  81.1 5.5 %all-to-all-start.1 = ((bf16[128,8,512]{2,1,0:T(8,128)(2,1)}), bf16[128,8,512]{2,1,0:T(8,128)(2,1)S(1)}, u32[]{:S(2)}, u32[]{:S(2)}) async-start(bf16[128,8,512]{2,1,0:T(8,128)(2,1)} %bitcast.13), calls=%async_computation.1 | async-start | bytes 2097152 | tf_op jit(solution)/shard_map/all_to_all | solution.py:821
  86.6 0.0 copy-done.7
  86.6 0.9 collective-permute-start.1
  87.5 3.8 %shard_map.150 = (bf16[1,8,1024,128]{3,2,1,0:T(8,128)(2,1)}, f32[8,128]{1,0:T(8,128)}) custom-call(bf16[1,8,1024,128]{3,2,1,0:T(8,128)(2,1)} %cells.1, bf16[1,8,1024,128]{3,2,1,0:T(8,128)(2,1)} %cells.1, bf16[1,1,1024,128]{3,2,1,0:T(8,128)(2,1)} %copy-done.1, bf16[1,1,1024,128]{3,2,1,0:T(8,128)(2,1)} %copy-done.2, ...), custom_call_target="tpu_custom_call", output_to_operand_aliasing={{0}: (5, {})} | custom-call | flops 2000000000 | bytes 2097152 | tf_op jit(solution)/shard_map/pallas_call | solution.py:703
  91.2 5.4 %shard_map.151.mix_part = f32[128,128]{1,0:T(8,128)} custom-call(bf16[1024,1024]{1,0:T(8,128)(2,1)} %bitcast.10, bf16[16,128,256]{2,1,0:T(8,128)(2,1)} %get-tuple-element.22.spec, bf16[256,256]{1,0:T(8,128)(2,1)} %constant.33.clone.forward_in.forward, f32[2,128,512]{2,1,0:T(8,128)} %constant.35.clone.twiddle_in.twiddle, ...), custom_call_target="tpu_custom_call" | custom-call | flops 6000000000 | bytes 5242880 | tf_op jit(solution)/shard_map/pallas_call | solution.py:489
  96.7 21.1 %all-to-all-done.1 = bf16[128,8,512]{2,1,0:T(8,128)(2,1)S(1)} async-done(((bf16[128,8,512]{2,1,0:T(8,128)(2,1)}), bf16[128,8,512]{2,1,0:T(8,128)(2,1)S(1)}, u32[]{:S(2)}, u32[]{:S(2)}) %all-to-all-start.1) | async-done | bytes 1048608 | tf_op jit(solution)/shard_map/all_to_all | solution.py:821
  117.8 3.7 %shard_map.152 = (bf16[1024,512]{1,0:T(8,128)(2,1)}, bf16[512,128]{1,0:T(8,128)(2,1)}) custom-call(bf16[4,256,256]{2,1,0:T(8,128)(2,1)} %constant.36.clone.table, bf16[1024,512]{1,0:T(8,128)(2,1)S(1)} %bitcast.11, bf16[1024,512]{1,0:T(8,128)(2,1)} %get-tuple-element.21.inner, bf16[1,8,1024,128]{3,2,1,0:T(8,128)(2,1)} %cot.3, ...), custom_call_target="tpu_custom_call" | custom-call | flops 2000000000 | bytes 8388608 | tf_op jit(solution)/shard_map/pallas_call | solution.py:566
  121.5 5.9 %all-to-all-start.2 = ((bf16[256,2,128]{2,1,0:T(2,128)(2,1)}), bf16[256,2,128]{2,1,0:T(2,128)(2,1)S(1)}, u32[]{:S(2)}, u32[]{:S(2)}) async-start(bf16[256,2,128]{2,1,0:T(2,128)(2,1)} %bitcast.15), calls=%async_computation.2 | async-start | bytes 262144 | tf_op jit(solution)/shard_map/all_to_all | solution.py:845
  127.4 4.1 %shard_map.154 = bf16[1,8,1024,128]{3,2,1,0:T(8,128)(2,1)} custom-call(bf16[1024,512]{1,0:T(8,128)(2,1)} %get-tuple-element.25.summed, bf16[64,128]{1,0:T(8,128)(2,1)} %out_w.3), custom_call_target="tpu_custom_call" | custom-call | flops 500000000 | bytes 3145728 | tf_op jit(solution)/shard_map/pallas_call | solution.py:614
  131.6 0.0 collective-permute-done.1.far
  131.6 2.6 %shard_map.153 = bf16[1,8,1024,128]{3,2,1,0:T(8,128)(2,1)} custom-call(bf16[1,8,1024,128]{3,2,1,0:T(8,128)(2,1)} %cells.1, bf16[1,1,1024,128]{3,2,1,0:T(8,128)(2,1)} %copy-done.1, bf16[1,1,1024,128]{3,2,1,0:T(8,128)(2,1)S(1)} %collective-permute-done.1.far, bf16[3,3,128,128]{3,2,1,0:T(8,128)(2,1)} %weight_in.1, ...), custom_call_target="tpu_custom_call", output_to_operand_aliasing={{}: (4, {})} | custom-call | flops 1000000000 | bytes 1048576 | tf_op jit(solution)/shard_map/pallas_call | solution.py:800
  134.2 6.0 %all-to-all-done.2 = bf16[256,2,128]{2,1,0:T(2,128)(2,1)S(1)} async-done(((bf16[256,2,128]{2,1,0:T(2,128)(2,1)}), bf16[256,2,128]{2,1,0:T(2,128)(2,1)S(1)}, u32[]{:S(2)}, u32[]{:S(2)}) %all-to-all-start.2) | async-done | bytes 131104 | tf_op jit(solution)/shard_map/all_to_all | solution.py:845
  140.2 0.7 shard_map.155
Async XLA Ops:
  6.4 68.7 %all-to-all-start = ((bf16[128,8,1024]{2,1,0:T(8,128)(2,1)}), bf16[128,8,1024]{2,1,0:T(8,128)(2,1)S(1)}, u32[]{:S(2)}, u32[]{:S(2)}) async-start(bf16[128,8,1024]{2,1,0:T(8,128)(2,1)} %bitcast.14), calls=%async_computation | async-start | bytes 4194304 | tf_op jit(solution)/shard_map/all_to_all | solution.py:821
  23.1 13.8 %collective-permute-start = (bf16[1,1,1024,128]{3,2,1,0:T(8,128)(2,1)S(1)}, bf16[1,1,1024,128]{3,2,1,0:T(8,128)(2,1)S(1)}, u32[]{:S(2)}, u32[]{:S(2)}) collective-permute-start(bf16[1,1,1024,128]{3,2,1,0:T(8,128)(2,1)S(1)} %get-tuple-element.30), channel_id=1, source_target_pairs={{0,2},{2,4},{4,6},{6,8},{8,10},{10,12},{12,14},{16,18},{18,20},{20... | collective-permute-start | bytes 786440 | tf_op jit(solution)/shard_map/ppermute | solution.py:739
  26.7 48.4 %copy-start.3 = (f32[2,128,512]{2,1,0:T(8,128)S(1)}, f32[2,128,512]{2,1,0:T(8,128)}, u32[]{:S(2)}) copy-start(f32[2,128,512]{2,1,0:T(8,128)} %constant.35.clone.twiddle_in.twiddle) | copy-start | bytes 1572868
  26.7 48.4 %copy-start.4 = (bf16[256,256]{1,0:T(8,128)(2,1)S(1)}, bf16[256,256]{1,0:T(8,128)(2,1)}, u32[]{:S(2)}) copy-start(bf16[256,256]{1,0:T(8,128)(2,1)} %constant.33.clone.forward_in.forward) | copy-start | bytes 393220
  26.7 48.4 %copy-start.5 = (bf16[256,256]{1,0:T(8,128)(2,1)S(1)}, bf16[256,256]{1,0:T(8,128)(2,1)}, u32[]{:S(2)}) copy-start(bf16[256,256]{1,0:T(8,128)(2,1)} %constant.34.clone.backward_in) | copy-start | bytes 393220
  26.7 10.6 %collective-permute-start.2 = (bf16[1,1,1024,128]{3,2,1,0:T(8,128)(2,1)S(1)}, bf16[1,1,1024,128]{3,2,1,0:T(8,128)(2,1)S(1)}, u32[]{:S(2)}, u32[]{:S(2)}) collective-permute-start(bf16[1,1,1024,128]{3,2,1,0:T(8,128)(2,1)S(1)} %get-tuple-element.28), channel_id=1, source_target_pairs={{2,0},{4,2},{6,4},{8,6},{10,8},{12,10},{14,12},{18,16},{20,18},{22... | collective-permute-start | bytes 786440 | tf_op jit(solution)/shard_map/ppermute | solution.py:740
  36.9 44.2 %copy-start.1 = (bf16[1,1,1024,128]{3,2,1,0:T(8,128)(2,1)}, bf16[1,1,1024,128]{3,2,1,0:T(8,128)(2,1)S(1)}, u32[]{:S(2)}) copy-start(bf16[1,1,1024,128]{3,2,1,0:T(8,128)(2,1)S(1)} %collective-permute-done.above.edge_above) | copy-start | bytes 786436
  37.3 43.8 %copy-start.2 = (bf16[1,1,1024,128]{3,2,1,0:T(8,128)(2,1)}, bf16[1,1,1024,128]{3,2,1,0:T(8,128)(2,1)S(1)}, u32[]{:S(2)}) copy-start(bf16[1,1,1024,128]{3,2,1,0:T(8,128)(2,1)S(1)} %collective-permute-done.2.below.edge_below) | copy-start | bytes 786436
  75.1 6.0 %copy-start = (bf16[128,8,1024]{2,1,0:T(8,128)(2,1)}, bf16[128,8,1024]{2,1,0:T(8,128)(2,1)S(1)}, u32[]{:S(2)}) copy-start(bf16[128,8,1024]{2,1,0:T(8,128)(2,1)S(1)} %all-to-all-done) | copy-start | bytes 6291460
  75.1 1.0 copy-start.6
  81.1 5.5 %copy-start.7 = (bf16[1,1,1024,128]{3,2,1,0:T(8,128)(2,1)S(1)}, bf16[1,1,1024,128]{3,2,1,0:T(8,128)(2,1)}, u32[]{:S(2)}) copy-start(bf16[1,1,1024,128]{3,2,1,0:T(8,128)(2,1)} %get-tuple-element.29) | copy-start | bytes 786436
  81.1 36.6 %all-to-all-start.1 = ((bf16[128,8,512]{2,1,0:T(8,128)(2,1)}), bf16[128,8,512]{2,1,0:T(8,128)(2,1)S(1)}, u32[]{:S(2)}, u32[]{:S(2)}) async-start(bf16[128,8,512]{2,1,0:T(8,128)(2,1)} %bitcast.13), calls=%async_computation.1 | async-start | bytes 2097152 | tf_op jit(solution)/shard_map/all_to_all | solution.py:821
  86.6 45.0 %collective-permute-start.1 = (bf16[1,1,1024,128]{3,2,1,0:T(8,128)(2,1)S(1)}, bf16[1,1,1024,128]{3,2,1,0:T(8,128)(2,1)S(1)}, u32[]{:S(2)}, u32[]{:S(2)}) collective-permute-start(bf16[1,1,1024,128]{3,2,1,0:T(8,128)(2,1)S(1)} %copy-done.7), channel_id=1, source_target_pairs={{14,16},{30,32},{46,48},{62,64},{78,80},{94,96},{110,112},{126,128... | collective-permute-start | bytes 786440 | tf_op jit(solution)/shard_map/ppermute | solution.py:748
  121.5 18.7 %all-to-all-start.2 = ((bf16[256,2,128]{2,1,0:T(2,128)(2,1)}), bf16[256,2,128]{2,1,0:T(2,128)(2,1)S(1)}, u32[]{:S(2)}, u32[]{:S(2)}) async-start(bf16[256,2,128]{2,1,0:T(2,128)(2,1)} %bitcast.15), calls=%async_computation.2 | async-start | bytes 262144 | tf_op jit(solution)/shard_map/all_to_all | solution.py:845

commit v7 on v6

--- a/solution.py
+++ b/solution.py
@@ -170,7 +170,7 @@
     for i in range(8):
         p, n = (i % 4, i // 4)
         if i == 3:
-            for copy in loads[1::2]:
+            for copy in loads[1::2] + [table_load]:
                 copy.wait()
         if i < 7:
             project(i + 1)
@@ -190,7 +190,6 @@
 
     stores = [pltpu.make_async_copy(inner, inner_out, out_sems.at[4])]
     stores[0].start()
-    table_load.wait()
     for b in range(4):
         rows = pl.ds(b * 256, 256)
         prod = dot(held[b], eights[b])
@@ -451,7 +450,7 @@
         ],
         compiler_params=params(SMALL),
         cost_estimate=cost(8 * 10**9, 5 * 2**20),
-    )(block, forward, backward, twiddle, wide, above, below)
+    )(block, forward, backward, twiddle, in_hbm(wide), above, below)
 
 
 def mix_kernel(block, spec, forward, twiddle, wide, grad, stage, prod, pre, slope, acc):

time: 142 us -> 141 us (level)
  no operation moved by 1% of the time
where the time goes in v7:
time: 141 us; the launch traced here: 140 us
  waiting for transfers between devices  65.2 us (46%)
  Pallas kernels  39.5 us (28%)
  starting transfers between devices  32.7 us (23%)
  local copies, waits for them, and re-layouts  1.9 us (1%)
    all_to_all x2, waiting for transfers between devices, exchange(): lax.all_to_all(block.reshape(GROUPS, ROWS, lanes), 'rows', split_axis=0,...  58.9 us
    all_to_all x2, starting transfers between devices, exchange(): lax.all_to_all(block.reshape(GROUPS, ROWS, lanes), 'rows', split_axis=0,...  20.3 us
    pallas_call x2, Pallas kernels, conv_call(): pl.pallas_call(kernel, grid=(rows,), in_specs=in_specs, out_specs=[row_sp...  11.9 us
    all_to_all x1, waiting for transfers between devices, shards(): lax.all_to_all(terms, ('rows', 'img'), split_axis=0, concat_axis=0, tiled...  5.99 us
    all_to_all x1, starting transfers between devices, shards(): lax.all_to_all(terms, ('rows', 'img'), split_axis=0, concat_axis=0, tiled...  5.88 us
    pallas_call x1, Pallas kernels, rows_forward(): pl.pallas_call(rows_kernel, grid=(1,), in_specs=[ANY, ANY, whole_spec((SP...  5.59 us
    pallas_call x1, Pallas kernels, mix_terms(): pl.pallas_call(mix_kernel, grid=(1,), in_specs=[pl.BlockSpec((1024, 512),...  5.45 us
    pallas_call x1, Pallas kernels, columns(): pl.pallas_call(columns_kernel, in_specs=[VMEM] + [ANY] * 6, out_specs=[AN...  5.33 us
  transfers between devices with their start and end apart: 6, of which 4 were waited for; matrix products, arithmetic and copies ran while one was open for 1% of the time, Pallas kernels for 20%

profile of v7, /device:TPU:1, one launch (start us, length us, event | category | flops | bytes accessed | tf_op | source)
XLA Modules:
  0.0 140.1 jit_solution(14623430020628876613)
XLA Ops:
  0.6 5.6 %shard_map.147 = (bf16[1024,1024]{1,0:T(8,128)(2,1)}, bf16[1024,512]{1,0:T(8,128)(2,1)}) custom-call(bf16[1,8,1024,128]{3,2,1,0:T(8,128)(2,1)} %maps.1, bf16[1,8,1024,128]{3,2,1,0:T(8,128)(2,1)} %cot.3, bf16[64,128]{1,0:T(8,128)(2,1)} %bitcast.16, bf16[64,128]{1,0:T(8,128)(2,1)} %out_w.3, bf16[4,256,256]{2,1,0:T(8,128)(2,1)} %constant.32.clone.table), custom_call_target="tpu_custom_call" | custom-call | flops 5000000000 | bytes 11534336 | tf_op jit(solution)/shard_map/pallas_call | solution.py:210
  6.2 14.9 %all-to-all-start = ((bf16[128,8,1024]{2,1,0:T(8,128)(2,1)}), bf16[128,8,1024]{2,1,0:T(8,128)(2,1)S(1)}, u32[]{:S(2)}, u32[]{:S(2)}) async-start(bf16[128,8,1024]{2,1,0:T(8,128)(2,1)} %bitcast.14), calls=%async_computation | async-start | bytes 4194304 | tf_op jit(solution)/shard_map/all_to_all | solution.py:820
  21.1 1.9 %fusion = (bf16[1,1,1024,128]{3,2,1,0:T(8,128)(2,1)S(1)}, bf16[1,1,1024,128]{3,2,1,0:T(8,128)(2,1)}, bf16[1,1,1024,128]{3,2,1,0:T(8,128)(2,1)S(1)}) fusion(bf16[1,8,1024,128]{3,2,1,0:T(8,128)(2,1)} %cells.1, s32[]{:T(128)S(6)} %select_n.13), kind=kLoop, calls=%fused_computation.1 | loop fusion | bytes 1572868 | tf_op jit(solution)/shard_map/slice | solution.py:736
  23.0 3.5 %collective-permute-start = (bf16[1,1,1024,128]{3,2,1,0:T(8,128)(2,1)S(1)}, bf16[1,1,1024,128]{3,2,1,0:T(8,128)(2,1)S(1)}, u32[]{:S(2)}, u32[]{:S(2)}) collective-permute-start(bf16[1,1,1024,128]{3,2,1,0:T(8,128)(2,1)S(1)} %get-tuple-element.30), channel_id=1, source_target_pairs={{0,2},{2,4},{4,6},{6,8},{8,10},{10,12},{12,14},{16,18},{18,20},{20... | collective-permute-start | bytes 786440 | tf_op jit(solution)/shard_map/ppermute | solution.py:738
  26.5 0.0 copy-start.3
  26.5 0.0 copy-start.4
  26.6 0.0 copy-start.5
  26.6 2.1 %collective-permute-start.2 = (bf16[1,1,1024,128]{3,2,1,0:T(8,128)(2,1)S(1)}, bf16[1,1,1024,128]{3,2,1,0:T(8,128)(2,1)S(1)}, u32[]{:S(2)}, u32[]{:S(2)}) collective-permute-start(bf16[1,1,1024,128]{3,2,1,0:T(8,128)(2,1)S(1)} %get-tuple-element.28), channel_id=1, source_target_pairs={{2,0},{4,2},{6,4},{8,6},{10,8},{12,10},{14,12},{18,16},{20,18},{22... | collective-permute-start | bytes 786440 | tf_op jit(solution)/shard_map/ppermute | solution.py:739
  28.6 8.2 %shard_map.148 = (bf16[1,8,1024,128]{3,2,1,0:T(8,128)(2,1)}, bf16[256,256]{1,0:T(8,128)(2,1)}) custom-call(bf16[1,8,1024,128]{3,2,1,0:T(8,128)(2,1)} %cells.1, bf16[1,8,1024,128]{3,2,1,0:T(8,128)(2,1)} %cells.1, bf16[1,8,1024,128]{3,2,1,0:T(8,128)(2,1)} %cells.1, bf16[3,3,128,128]{3,2,1,0:T(8,128)(2,1)} %weight_in.1, bf16[128,128]{1,0:T(8,128)(2,1)} %mix_w.1, ...), custom_call_target="tpu_custom_call" | custom-call | flops 6000000000 | bytes 6291456 | tf_op jit(solution)/shard_map/pallas_call | solution.py:702
  36.8 0.0 collective-permute-done.above.edge_above
  36.8 0.0 copy-start.1
  36.8 0.4 collective-permute-done.2.below.edge_below
  37.2 0.0 copy-start.2
  37.2 37.8 %all-to-all-done = bf16[128,8,1024]{2,1,0:T(8,128)(2,1)S(1)} async-done(((bf16[128,8,1024]{2,1,0:T(8,128)(2,1)}), bf16[128,8,1024]{2,1,0:T(8,128)(2,1)S(1)}, u32[]{:S(2)}, u32[]{:S(2)}) %all-to-all-start) | async-done | bytes 2097184 | tf_op jit(solution)/shard_map/all_to_all | solution.py:820
  75.0 0.0 copy-start
  75.0 0.0 copy-done.3
  75.0 0.0 copy-done.4
  75.0 0.0 copy-done.5
  75.0 5.3 %shard_map.149 = (bf16[16,128,256]{2,1,0:T(8,128)(2,1)}, bf16[1024,512]{1,0:T(8,128)(2,1)}) custom-call(bf16[1024,1024]{1,0:T(8,128)(2,1)S(1)} %bitcast.9, bf16[256,256]{1,0:T(8,128)(2,1)S(1)} %copy-done.4, bf16[256,256]{1,0:T(8,128)(2,1)S(1)} %copy-done.5, f32[2,128,512]{2,1,0:T(8,128)S(1)} %copy-done.3, bf16[256,256]{1,0:T(8,128)(2,1)} %get-tuple-element.18.mix_in.wide, ...), custom_call_target="tpu_custom_call" | custom-call | flops 8000000000 | bytes 5242880 | tf_op jit(solution)/shard_map/pallas_call | solution.py:428
  80.3 0.0 copy-done.1
  80.3 0.0 copy-done.2
  80.3 0.0 copy-done
  80.3 0.0 copy-start.6
  80.3 5.5 %all-to-all-start.1 = ((bf16[128,8,512]{2,1,0:T(8,128)(2,1)}), bf16[128,8,512]{2,1,0:T(8,128)(2,1)S(1)}, u32[]{:S(2)}, u32[]{:S(2)}) async-start(bf16[128,8,512]{2,1,0:T(8,128)(2,1)} %bitcast.13), calls=%async_computation.1 | async-start | bytes 2097152 | tf_op jit(solution)/shard_map/all_to_all | solution.py:820
  85.8 0.0 copy-done.6
  85.8 0.9 collective-permute-start.1
  86.7 3.8 %shard_map.150 = (bf16[1,8,1024,128]{3,2,1,0:T(8,128)(2,1)}, f32[8,128]{1,0:T(8,128)}) custom-call(bf16[1,8,1024,128]{3,2,1,0:T(8,128)(2,1)} %cells.1, bf16[1,8,1024,128]{3,2,1,0:T(8,128)(2,1)} %cells.1, bf16[1,1,1024,128]{3,2,1,0:T(8,128)(2,1)} %copy-done.1, bf16[1,1,1024,128]{3,2,1,0:T(8,128)(2,1)} %copy-done.2, ...), custom_call_target="tpu_custom_call", output_to_operand_aliasing={{0}: (5, {})} | custom-call | flops 2000000000 | bytes 2097152 | tf_op jit(solution)/shard_map/pallas_call | solution.py:702
  90.4 5.4 %shard_map.151.mix_part = f32[128,128]{1,0:T(8,128)} custom-call(bf16[1024,1024]{1,0:T(8,128)(2,1)} %bitcast.10, bf16[16,128,256]{2,1,0:T(8,128)(2,1)} %get-tuple-element.22.spec, bf16[256,256]{1,0:T(8,128)(2,1)} %constant.33.clone.forward_in.forward, f32[2,128,512]{2,1,0:T(8,128)} %constant.35.clone.twiddle_in.twiddle, ...), custom_call_target="tpu_custom_call" | custom-call | flops 6000000000 | bytes 5242880 | tf_op jit(solution)/shard_map/pallas_call | solution.py:488
  95.9 21.1 %all-to-all-done.1 = bf16[128,8,512]{2,1,0:T(8,128)(2,1)S(1)} async-done(((bf16[128,8,512]{2,1,0:T(8,128)(2,1)}), bf16[128,8,512]{2,1,0:T(8,128)(2,1)S(1)}, u32[]{:S(2)}, u32[]{:S(2)}) %all-to-all-start.1) | async-done | bytes 1048608 | tf_op jit(solution)/shard_map/all_to_all | solution.py:820
  117.0 3.7 %shard_map.152 = (bf16[1024,512]{1,0:T(8,128)(2,1)}, bf16[512,128]{1,0:T(8,128)(2,1)}) custom-call(bf16[4,256,256]{2,1,0:T(8,128)(2,1)} %constant.36.clone.table, bf16[1024,512]{1,0:T(8,128)(2,1)S(1)} %bitcast.11, bf16[1024,512]{1,0:T(8,128)(2,1)} %get-tuple-element.21.inner, bf16[1,8,1024,128]{3,2,1,0:T(8,128)(2,1)} %cot.3, ...), custom_call_target="tpu_custom_call" | custom-call | flops 2000000000 | bytes 8388608 | tf_op jit(solution)/shard_map/pallas_call | solution.py:565
  120.7 5.9 %all-to-all-start.2 = ((bf16[256,2,128]{2,1,0:T(2,128)(2,1)}), bf16[256,2,128]{2,1,0:T(2,128)(2,1)S(1)}, u32[]{:S(2)}, u32[]{:S(2)}) async-start(bf16[256,2,128]{2,1,0:T(2,128)(2,1)} %bitcast.15), calls=%async_computation.2 | async-start | bytes 262144 | tf_op jit(solution)/shard_map/all_to_all | solution.py:844
  126.6 4.1 %shard_map.154 = bf16[1,8,1024,128]{3,2,1,0:T(8,128)(2,1)} custom-call(bf16[1024,512]{1,0:T(8,128)(2,1)} %get-tuple-element.25.summed, bf16[64,128]{1,0:T(8,128)(2,1)} %out_w.3), custom_call_target="tpu_custom_call" | custom-call | flops 500000000 | bytes 3145728 | tf_op jit(solution)/shard_map/pallas_call | solution.py:613
  130.8 0.0 collective-permute-done.1.far
  130.8 2.6 %shard_map.153 = bf16[1,8,1024,128]{3,2,1,0:T(8,128)(2,1)} custom-call(bf16[1,8,1024,128]{3,2,1,0:T(8,128)(2,1)} %cells.1, bf16[1,1,1024,128]{3,2,1,0:T(8,128)(2,1)} %copy-done.1, bf16[1,1,1024,128]{3,2,1,0:T(8,128)(2,1)S(1)} %collective-permute-done.1.far, bf16[3,3,128,128]{3,2,1,0:T(8,128)(2,1)} %weight_in.1, ...), custom_call_target="tpu_custom_call", output_to_operand_aliasing={{}: (4, {})} | custom-call | flops 1000000000 | bytes 1048576 | tf_op jit(solution)/shard_map/pallas_call | solution.py:799
  133.4 6.0 %all-to-all-done.2 = bf16[256,2,128]{2,1,0:T(2,128)(2,1)S(1)} async-done(((bf16[256,2,128]{2,1,0:T(2,128)(2,1)}), bf16[256,2,128]{2,1,0:T(2,128)(2,1)S(1)}, u32[]{:S(2)}, u32[]{:S(2)}) %all-to-all-start.2) | async-done | bytes 131104 | tf_op jit(solution)/shard_map/all_to_all | solution.py:844
  139.4 0.7 shard_map.155
Async XLA Ops:
  6.2 68.7 %all-to-all-start = ((bf16[128,8,1024]{2,1,0:T(8,128)(2,1)}), bf16[128,8,1024]{2,1,0:T(8,128)(2,1)S(1)}, u32[]{:S(2)}, u32[]{:S(2)}) async-start(bf16[128,8,1024]{2,1,0:T(8,128)(2,1)} %bitcast.14), calls=%async_computation | async-start | bytes 4194304 | tf_op jit(solution)/shard_map/all_to_all | solution.py:820
  23.0 13.8 %collective-permute-start = (bf16[1,1,1024,128]{3,2,1,0:T(8,128)(2,1)S(1)}, bf16[1,1,1024,128]{3,2,1,0:T(8,128)(2,1)S(1)}, u32[]{:S(2)}, u32[]{:S(2)}) collective-permute-start(bf16[1,1,1024,128]{3,2,1,0:T(8,128)(2,1)S(1)} %get-tuple-element.30), channel_id=1, source_target_pairs={{0,2},{2,4},{4,6},{6,8},{8,10},{10,12},{12,14},{16,18},{18,20},{20... | collective-permute-start | bytes 786440 | tf_op jit(solution)/shard_map/ppermute | solution.py:738
  26.5 48.4 %copy-start.3 = (f32[2,128,512]{2,1,0:T(8,128)S(1)}, f32[2,128,512]{2,1,0:T(8,128)}, u32[]{:S(2)}) copy-start(f32[2,128,512]{2,1,0:T(8,128)} %constant.35.clone.twiddle_in.twiddle) | copy-start | bytes 1572868
  26.5 48.4 %copy-start.4 = (bf16[256,256]{1,0:T(8,128)(2,1)S(1)}, bf16[256,256]{1,0:T(8,128)(2,1)}, u32[]{:S(2)}) copy-start(bf16[256,256]{1,0:T(8,128)(2,1)} %constant.33.clone.forward_in.forward) | copy-start | bytes 393220
  26.6 48.4 %copy-start.5 = (bf16[256,256]{1,0:T(8,128)(2,1)S(1)}, bf16[256,256]{1,0:T(8,128)(2,1)}, u32[]{:S(2)}) copy-start(bf16[256,256]{1,0:T(8,128)(2,1)} %constant.34.clone.backward_in) | copy-start | bytes 393220
  26.6 10.6 %collective-permute-start.2 = (bf16[1,1,1024,128]{3,2,1,0:T(8,128)(2,1)S(1)}, bf16[1,1,1024,128]{3,2,1,0:T(8,128)(2,1)S(1)}, u32[]{:S(2)}, u32[]{:S(2)}) collective-permute-start(bf16[1,1,1024,128]{3,2,1,0:T(8,128)(2,1)S(1)} %get-tuple-element.28), channel_id=1, source_target_pairs={{2,0},{4,2},{6,4},{8,6},{10,8},{12,10},{14,12},{18,16},{20,18},{22... | collective-permute-start | bytes 786440 | tf_op jit(solution)/shard_map/ppermute | solution.py:739
  36.8 43.5 %copy-start.1 = (bf16[1,1,1024,128]{3,2,1,0:T(8,128)(2,1)}, bf16[1,1,1024,128]{3,2,1,0:T(8,128)(2,1)S(1)}, u32[]{:S(2)}) copy-start(bf16[1,1,1024,128]{3,2,1,0:T(8,128)(2,1)S(1)} %collective-permute-done.above.edge_above) | copy-start | bytes 786436
  37.2 43.1 %copy-start.2 = (bf16[1,1,1024,128]{3,2,1,0:T(8,128)(2,1)}, bf16[1,1,1024,128]{3,2,1,0:T(8,128)(2,1)S(1)}, u32[]{:S(2)}) copy-start(bf16[1,1,1024,128]{3,2,1,0:T(8,128)(2,1)S(1)} %collective-permute-done.2.below.edge_below) | copy-start | bytes 786436
  75.0 5.4 %copy-start = (bf16[128,8,1024]{2,1,0:T(8,128)(2,1)}, bf16[128,8,1024]{2,1,0:T(8,128)(2,1)S(1)}, u32[]{:S(2)}) copy-start(bf16[128,8,1024]{2,1,0:T(8,128)(2,1)S(1)} %all-to-all-done) | copy-start | bytes 6291460
  80.3 5.5 %copy-start.6 = (bf16[1,1,1024,128]{3,2,1,0:T(8,128)(2,1)S(1)}, bf16[1,1,1024,128]{3,2,1,0:T(8,128)(2,1)}, u32[]{:S(2)}) copy-start(bf16[1,1,1024,128]{3,2,1,0:T(8,128)(2,1)} %get-tuple-element.29) | copy-start | bytes 786436
  80.3 36.7 %all-to-all-start.1 = ((bf16[128,8,512]{2,1,0:T(8,128)(2,1)}), bf16[128,8,512]{2,1,0:T(8,128)(2,1)S(1)}, u32[]{:S(2)}, u32[]{:S(2)}) async-start(bf16[128,8,512]{2,1,0:T(8,128)(2,1)} %bitcast.13), calls=%async_computation.1 | async-start | bytes 2097152 | tf_op jit(solution)/shard_map/all_to_all | solution.py:820
  85.8 45.0 %collective-permute-start.1 = (bf16[1,1,1024,128]{3,2,1,0:T(8,128)(2,1)S(1)}, bf16[1,1,1024,128]{3,2,1,0:T(8,128)(2,1)S(1)}, u32[]{:S(2)}, u32[]{:S(2)}) collective-permute-start(bf16[1,1,1024,128]{3,2,1,0:T(8,128)(2,1)S(1)} %copy-done.6), channel_id=1, source_target_pairs={{14,16},{30,32},{46,48},{62,64},{78,80},{94,96},{110,112},{126,128... | collective-permute-start | bytes 786440 | tf_op jit(solution)/shard_map/ppermute | solution.py:747
  120.7 18.7 %all-to-all-start.2 = ((bf16[256,2,128]{2,1,0:T(2,128)(2,1)}), bf16[256,2,128]{2,1,0:T(2,128)(2,1)S(1)}, u32[]{:S(2)}, u32[]{:S(2)}) async-start(bf16[256,2,128]{2,1,0:T(2,128)(2,1)} %bitcast.15), calls=%async_computation.2 | async-start | bytes 262144 | tf_op jit(solution)/shard_map/all_to_all | solution.py:844

commit v8 on v7

--- a/solution.py
+++ b/solution.py
@@ -350,7 +350,6 @@
         copy.start()
     for m in range(4):
         stage[m] = block[:, m * PAIR : (m + 1) * PAIR].astype(F32)
-    mix_load.wait()
     forward_load.wait()
     twiddle_load.wait()
     backward_load.wait()
@@ -406,6 +405,8 @@
             spectrum(kk)
         if 0 <= kk - 1 < PER_GROUP:
             activate(kk - 1)
+        if kk == 0:
+            mix_load.wait()
         if kk < PER_GROUP:
             mix(kk)
         if 0 <= kk - 1 < PER_GROUP:
@@ -597,8 +598,9 @@
     wide[0:SPEC_CH, :] = jnp.concatenate([out_w[...], zero], axis=1)
     wide[SPEC_CH:, :] = jnp.concatenate([zero, out_w[...]], axis=1)
     stores = []
+    for copy in loads:
+        copy.wait()
     for p in range(4):
-        loads[p].wait()
         prod = dot(held[p], wide[...])
         result[2 * p] = prod[:, 0:128].astype(BF16)
         result[2 * p + 1] = prod[:, 128:].astype(BF16)

time: 141 us -> 140 us (level)
  no operation moved by 1% of the time
where the time goes in v8:
time: 140 us
  waiting for transfers between devices  65.7 us (47%)
  Pallas kernels  38.7 us (28%)
  starting transfers between devices  32.7 us (23%)
  local copies, waits for them, and re-layouts  1.9 us (1%)
    all_to_all x2, waiting for transfers between devices, exchange(): lax.all_to_all(block.reshape(GROUPS, ROWS, lanes), 'rows', split_axis=0,...  58.9 us
    all_to_all x2, starting transfers between devices, exchange(): lax.all_to_all(block.reshape(GROUPS, ROWS, lanes), 'rows', split_axis=0,...  20.3 us
    pallas_call x2, Pallas kernels, conv_call(): pl.pallas_call(kernel, grid=(rows,), in_specs=in_specs, out_specs=[row_sp...  11.9 us
    all_to_all x1, waiting for transfers between devices, shards(): lax.all_to_all(terms, ('rows', 'img'), split_axis=0, concat_axis=0, tiled...  6.42 us
    all_to_all x1, starting transfers between devices, shards(): lax.all_to_all(terms, ('rows', 'img'), split_axis=0, concat_axis=0, tiled...  5.88 us
    pallas_call x1, Pallas kernels, rows_forward(): pl.pallas_call(rows_kernel, grid=(1,), in_specs=[ANY, ANY, whole_spec((SP...  5.59 us
    pallas_call x1, Pallas kernels, mix_terms(): pl.pallas_call(mix_kernel, grid=(1,), in_specs=[pl.BlockSpec((1024, 512),...  5.45 us
    pallas_call x1, Pallas kernels, columns(): pl.pallas_call(columns_kernel, in_specs=[VMEM] + [ANY] * 6, out_specs=[AN...  4.93 us
  transfers between devices with their start and end apart: 6, of which 4 were waited for; matrix products, arithmetic and copies ran while one was open for 1% of the time, Pallas kernels for 20%

profile of v8, /device:TPU:1, one launch (start us, length us, event | category | flops | bytes accessed | tf_op | source)
XLA Modules:
  0.0 139.7 jit_solution(4071537398952385558)
XLA Ops:
  0.6 5.6 %shard_map.147 = (bf16[1024,1024]{1,0:T(8,128)(2,1)}, bf16[1024,512]{1,0:T(8,128)(2,1)}) custom-call(bf16[1,8,1024,128]{3,2,1,0:T(8,128)(2,1)} %maps.1, bf16[1,8,1024,128]{3,2,1,0:T(8,128)(2,1)} %cot.3, bf16[64,128]{1,0:T(8,128)(2,1)} %bitcast.16, bf16[64,128]{1,0:T(8,128)(2,1)} %out_w.3, bf16[4,256,256]{2,1,0:T(8,128)(2,1)} %constant.32.clone.table), custom_call_target="tpu_custom_call" | custom-call | flops 5000000000 | bytes 11534336 | tf_op jit(solution)/shard_map/pallas_call | solution.py:210
  6.2 14.9 %all-to-all-start = ((bf16[128,8,1024]{2,1,0:T(8,128)(2,1)}), bf16[128,8,1024]{2,1,0:T(8,128)(2,1)S(1)}, u32[]{:S(2)}, u32[]{:S(2)}) async-start(bf16[128,8,1024]{2,1,0:T(8,128)(2,1)} %bitcast.14), calls=%async_computation | async-start | bytes 4194304 | tf_op jit(solution)/shard_map/all_to_all | solution.py:822
  21.1 1.9 %fusion = (bf16[1,1,1024,128]{3,2,1,0:T(8,128)(2,1)S(1)}, bf16[1,1,1024,128]{3,2,1,0:T(8,128)(2,1)}, bf16[1,1,1024,128]{3,2,1,0:T(8,128)(2,1)S(1)}) fusion(bf16[1,8,1024,128]{3,2,1,0:T(8,128)(2,1)} %cells.1, s32[]{:T(128)S(6)} %select_n.13), kind=kLoop, calls=%fused_computation.1 | loop fusion | bytes 1572868 | tf_op jit(solution)/shard_map/slice | solution.py:738
  23.0 3.5 %collective-permute-start = (bf16[1,1,1024,128]{3,2,1,0:T(8,128)(2,1)S(1)}, bf16[1,1,1024,128]{3,2,1,0:T(8,128)(2,1)S(1)}, u32[]{:S(2)}, u32[]{:S(2)}) collective-permute-start(bf16[1,1,1024,128]{3,2,1,0:T(8,128)(2,1)S(1)} %get-tuple-element.30), channel_id=1, source_target_pairs={{0,2},{2,4},{4,6},{6,8},{8,10},{10,12},{12,14},{16,18},{18,20},{20... | collective-permute-start | bytes 786440 | tf_op jit(solution)/shard_map/ppermute | solution.py:740
  26.5 0.0 copy-start.3
  26.5 0.0 copy-start.4
  26.6 0.0 copy-start.5
  26.6 2.1 %collective-permute-start.2 = (bf16[1,1,1024,128]{3,2,1,0:T(8,128)(2,1)S(1)}, bf16[1,1,1024,128]{3,2,1,0:T(8,128)(2,1)S(1)}, u32[]{:S(2)}, u32[]{:S(2)}) collective-permute-start(bf16[1,1,1024,128]{3,2,1,0:T(8,128)(2,1)S(1)} %get-tuple-element.28), channel_id=1, source_target_pairs={{2,0},{4,2},{6,4},{8,6},{10,8},{12,10},{14,12},{18,16},{20,18},{22... | collective-permute-start | bytes 786440 | tf_op jit(solution)/shard_map/ppermute | solution.py:741
  28.6 8.2 %shard_map.148 = (bf16[1,8,1024,128]{3,2,1,0:T(8,128)(2,1)}, bf16[256,256]{1,0:T(8,128)(2,1)}) custom-call(bf16[1,8,1024,128]{3,2,1,0:T(8,128)(2,1)} %cells.1, bf16[1,8,1024,128]{3,2,1,0:T(8,128)(2,1)} %cells.1, bf16[1,8,1024,128]{3,2,1,0:T(8,128)(2,1)} %cells.1, bf16[3,3,128,128]{3,2,1,0:T(8,128)(2,1)} %weight_in.1, bf16[128,128]{1,0:T(8,128)(2,1)} %mix_w.1, ...), custom_call_target="tpu_custom_call" | custom-call | flops 6000000000 | bytes 6291456 | tf_op jit(solution)/shard_map/pallas_call | solution.py:704
  36.8 0.0 collective-permute-done.above.edge_above
  36.8 0.0 copy-start.1
  36.8 0.4 collective-permute-done.2.below.edge_below
  37.2 0.0 copy-start.2
  37.2 37.8 %all-to-all-done = bf16[128,8,1024]{2,1,0:T(8,128)(2,1)S(1)} async-done(((bf16[128,8,1024]{2,1,0:T(8,128)(2,1)}), bf16[128,8,1024]{2,1,0:T(8,128)(2,1)S(1)}, u32[]{:S(2)}, u32[]{:S(2)}) %all-to-all-start) | async-done | bytes 2097184 | tf_op jit(solution)/shard_map/all_to_all | solution.py:822
  75.0 0.0 copy-start
  75.0 0.0 copy-done.3
  75.0 0.0 copy-done.4
  75.0 0.0 copy-done.5
  75.0 4.9 %shard_map.149 = (bf16[16,128,256]{2,1,0:T(8,128)(2,1)}, bf16[1024,512]{1,0:T(8,128)(2,1)}) custom-call(bf16[1024,1024]{1,0:T(8,128)(2,1)S(1)} %bitcast.9, bf16[256,256]{1,0:T(8,128)(2,1)S(1)} %copy-done.4, bf16[256,256]{1,0:T(8,128)(2,1)S(1)} %copy-done.5, f32[2,128,512]{2,1,0:T(8,128)S(1)} %copy-done.3, bf16[256,256]{1,0:T(8,128)(2,1)} %get-tuple-element.18.mix_in.wide, ...), custom_call_target="tpu_custom_call" | custom-call | flops 8000000000 | bytes 5242880 | tf_op jit(solution)/shard_map/pallas_call | solution.py:429
  79.9 0.0 copy-done.1
  79.9 0.0 copy-done.2
  79.9 0.0 copy-done
  79.9 0.0 copy-start.6
  79.9 5.5 %all-to-all-start.1 = ((bf16[128,8,512]{2,1,0:T(8,128)(2,1)}), bf16[128,8,512]{2,1,0:T(8,128)(2,1)S(1)}, u32[]{:S(2)}, u32[]{:S(2)}) async-start(bf16[128,8,512]{2,1,0:T(8,128)(2,1)} %bitcast.13), calls=%async_computation.1 | async-start | bytes 2097152 | tf_op jit(solution)/shard_map/all_to_all | solution.py:822
  85.4 0.0 copy-done.6
  85.4 0.9 collective-permute-start.1
  86.3 3.8 %shard_map.150 = (bf16[1,8,1024,128]{3,2,1,0:T(8,128)(2,1)}, f32[8,128]{1,0:T(8,128)}) custom-call(bf16[1,8,1024,128]{3,2,1,0:T(8,128)(2,1)} %cells.1, bf16[1,8,1024,128]{3,2,1,0:T(8,128)(2,1)} %cells.1, bf16[1,1,1024,128]{3,2,1,0:T(8,128)(2,1)} %copy-done.1, bf16[1,1,1024,128]{3,2,1,0:T(8,128)(2,1)} %copy-done.2, ...), custom_call_target="tpu_custom_call", output_to_operand_aliasing={{0}: (5, {})} | custom-call | flops 2000000000 | bytes 2097152 | tf_op jit(solution)/shard_map/pallas_call | solution.py:704
  90.0 5.4 %shard_map.151.mix_part = f32[128,128]{1,0:T(8,128)} custom-call(bf16[1024,1024]{1,0:T(8,128)(2,1)} %bitcast.10, bf16[16,128,256]{2,1,0:T(8,128)(2,1)} %get-tuple-element.22.spec, bf16[256,256]{1,0:T(8,128)(2,1)} %constant.33.clone.forward_in.forward, f32[2,128,512]{2,1,0:T(8,128)} %constant.35.clone.twiddle_in.twiddle, ...), custom_call_target="tpu_custom_call" | custom-call | flops 6000000000 | bytes 5242880 | tf_op jit(solution)/shard_map/pallas_call | solution.py:489
  95.5 21.1 %all-to-all-done.1 = bf16[128,8,512]{2,1,0:T(8,128)(2,1)S(1)} async-done(((bf16[128,8,512]{2,1,0:T(8,128)(2,1)}), bf16[128,8,512]{2,1,0:T(8,128)(2,1)S(1)}, u32[]{:S(2)}, u32[]{:S(2)}) %all-to-all-start.1) | async-done | bytes 1048608 | tf_op jit(solution)/shard_map/all_to_all | solution.py:822
  116.6 3.7 %shard_map.152 = (bf16[1024,512]{1,0:T(8,128)(2,1)}, bf16[512,128]{1,0:T(8,128)(2,1)}) custom-call(bf16[4,256,256]{2,1,0:T(8,128)(2,1)} %constant.36.clone.table, bf16[1024,512]{1,0:T(8,128)(2,1)S(1)} %bitcast.11, bf16[1024,512]{1,0:T(8,128)(2,1)} %get-tuple-element.21.inner, bf16[1,8,1024,128]{3,2,1,0:T(8,128)(2,1)} %cot.3, ...), custom_call_target="tpu_custom_call" | custom-call | flops 2000000000 | bytes 8388608 | tf_op jit(solution)/shard_map/pallas_call | solution.py:566
  120.3 5.9 %all-to-all-start.2 = ((bf16[256,2,128]{2,1,0:T(2,128)(2,1)}), bf16[256,2,128]{2,1,0:T(2,128)(2,1)S(1)}, u32[]{:S(2)}, u32[]{:S(2)}) async-start(bf16[256,2,128]{2,1,0:T(2,128)(2,1)} %bitcast.15), calls=%async_computation.2 | async-start | bytes 262144 | tf_op jit(solution)/shard_map/all_to_all | solution.py:846
  126.2 3.7 %shard_map.154 = bf16[1,8,1024,128]{3,2,1,0:T(8,128)(2,1)} custom-call(bf16[1024,512]{1,0:T(8,128)(2,1)} %get-tuple-element.25.summed, bf16[64,128]{1,0:T(8,128)(2,1)} %out_w.3), custom_call_target="tpu_custom_call" | custom-call | flops 500000000 | bytes 3145728 | tf_op jit(solution)/shard_map/pallas_call | solution.py:615
  130.0 0.0 collective-permute-done.1.far
  130.0 2.6 %shard_map.153 = bf16[1,8,1024,128]{3,2,1,0:T(8,128)(2,1)} custom-call(bf16[1,8,1024,128]{3,2,1,0:T(8,128)(2,1)} %cells.1, bf16[1,1,1024,128]{3,2,1,0:T(8,128)(2,1)} %copy-done.1, bf16[1,1,1024,128]{3,2,1,0:T(8,128)(2,1)S(1)} %collective-permute-done.1.far, bf16[3,3,128,128]{3,2,1,0:T(8,128)(2,1)} %weight_in.1, ...), custom_call_target="tpu_custom_call", output_to_operand_aliasing={{}: (4, {})} | custom-call | flops 1000000000 | bytes 1048576 | tf_op jit(solution)/shard_map/pallas_call | solution.py:801
  132.6 6.4 %all-to-all-done.2 = bf16[256,2,128]{2,1,0:T(2,128)(2,1)S(1)} async-done(((bf16[256,2,128]{2,1,0:T(2,128)(2,1)}), bf16[256,2,128]{2,1,0:T(2,128)(2,1)S(1)}, u32[]{:S(2)}, u32[]{:S(2)}) %all-to-all-start.2) | async-done | bytes 131104 | tf_op jit(solution)/shard_map/all_to_all | solution.py:846
  139.0 0.7 shard_map.155
Async XLA Ops:
  6.2 68.7 %all-to-all-start = ((bf16[128,8,1024]{2,1,0:T(8,128)(2,1)}), bf16[128,8,1024]{2,1,0:T(8,128)(2,1)S(1)}, u32[]{:S(2)}, u32[]{:S(2)}) async-start(bf16[128,8,1024]{2,1,0:T(8,128)(2,1)} %bitcast.14), calls=%async_computation | async-start | bytes 4194304 | tf_op jit(solution)/shard_map/all_to_all | solution.py:822
  23.0 13.8 %collective-permute-start = (bf16[1,1,1024,128]{3,2,1,0:T(8,128)(2,1)S(1)}, bf16[1,1,1024,128]{3,2,1,0:T(8,128)(2,1)S(1)}, u32[]{:S(2)}, u32[]{:S(2)}) collective-permute-start(bf16[1,1,1024,128]{3,2,1,0:T(8,128)(2,1)S(1)} %get-tuple-element.30), channel_id=1, source_target_pairs={{0,2},{2,4},{4,6},{6,8},{8,10},{10,12},{12,14},{16,18},{18,20},{20... | collective-permute-start | bytes 786440 | tf_op jit(solution)/shard_map/ppermute | solution.py:740
  26.5 48.4 %copy-start.3 = (f32[2,128,512]{2,1,0:T(8,128)S(1)}, f32[2,128,512]{2,1,0:T(8,128)}, u32[]{:S(2)}) copy-start(f32[2,128,512]{2,1,0:T(8,128)} %constant.35.clone.twiddle_in.twiddle) | copy-start | bytes 1572868
  26.5 48.4 %copy-start.4 = (bf16[256,256]{1,0:T(8,128)(2,1)S(1)}, bf16[256,256]{1,0:T(8,128)(2,1)}, u32[]{:S(2)}) copy-start(bf16[256,256]{1,0:T(8,128)(2,1)} %constant.33.clone.forward_in.forward) | copy-start | bytes 393220
  26.6 48.4 %copy-start.5 = (bf16[256,256]{1,0:T(8,128)(2,1)S(1)}, bf16[256,256]{1,0:T(8,128)(2,1)}, u32[]{:S(2)}) copy-start(bf16[256,256]{1,0:T(8,128)(2,1)} %constant.34.clone.backward_in) | copy-start | bytes 393220
  26.6 10.6 %collective-permute-start.2 = (bf16[1,1,1024,128]{3,2,1,0:T(8,128)(2,1)S(1)}, bf16[1,1,1024,128]{3,2,1,0:T(8,128)(2,1)S(1)}, u32[]{:S(2)}, u32[]{:S(2)}) collective-permute-start(bf16[1,1,1024,128]{3,2,1,0:T(8,128)(2,1)S(1)} %get-tuple-element.28), channel_id=1, source_target_pairs={{2,0},{4,2},{6,4},{8,6},{10,8},{12,10},{14,12},{18,16},{20,18},{22... | collective-permute-start | bytes 786440 | tf_op jit(solution)/shard_map/ppermute | solution.py:741
  36.8 43.1 %copy-start.1 = (bf16[1,1,1024,128]{3,2,1,0:T(8,128)(2,1)}, bf16[1,1,1024,128]{3,2,1,0:T(8,128)(2,1)S(1)}, u32[]{:S(2)}) copy-start(bf16[1,1,1024,128]{3,2,1,0:T(8,128)(2,1)S(1)} %collective-permute-done.above.edge_above) | copy-start | bytes 786436
  37.2 42.7 %copy-start.2 = (bf16[1,1,1024,128]{3,2,1,0:T(8,128)(2,1)}, bf16[1,1,1024,128]{3,2,1,0:T(8,128)(2,1)S(1)}, u32[]{:S(2)}) copy-start(bf16[1,1,1024,128]{3,2,1,0:T(8,128)(2,1)S(1)} %collective-permute-done.2.below.edge_below) | copy-start | bytes 786436
  75.0 5.0 %copy-start = (bf16[128,8,1024]{2,1,0:T(8,128)(2,1)}, bf16[128,8,1024]{2,1,0:T(8,128)(2,1)S(1)}, u32[]{:S(2)}) copy-start(bf16[128,8,1024]{2,1,0:T(8,128)(2,1)S(1)} %all-to-all-done) | copy-start | bytes 6291460
  79.9 5.5 %copy-start.6 = (bf16[1,1,1024,128]{3,2,1,0:T(8,128)(2,1)S(1)}, bf16[1,1,1024,128]{3,2,1,0:T(8,128)(2,1)}, u32[]{:S(2)}) copy-start(bf16[1,1,1024,128]{3,2,1,0:T(8,128)(2,1)} %get-tuple-element.29) | copy-start | bytes 786436
  79.9 36.6 %all-to-all-start.1 = ((bf16[128,8,512]{2,1,0:T(8,128)(2,1)}), bf16[128,8,512]{2,1,0:T(8,128)(2,1)S(1)}, u32[]{:S(2)}, u32[]{:S(2)}) async-start(bf16[128,8,512]{2,1,0:T(8,128)(2,1)} %bitcast.13), calls=%async_computation.1 | async-start | bytes 2097152 | tf_op jit(solution)/shard_map/all_to_all | solution.py:822
  85.4 44.5 %collective-permute-start.1 = (bf16[1,1,1024,128]{3,2,1,0:T(8,128)(2,1)S(1)}, bf16[1,1,1024,128]{3,2,1,0:T(8,128)(2,1)S(1)}, u32[]{:S(2)}, u32[]{:S(2)}) collective-permute-start(bf16[1,1,1024,128]{3,2,1,0:T(8,128)(2,1)S(1)} %copy-done.6), channel_id=1, source_target_pairs={{14,16},{30,32},{46,48},{62,64},{78,80},{94,96},{110,112},{126,128... | collective-permute-start | bytes 786440 | tf_op jit(solution)/shard_map/ppermute | solution.py:749
  120.3 18.7 %all-to-all-start.2 = ((bf16[256,2,128]{2,1,0:T(2,128)(2,1)}), bf16[256,2,128]{2,1,0:T(2,128)(2,1)S(1)}, u32[]{:S(2)}, u32[]{:S(2)}) async-start(bf16[256,2,128]{2,1,0:T(2,128)(2,1)} %bitcast.15), calls=%async_computation.2 | async-start | bytes 262144 | tf_op jit(solution)/shard_map/all_to_all | solution.py:846
